TPU v7x, 128 devices: a whole 4x4x4 slice. The times are simulated.
128 devices in a mesh: island: 2 (over y_lo), fsdp: 64 (over z, x, y_hi, core).
Axes of the slice: x: 4, y: 4 (y_hi: 2, y_lo: 2; y = y_hi * 2 + y_lo), z: 4, core: 2. Of those that a mesh axis runs over, the one named last changes fastest.
Arguments:
- inner_params: float32 [2, 3, 3584, 3584], P('island', None, 'fsdp'), may hold values from -0.09375 to 0.09375
- inner_grads: bfloat16 [2, 3, 3584, 3584], P('island', None, 'fsdp'), may hold values from -6 to 6
- adam_first: float32 [2, 3, 3584, 3584], P('island', None, 'fsdp'), may hold values from -0.6 to 0.6
- adam_second: float32 [2, 3, 3584, 3584], P('island', None, 'fsdp'), may hold values from 0.0001 to 0.01
- anchor: float32 [3584, 3584], P('fsdp'), may hold values from -0.09375 to 0.09375
- momentum: float32 [3584, 3584], P('fsdp'), may hold values from -0.046875 to 0.046875
- tokens: bfloat16 [65536, 3584], P(('island', 'fsdp')), may hold values from -6 to 6
- frag_index: int32 [1], replicated, may hold values from 0 to 99999
- plan: int32 [3], replicated, may hold values from 0 to 2, each once
Outputs:
- params_out: float32 [2, 3, 3584, 3584], P('island', None, 'fsdp')
- first_out: float32 [2, 3, 3584, 3584], P('island', None, 'fsdp')
- second_out: float32 [2, 3, 3584, 3584], P('island', None, 'fsdp')
- momentum_out: float32 [3584, 3584], P('fsdp')
- projected: bfloat16 [65536, 3584], P(('island', 'fsdp'))
Inputs may be any that keep to these rules, and one draw needn't show every extreme that they name: `plan`: each fragment number names exactly one layer.
All inputs are finite; a program needn't handle non-finite values.
Results may differ from a plain program's by a relative error of at most 0.0065.
Values may be sent and summed in bfloat16 or wider, within the bound.
No kernel may reach another device: no remote copies, remote signals or barrier semaphores. Data moves between devices by JAX's collectives and lax.ppermute only.
A program may use at most 192 MiB of HBM per device.

v0:
```python
import jax
import jax.numpy as jnp
from jax import lax
from jax.sharding import PartitionSpec as P

STEP = 40


outer_rate = 0.7
outer_mu = 0.9
inner_rate = 0.01
decay_rate = 0.1
beta_one = 0.9
beta_two = 0.95
adam_eps = 1e-08


def adamw_step(params, grads, first, second):
    grad_f = grads.astype(jnp.float32)
    first_new = beta_one * first + (1.0 - beta_one) * grad_f
    second_new = beta_two * second + (1.0 - beta_two) * grad_f * grad_f
    first_hat = first_new / (1.0 - beta_one**STEP)
    second_hat = second_new / (1.0 - beta_two**STEP)
    stepped = params * (1.0 - inner_rate * decay_rate) - inner_rate * first_hat / (
        jnp.sqrt(second_hat) + adam_eps
    )
    return (stepped, first_new, second_new)


def outer_update(anchor_rows, momentum_rows, summed, replicas):
    pseudo_grad = summed / replicas
    momentum_new = outer_mu * momentum_rows + pseudo_grad
    anchor_new = anchor_rows - outer_rate * (pseudo_grad + outer_mu * momentum_new)
    return (anchor_new, momentum_new)


def body(
    inner_params, inner_grads, adam_first, adam_second, anchor, momentum, tokens, frag_index, plan
):
    layer_count = inner_params.shape[1]
    layer_ids = jnp.arange(layer_count, dtype=jnp.int32)
    current = frag_index[0] % layer_count
    chosen = jnp.sum(jnp.where(plan == current, layer_ids, 0))
    drifted = lax.dynamic_index_in_dim(inner_params[0], chosen, 0, keepdims=False)
    local_diff = anchor - drifted
    replicas = lax.axis_size("island")
    summed = lax.psum(local_diff, "island")
    new_anchor, momentum_out = outer_update(anchor, momentum, summed, replicas)
    weight_bf = new_anchor.astype(jnp.bfloat16)
    result = jnp.dot(
        tokens,
        lax.all_gather(weight_bf, "fsdp", axis=0, tiled=True),
        preferred_element_type=jnp.float32,
    )
    stepped, first_new, second_new = adamw_step(inner_params, inner_grads, adam_first, adam_second)
    is_frag = (layer_ids == chosen)[None, :, None, None]
    params_out = jnp.where(is_frag, new_anchor[None, None], stepped)
    first_out = jnp.where(is_frag, adam_first, first_new)
    second_out = jnp.where(is_frag, adam_second, second_new)
    projected = result.astype(jnp.bfloat16)
    return (params_out, first_out, second_out, momentum_out, projected)


def solution(mesh):
    placed = (
        P("island", None, "fsdp", None),
        P("island", None, "fsdp", None),
        P("island", None, "fsdp", None),
        P("island", None, "fsdp", None),
        P("fsdp", None),
        P("fsdp", None),
        P(("island", "fsdp"), None),
        P(),
        P(),
    )
    return jax.shard_map(
        body,
        mesh=mesh,
        in_specs=placed,
        out_specs=(
            P("island", None, "fsdp", None),
            P("island", None, "fsdp", None),
            P("island", None, "fsdp", None),
            P("fsdp", None),
            P(("island", "fsdp"), None),
        ),
        check_vma=False,
    )
```

profile of v0, /device:TPU:1, one launch (start us, length us, event | category | flops | bytes accessed | tf_op | source)
XLA Modules:
  0.0 230.0 jit_solution(1312125726610980232)
XLA Ops:
  7.2 0.0 copy-start.1
  7.2 0.0 all-reduce.2.cloned.1.call-start
  7.9 1.3 fusion.5
  11.2 2.4 %bitcast_subtract_fusion = f32[56,3584]{1,0:T(8,128)} fusion(f32[56,3584]{1,0:T(8,128)} %param.13, f32[1,3,56,3584]{3,2,1,0:T(8,128)} %param.9, s32[]{:T(128)S(6)} %select_n.28), kind=kLoop, calls=%fused_computation.9 | loop fusion | flops 200704 | bytes 2408452 | tf_op jit(solution)/shard_map/sub | solution.py:45
  13.5 0.0 all-reduce.2.cloned.1.call-update
  13.6 0.0 copy-start
  13.6 0.0 all-gather.2.cloned.1.call-start
  13.6 44.6 %all-reduce.2.cloned.1.call-done = f32[56,3584]{1,0:T(8,128)} async-done(((f32[56,3584]{1,0:T(8,128)}), f32[56,3584]{1,0:T(8,128)}) %all-reduce.2.cloned.1.call-update) | async-done | bytes 802832 | tf_op jit(solution)/shard_map/psum | solution.py:47
  58.2 0.0 copy-done.1
  58.2 2.9 %fusion.6 = (bf16[56,3584]{1,0:T(8,128)(2,1)}, f32[56,3584]{1,0:T(8,128)}, f32[56,3584]{1,0:T(8,128)}) fusion(f32[56,3584]{1,0:T(8,128)S(1)} %copy-done.1, f32[56,3584]{1,0:T(8,128)} %all-reduce.2.cloned.1.call-done, f32[56,3584]{1,0:T(8,128)} %param.14), kind=kLoop, calls=%fused_computation.15 | loop fusion | flops 1605632 | bytes 4415488 | tf_op jit(solution)/shard_map/convert_element_type | solution.py:49
  61.1 0.0 all-gather.2.cloned.1.call-update
  61.2 0.7 iota_compare_fusion
  61.8 0.0 copy-done
  61.8 8.4 %fusion.3 = (f32[1,3,56,3584]{3,2,1,0:T(8,128)}, f32[1,3,56,3584]{3,2,1,0:T(8,128)}, f32[1,3,56,3584]{3,2,1,0:T(8,128)}) fusion(f32[1,3,56,3584]{3,2,1,0:T(8,128)} %param.12, bf16[1,3,56,3584]{3,2,1,0:T(8,128)(2,1)} %param.10, pred[3]{0:T(512)(128)(4,1)S(1)} %iota_compare_fusion, f32[1,3,56,3584]{3,2,1,0:T(8,128)} %param.11, ...), kind=kLoop, calls=%fused_computation.7 | loop fusion | flops 10235904 | bytes 16457731 | tf_op jit(solution)/shard_map/jit(_where)/select_n | solution.py:59
  70.2 126.1 %all-gather.2.cloned.1.call-done = bf16[3584,3584]{1,0:T(8,128)(2,1)} async-done(((bf16[56,3584]{1,0:T(8,128)(2,1)}), bf16[3584,3584]{1,0:T(8,128)(2,1)}) %all-gather.2.cloned.1.call-update) | async-done | bytes 25690128 | tf_op jit(solution)/shard_map/all_gather | solution.py:52
  196.3 21.0 %fusion = bf16[512,3584]{0,1:T(8,128)(2,1)} fusion(bf16[3584,3584]{1,0:T(8,128)(2,1)} %all-gather.2.cloned.1.call-done, bf16[512,3584]{1,0:T(8,128)(2,1)} %param.15), kind=kOutput, calls=%fused_computation.1 | convolution fusion | flops 13155172352 | bytes 33030144 | tf_op jit(solution)/shard_map/dot_general | solution.py:50
  217.2 5.9 %copy.14 = bf16[512,3584]{1,0:T(8,128)(2,1)} copy(bf16[512,3584]{0,1:T(8,128)(2,1)} %fusion) | data formatting | bytes 7340032
Async XLA Ops:
  7.2 51.0 %copy-start.1 = (f32[56,3584]{1,0:T(8,128)S(1)}, f32[56,3584]{1,0:T(8,128)}, u32[]{:S(2)}) copy-start(f32[56,3584]{1,0:T(8,128)} %param.13) | copy-start | bytes 2408452
  7.2 51.0 %all-reduce.2.cloned.1.call-start = ((), (), s32[]{:S(2)}) async-start(), calls=%async_computation | async-start | bytes 1605632 | tf_op jit(solution)/shard_map/psum | solution.py:47
  13.6 48.3 %copy-start = (f32[1,3,56,3584]{3,2,1,0:T(8,128)S(1)}, f32[1,3,56,3584]{3,2,1,0:T(8,128)}, u32[]{:S(2)}) copy-start(f32[1,3,56,3584]{3,2,1,0:T(8,128)} %param.9) | copy-start | bytes 7225348
  13.6 182.7 %all-gather.2.cloned.1.call-start = ((), (), s32[]{:S(2)}) async-start(), calls=%async_computation.1 | async-start | bytes 26091520 | tf_op jit(solution)/shard_map/all_gather | solution.py:52
Sparse Core Ops, SparseCore 0:
  13.7 44.4 all-reduce.1
  61.7 134.5 all-gather.1
where the time goes:
time: 230 us
  waiting for transfers between devices  171 us (74%)
  matrix products  21 us (9%)
  between operations  16.7 us (7%)
  other arithmetic  15.6 us (7%)
  local copies, waits for them, and re-layouts  5.92 us (3%)
    all_gather x1, waiting for transfers between devices, body(): lax.all_gather(weight_bf, 'fsdp', axis=0, tiled=True)  126 us
    psum x1, waiting for transfers between devices, body(): summed = lax.psum(local_diff, 'island')  44.6 us
    dot_general x1, matrix products, body(): jnp.dot(tokens, lax.all_gather(weight_bf, 'fsdp', axis=0, tiled=True), pr...  21 us
    select_n x1, other arithmetic, body(): second_out = jnp.where(is_frag, adam_second, second_new)  8.37 us
    unnamed x5, local copies, waits for them, and re-layouts  5.92 us
  transfers between devices with their start and end apart: 2, of which 2 were waited for; matrix products, arithmetic and copies ran while one was open for 4% of the time, Pallas kernels for 0%

commit v1 on v0

v1 whole, which is shorter than its diff:
```python
import functools

import jax
import jax.numpy as jnp
import numpy as np
from jax import lax
from jax.experimental import pallas as pl
from jax.experimental.pallas import tpu as pltpu
from jax.sharding import Mesh
from jax.sharding import PartitionSpec as P

STEP = 40
LAYERS = 3
outer_rate = 0.7
outer_mu = 0.9
inner_rate = 0.01
decay_rate = 0.1
beta_one = 0.9
beta_two = 0.95
adam_eps = 1e-08

ROWS = 56
CHIP = 2 * ROWS
D = 3584
HALF = D // 2
PART = 768
SIDE = 256
GROUP = 256
GROUPS = 3
SENT = PART + SIDE
TOK = 512

ALL = ("yl", "z", "x", "yh", "core")
CHIPS = ("z", "x", "yh")
FLIPS = (("x", 1), ("y", 1), ("z", 1), ("x", 3), ("y", 3), ("z", 3))


def order(group, core):
    s = (group + 3 * core) % 6
    return FLIPS[s:] + FLIPS[:s]


def flipped(i, flip):
    core, yh, x, z, yl = i % 2, i // 2 % 2, i // 4 % 4, i // 16 % 4, i // 64
    y = yh * 2 + yl
    axis, mask = flip
    x, y, z = (v ^ mask if name == axis else v for name, v in (("x", x), ("y", y), ("z", z)))
    return ((y % 2 * 4 + z) * 4 + x) * 4 + y // 2 * 2 + core


def exchange(value, group, step):
    flips = [order(group, core)[step] for core in (0, 1)]
    return lax.ppermute(value, ALL, [(i, flipped(i, flips[i % 2])) for i in range(128)])


def code_masks(group, core):
    shift = {"z": 4, "x": 2, "y": 0}
    bits = [mask << shift[axis] for axis, mask in order(group, core)]
    return [functools.reduce(lambda a, b: a ^ b, [bits[k] for k in range(6) if r >> k & 1], 0) for r in range(64)]


def swap_cores(value):
    return lax.ppermute(value, "core", [(0, 1), (1, 0)])


def chosen_of(frag_ref, plan_ref):
    current = lax.rem(frag_ref[0], LAYERS)
    return jnp.where(plan_ref[0] == current, 0, jnp.where(plan_ref[1] == current, 1, 2))


def lanes(start, size):
    return pl.ds(pl.multiple_of(start, 128), size)


def outer(anchor, momentum, summed):
    pseudo = summed * 0.5
    momentum_new = outer_mu * momentum + pseudo
    return anchor - outer_rate * (pseudo + outer_mu * momentum_new), momentum_new


def diff_kernel(frag_ref, plan_ref, anchor_ref, params_ref, diff_ref, sent_ref):
    other = 1 - lax.axis_index("yl")
    diff_ref[...] = anchor_ref[...] - params_ref[0, 0]
    for half in (0, 1):
        at = half * SENT
        sent_ref[:, at : at + PART] = diff_ref[:, lanes(half * HALF + other * PART, PART)].astype(jnp.bfloat16)
        side = half * HALF + 2 * PART
        sent_ref[:, at + PART : at + SENT] = diff_ref[:, side : side + SIDE].astype(jnp.bfloat16)


def weight_kernel(anchor_ref, momentum_ref, diff_ref, received_ref, keep_ref, give_ref):
    island, core = lax.axis_index("yl"), lax.axis_index("core")
    for out_ref, half in ((keep_ref, core), (give_ref, 1 - core)):
        for at, src, size in (
            (0, half * HALF + island * PART, PART),
            (PART, half * HALF + 2 * PART, SIDE),
        ):
            cols = lanes(src, size)
            got = received_ref[:, lanes(half * SENT + at, size)].astype(jnp.float32)
            new, _ = outer(anchor_ref[:, cols], momentum_ref[:, cols], diff_ref[:, cols] + got)
            out_ref[:, at : at + size] = new


def join_kernel(keep_ref, got_ref, *refs):
    outs, rows_ref = refs[:-1], refs[-1]
    core = lax.axis_index("core")
    rows_ref[pl.ds(pl.multiple_of(core * ROWS, 8), ROWS), :] = keep_ref[...]
    rows_ref[pl.ds(pl.multiple_of((1 - core) * ROWS, 8), ROWS), :] = got_ref[...]
    for i, out_ref in enumerate(outs):
        out_ref[0] = rows_ref[:, i * GROUP : (i + 1) * GROUP].astype(jnp.bfloat16)


def adam_kernel(frag_ref, plan_ref, p_ref, g_ref, m_ref, v_ref, p_out, m_out, v_out):
    chosen = chosen_of(frag_ref, plan_ref)
    frozen = pl.program_id(0) == chosen

    @pl.when(frozen)
    def _():
        p_out[...] = p_ref[...]
        m_out[...] = m_ref[...]
        v_out[...] = v_ref[...]

    @pl.when(jnp.logical_not(frozen))
    def _():
        grad = g_ref[...].astype(jnp.float32)
        first = beta_one * m_ref[...] + (1.0 - beta_one) * grad
        second = beta_two * v_ref[...] + (1.0 - beta_two) * grad * grad
        first_hat = first * (1.0 / (1.0 - beta_one**STEP))
        second_hat = second * (1.0 / (1.0 - beta_two**STEP))
        p_out[...] = p_ref[...] * (1.0 - inner_rate * decay_rate) - inner_rate * first_hat / (
            jnp.sqrt(second_hat) + adam_eps
        )
        m_out[...] = first
        v_out[...] = second


def outer_kernel(frag_ref, plan_ref, anchor_ref, momentum_ref, diff_ref, got_ref, held_ref, momentum_out, p_out):
    new, momentum_new = outer(anchor_ref[...], momentum_ref[...], diff_ref[...] + got_ref[...])
    momentum_out[...] = momentum_new
    p_out[0, 0] = new


TILE = 256


def result_columns(group, half):
    return [half * HALF + group * GROUP, half * HALF + PART + group * GROUP]


def multiply(step, mine_ref, theirs_ref, weight, out_ref, result_ref, staged, sem, columns):
    n = TOK // TILE

    @pl.when(step < n)
    def _():
        out_ref[...] = jnp.dot(theirs_ref[...], weight(), preferred_element_type=jnp.float32).astype(jnp.bfloat16)

    @pl.when(step >= n)
    def _():
        staged[...] = jnp.dot(mine_ref[...], weight(), preferred_element_type=jnp.float32).astype(jnp.bfloat16)
        rows = pl.ds(pl.multiple_of((step - n) * TILE, TILE), TILE)
        copies = [
            pltpu.make_async_copy(
                staged.at[:, i * GROUP : (i + 1) * GROUP], result_ref.at[rows, lanes(at, GROUP)], sem.at[i]
            )
            for i, at in enumerate(columns)
        ]
        for copy in copies:
            copy.start()
        for copy in copies:
            copy.wait()


def group_kernel(group, has_buffer, mine_ref, theirs_ref, *refs):
    pieces, refs = refs[:4], refs[4 + has_buffer :]
    result_ref, out_ref, weight, staged, sem, load_sem = refs
    step = pl.program_id(0)
    core = lax.axis_index("core")

    @pl.when(step == 0)
    def _():
        here = lax.axis_index("z") * 16 + lax.axis_index("x") * 4 + lax.axis_index("yh") * 2 + lax.axis_index("yl")
        masks = [code_masks(group, c) for c in (0, 1)]
        for r in range(64):
            code = here ^ jnp.where(core == 0, masks[0][r], masks[1][r])
            pltpu.make_async_copy(
                pieces[r // 16].at[r % 16],
                weight.at[code // 2, :, lanes(code % 2 * GROUP, GROUP)],
                load_sem,
            ).start()
        pltpu.make_async_copy(weight, weight, load_sem).wait()

    multiply(
        step, mine_ref, theirs_ref, lambda: weight[...].reshape(D, 2 * GROUP),
        out_ref, result_ref, staged, sem, result_columns(group, core),
    )


def side_kernel(mine_ref, theirs_ref, weight_ref, result_ref, out_ref, staged, sem):
    core = lax.axis_index("core")
    multiply(
        pl.program_id(0), mine_ref, theirs_ref, lambda: weight_ref[...],
        out_ref, result_ref, staged, sem, [core * HALF + 2 * PART],
    )


def place_kernel(buffer_ref, *refs):
    received, result_ref, sem = refs[:-2], refs[-2], refs[-1]
    half = 1 - lax.axis_index("core")
    copies = []
    for group, got in enumerate(received):
        columns = result_columns(group, half) if group < GROUPS else [half * HALF + 2 * PART]
        for i, at in enumerate(columns):
            copies.append(
                pltpu.make_async_copy(
                    got.at[:, i * GROUP : (i + 1) * GROUP], result_ref.at[:, lanes(at, GROUP)], sem.at[len(copies)]
                )
            )
    for copy in copies:
        copy.start()
    for copy in copies:
        copy.wait()


ANY = pl.BlockSpec(memory_space=pl.ANY)
VMEM = pl.BlockSpec(memory_space=pltpu.VMEM)
LIMIT = pltpu.CompilerParams(vmem_limit_bytes=48 * 2**20)


def shape(dims, dtype):
    return jax.ShapeDtypeStruct(dims, dtype)


def cost(flops, moved):
    return pl.CostEstimate(flops=flops, bytes_accessed=moved, transcendentals=0)


def token_specs():
    n = TOK // TILE
    return [
        pl.BlockSpec((TILE, D), lambda i: (jnp.maximum(i - n, 0), 0)),
        pl.BlockSpec((TILE, D), lambda i: (jnp.minimum(i, n - 1), 0)),
    ]


def multiply_call(kernel, extra, extra_specs, tokens, others, width, scratch, buffer):
    n = TOK // TILE
    args = [tokens, others, *extra] + ([] if buffer is None else [buffer])
    return pl.pallas_call(
        kernel,
        grid=(2 * n,),
        in_specs=token_specs() + extra_specs + ([] if buffer is None else [ANY]),
        out_specs=[ANY, pl.BlockSpec((TILE, width), lambda i: (jnp.minimum(i, n - 1), 0))],
        out_shape=[shape((TOK, D), jnp.bfloat16), shape((TOK, width), jnp.bfloat16)],
        scratch_shapes=scratch + [
            pltpu.VMEM((TILE, width), jnp.bfloat16),
            pltpu.SemaphoreType.DMA((width // GROUP,)),
        ] + ([pltpu.SemaphoreType.DMA] if scratch else []),
        input_output_aliases={} if buffer is None else {len(args) - 1: 0},
        compiler_params=LIMIT,
        cost_estimate=cost(2 * 2 * TOK * D * width, 4 * TOK * D + 2 * D * width),
    )(*args)


def body(inner_params, inner_grads, adam_first, adam_second, anchor, momentum, tokens, frag_index, plan):
    f32, bf16 = jnp.float32, jnp.bfloat16
    others = swap_cores(tokens)

    def layer(i, frag_ref, plan_ref):
        return (0, chosen_of(frag_ref, plan_ref), 0, 0)

    def whole(i, frag_ref, plan_ref):
        return (0, 0)

    block = pl.BlockSpec((ROWS, D), whole)
    diff, sent = pl.pallas_call(
        diff_kernel,
        grid_spec=pltpu.PrefetchScalarGridSpec(
            num_scalar_prefetch=2,
            grid=(1,),
            in_specs=[block, pl.BlockSpec((1, 1, ROWS, D), layer)],
            out_specs=[block, pl.BlockSpec((ROWS, 2 * SENT), whole)],
        ),
        out_shape=[shape((ROWS, D), f32), shape((ROWS, 2 * SENT), bf16)],
        compiler_params=LIMIT,
    )(frag_index, plan, anchor, inner_params)
    islands = [(0, 1), (1, 0)]
    received = lax.ppermute(sent, "yl", islands)
    keep, give = pl.pallas_call(
        weight_kernel,
        in_specs=[VMEM] * 4,
        out_specs=[VMEM] * 2,
        out_shape=[shape((ROWS, SENT), f32)] * 2,
        compiler_params=LIMIT,
    )(anchor, momentum, diff, received)
    got = swap_cores(give)
    *cur, side = pl.pallas_call(
        join_kernel,
        in_specs=[VMEM] * 2,
        out_specs=[VMEM] * (GROUPS + 1),
        out_shape=[shape((1, CHIP, GROUP), bf16)] * (GROUPS + 1),
        scratch_shapes=[pltpu.VMEM((CHIP, SENT), f32)],
        compiler_params=LIMIT,
    )(keep, got)

    side_weight = lax.all_gather(side[0], CHIPS, axis=0, tiled=True)
    for step in range(4):
        arrived = [exchange(cur[q], q, step) for q in range(GROUPS)]
        cur = [jnp.concatenate([cur[q], arrived[q]], axis=0) for q in range(GROUPS)]
    fifth = [exchange(cur[q], q, 4) for q in range(GROUPS)]
    sixth = [exchange(cur[q], q, 5) for q in range(GROUPS)]
    last = [exchange(fifth[q], q, 5) for q in range(GROUPS)]

    width = 896
    stepped = pl.BlockSpec((1, 1, ROWS, width), lambda i, j, *_: (0, i, 0, j))
    state = shape((1, LAYERS, ROWS, D), f32)
    params_held, first_out, second_out = pl.pallas_call(
        adam_kernel,
        grid_spec=pltpu.PrefetchScalarGridSpec(
            num_scalar_prefetch=2,
            grid=(LAYERS, pl.cdiv(D, width)),
            in_specs=[stepped] * 4,
            out_specs=[stepped] * 3,
        ),
        out_shape=[state] * 3,
        compiler_params=LIMIT,
        cost_estimate=cost(20 * LAYERS * ROWS * D, 26 * LAYERS * ROWS * D),
    )(frag_index, plan, inner_params, inner_grads, adam_first, adam_second)

    diff_other = lax.ppermute(diff, "yl", islands)
    momentum_out, params_out = pl.pallas_call(
        outer_kernel,
        grid_spec=pltpu.PrefetchScalarGridSpec(
            num_scalar_prefetch=2,
            grid=(1,),
            in_specs=[block] * 4 + [ANY],
            out_specs=[block, pl.BlockSpec((1, 1, ROWS, D), layer)],
        ),
        out_shape=[shape((ROWS, D), f32), state],
        input_output_aliases={6: 1},
        compiler_params=LIMIT,
    )(frag_index, plan, anchor, momentum, diff, diff_other, params_held)

    result, out = multiply_call(side_kernel, [side_weight], [VMEM], tokens, others, SIDE, [], None)
    swapped = [swap_cores(out)]
    for q in range(GROUPS):
        result, out = multiply_call(
            functools.partial(group_kernel, q, 1), [cur[q], fifth[q], sixth[q], last[q]], [ANY] * 4, tokens, others,
            2 * GROUP, [pltpu.VMEM((D // CHIP, CHIP, 2 * GROUP), bf16)], result,
        )
        swapped.insert(q, swap_cores(out))
    projected = pl.pallas_call(
        place_kernel,
        in_specs=[ANY] * (GROUPS + 2),
        out_specs=ANY,
        out_shape=shape((TOK, D), bf16),
        scratch_shapes=[pltpu.SemaphoreType.DMA((2 * GROUPS + 1,))],
        input_output_aliases={0: 0},
        compiler_params=LIMIT,
    )(result, *swapped)
    return (params_out, first_out, second_out, momentum_out, projected)


def solution(mesh):
    torus = Mesh(np.asarray(mesh.devices).reshape(2, 4, 4, 2, 2), ALL)
    fsdp = ("z", "x", "yh", "core")
    state = P("yl", None, fsdp, None)
    rows = P(fsdp, None)
    tokens = P(ALL, None)
    return jax.shard_map(
        body,
        mesh=torus,
        in_specs=(state, state, state, state, rows, rows, tokens, P(), P()),
        out_specs=(state, state, state, rows, tokens),
        check_vma=False,
    )
```

time: 230 us -> 158 us (0.69)
  waiting for transfers between devices: 171 us -> 51.1 us
  Pallas kernels: 0 us -> 51.3 us
  starting transfers between devices: 0.08 us -> 30 us
  matrix products: 21 us -> 0 us
  other arithmetic: 15.6 us -> 0.26 us
  local copies, waits for them, and re-layouts: 5.92 us -> 9.5 us
    all_gather x1, waiting for transfers between devices: 126 us -> 4.93 us  [body(): side_weight = lax.all_gather(side[0], CHIPS, axis=0, tiled=True)]
    pallas_call x0 -> x10, Pallas kernels: none -> 51.3 us  [the longest x4 36.9 us: multiply_call(): pl.pallas_call(kernel, grid=(2 * n,), in_specs=token_specs() + extra_spec...]
    ppermute x0 -> x29, waiting for transfers between devices: none -> 46.2 us  [the longest x21 40.2 us: exchange(): lax.ppermute(value, ALL, [(i, flipped(i, flips[i % 2])) for i in range(12...]
    psum x1 -> x0, waiting for transfers between devices: 44.6 us -> none  [body(): summed = lax.psum(local_diff, 'island')]
    ppermute x0 -> x29, starting transfers between devices: none -> 29.9 us  [the longest x21 22.1 us: exchange(): lax.ppermute(value, ALL, [(i, flipped(i, flips[i % 2])) for i in range(12...]
    dot_general x1 -> x0, matrix products: 21 us -> none  [body(): jnp.dot(tokens, lax.all_gather(weight_bf, 'fsdp', axis=0, tiled=True), pr...]
    select_n x1 -> x0, other arithmetic: 8.37 us -> none  [body(): second_out = jnp.where(is_frag, adam_second, second_new)]
    convert_element_type x1 -> x0, other arithmetic: 2.93 us -> none  [body(): weight_bf = new_anchor.astype(jnp.bfloat16)]
  transfers between devices with their start and end apart: 2 -> 30, of which waited for: 2 -> 11; matrix products, arithmetic and copies ran while one was open for 4% -> 2% of each run, Pallas kernels for 0% -> 31%
where the time goes in v1:
time: 158 us; the launch traced here: 157 us
  Pallas kernels  51.3 us (32%)
  waiting for transfers between devices  51.1 us (32%)
  starting transfers between devices  30 us (19%)
  between operations  15 us (9%)
  local copies, waits for them, and re-layouts  9.5 us (6%)
    ppermute x21, waiting for transfers between devices, exchange(): lax.ppermute(value, ALL, [(i, flipped(i, flips[i % 2])) for i in range(12...  40.2 us
    pallas_call x4, Pallas kernels, multiply_call(): pl.pallas_call(kernel, grid=(2 * n,), in_specs=token_specs() + extra_spec...  36.9 us
    ppermute x21, starting transfers between devices, exchange(): lax.ppermute(value, ALL, [(i, flipped(i, flips[i % 2])) for i in range(12...  22.1 us
    pallas_call x1, Pallas kernels, body(): pl.pallas_call(adam_kernel, grid_spec=pltpu.PrefetchScalarGridSpec(num_sc...  9.68 us
    unnamed x39, local copies, waits for them, and re-layouts  8.64 us
    ppermute x6, starting transfers between devices, swap_cores(): return lax.ppermute(value, 'core', [(0, 1), (1, 0)])  5.01 us
    all_gather x1, waiting for transfers between devices, body(): side_weight = lax.all_gather(side[0], CHIPS, axis=0, tiled=True)  4.93 us
    ppermute x1, waiting for transfers between devices, body(): received = lax.ppermute(sent, 'yl', islands)  4.92 us
  transfers between devices with their start and end apart: 30, of which 11 were waited for; matrix products, arithmetic and copies ran while one was open for 2% of the time, Pallas kernels for 31%

profile of v1, /device:TPU:1, one launch (start us, length us, event | category | flops | bytes accessed | tf_op | source)
XLA Modules:
  0.0 157.2 jit_solution(14411498953336748101)
XLA Ops:
  7.2 0.0 all-gather.3.cloned.1.call-start
  7.9 0.0 copy-start
  7.9 1.7 %copy-done = f32[1,3,56,3584]{3,2,1,0:T(8,128)S(1)} copy-done((f32[1,3,56,3584]{3,2,1,0:T(8,128)S(1)}, f32[1,3,56,3584]{3,2,1,0:T(8,128)}, u32[]{:S(2)}) %copy-start) | copy-done | bytes 2408472
  9.5 1.1 copy-done.2
  10.7 0.7 copy-done.12
  11.3 0.6 shard_map.128
  12.0 2.2 %collective-permute-start.2 = (bf16[56,2048]{1,0:T(8,128)(2,1)S(1)}, bf16[56,2048]{1,0:T(8,128)(2,1)S(1)}, u32[]{:S(2)}, u32[]{:S(2)}) collective-permute-start(bf16[56,2048]{1,0:T(8,128)(2,1)S(1)} %get-tuple-element.32), channel_id=1, source_target_pairs={{0,64},{64,0},{1,65},{65,1},{2,66},{66,2},{3,67},{67,3},{4,68},{68... | collective-permute-start | bytes 688136 | tf_op jit(solution)/shard_map/ppermute | solution.py:287
  14.2 4.9 %collective-permute-done.2.received_ref = bf16[56,2048]{1,0:T(8,128)(2,1)S(1)} collective-permute-done((bf16[56,2048]{1,0:T(8,128)(2,1)S(1)}, bf16[56,2048]{1,0:T(8,128)(2,1)S(1)}, u32[]{:S(2)}, u32[]{:S(2)}) %collective-permute-start.2) | collective-permute-done | bytes 229408 | tf_op jit(solution)/shard_map/ppermute | solution.py:287
  19.1 0.1 shard_map.131
  19.3 1.7 %collective-permute-start.3 = (f32[56,1024]{1,0:T(8,128)S(1)}, f32[56,1024]{1,0:T(8,128)S(1)}, u32[]{:S(2)}, u32[]{:S(2)}) collective-permute-start(f32[56,1024]{1,0:T(8,128)S(1)} %get-tuple-element.34), channel_id=1, source_target_pairs={{0,1},{1,0},{2,3},{3,2},{4,5},{5,4},{6,7},{7,6},{8,9},{9,8},{10,11... | collective-permute-start | bytes 688136 | tf_op jit(solution)/shard_map/ppermute | solution.py:63
  21.0 0.1 collective-permute-start.1
  21.1 1.0 collective-permute-done.3.got_ref
  22.1 0.7 shard_map.132
  22.8 0.0 all-gather.3.cloned.1.call-update
  22.8 3.0 %collective-permute-start.11 = (bf16[1,112,256]{2,1,0:T(8,128)(2,1)S(1)}, bf16[1,112,256]{2,1,0:T(8,128)(2,1)S(1)}, u32[]{:S(2)}, u32[]{:S(2)}) collective-permute-start(bf16[1,112,256]{2,1,0:T(8,128)(2,1)S(1)} %get-tuple-element.36), channel_id=1, source_target_pairs={{0,64},{1,67},{2,66},{3,65},{4,68},{5,71},{6,70},{7,69},{8,72},{9,... | collective-permute-start | bytes 172040 | tf_op jit(solution)/shard_map/ppermute | solution.py:53
  25.8 0.6 constant_dynamic-update-slice_fusion.4
  26.4 3.8 %collective-permute-start.4 = (bf16[1,112,256]{2,1,0:T(8,128)(2,1)S(1)}, bf16[1,112,256]{2,1,0:T(8,128)(2,1)S(1)}, u32[]{:S(2)}, u32[]{:S(2)}) collective-permute-start(bf16[1,112,256]{2,1,0:T(8,128)(2,1)S(1)} %get-tuple-element.35), channel_id=1, source_target_pairs={{0,16},{1,49},{2,18},{3,51},{4,20},{5,53},{6,22},{7,55},{8,24},{9,... | collective-permute-start | bytes 172040 | tf_op jit(solution)/shard_map/ppermute | solution.py:53
  30.2 2.5 %collective-permute-start.18 = (bf16[1,112,256]{2,1,0:T(8,128)(2,1)S(1)}, bf16[1,112,256]{2,1,0:T(8,128)(2,1)S(1)}, u32[]{:S(2)}, u32[]{:S(2)}) collective-permute-start(bf16[1,112,256]{2,1,0:T(8,128)(2,1)S(1)} %get-tuple-element.37), channel_id=1, source_target_pairs={{0,4},{1,13},{2,6},{3,15},{4,0},{5,9},{6,2},{7,11},{8,12},{9,5},{1... | collective-permute-start | bytes 172040 | tf_op jit(solution)/shard_map/ppermute | solution.py:53
  32.7 1.8 %collective-permute-done.18 = bf16[1,112,256]{2,1,0:T(8,128)(2,1)S(1)} collective-permute-done((bf16[1,112,256]{2,1,0:T(8,128)(2,1)S(1)}, bf16[1,112,256]{2,1,0:T(8,128)(2,1)S(1)}, u32[]{:S(2)}, u32[]{:S(2)}) %collective-permute-start.18) | collective-permute-done | bytes 57376 | tf_op jit(solution)/shard_map/ppermute | solution.py:53
  34.4 0.1 collective-permute-start.19
  34.6 0.1 collective-permute-start.12
  34.7 0.4 collective-permute-start.5
  35.0 0.6 constant_dynamic-update-slice_fusion.8
  35.7 3.7 %collective-permute-done.19 = bf16[2,112,256]{2,1,0:T(8,128)(2,1)S(1)} collective-permute-done((bf16[2,112,256]{2,1,0:T(8,128)(2,1)S(1)}, bf16[2,112,256]{2,1,0:T(8,128)(2,1)S(1)}, u32[]{:S(2)}, u32[]{:S(2)}) %collective-permute-start.19) | collective-permute-done | bytes 114720 | tf_op jit(solution)/shard_map/ppermute | solution.py:53
  39.4 0.1 collective-permute-start.20
  39.5 0.4 collective-permute-start.13
  39.9 0.1 collective-permute-start.6
  40.0 6.1 %collective-permute-done.20 = bf16[4,112,256]{2,1,0:T(8,128)(2,1)S(1)} collective-permute-done((bf16[4,112,256]{2,1,0:T(8,128)(2,1)S(1)}, bf16[4,112,256]{2,1,0:T(8,128)(2,1)S(1)}, u32[]{:S(2)}, u32[]{:S(2)}) %collective-permute-start.20) | collective-permute-done | bytes 229408 | tf_op jit(solution)/shard_map/ppermute | solution.py:53
  46.2 0.1 collective-permute-start.21
  46.3 0.7 constant_dynamic-update-slice_fusion.7
  47.0 0.1 collective-permute-start.14
  47.2 6.8 %collective-permute-done.21 = bf16[8,112,256]{2,1,0:T(8,128)(2,1)S(1)} collective-permute-done((bf16[8,112,256]{2,1,0:T(8,128)(2,1)S(1)}, bf16[8,112,256]{2,1,0:T(8,128)(2,1)S(1)}, u32[]{:S(2)}, u32[]{:S(2)}) %collective-permute-start.21) | collective-permute-done | bytes 458784 | tf_op jit(solution)/shard_map/ppermute | solution.py:53
  54.0 0.1 collective-permute-start.22
  54.2 0.1 collective-permute-start.7
  54.3 0.7 constant_dynamic-update-slice_fusion.6
  55.0 1.4 collective-permute-start.23
  56.4 0.8 constant_dynamic-update-slice_fusion.5.refs_0_
  57.2 0.0 collective-permute-start.15
  57.3 5.1 %collective-permute-done.7 = bf16[8,112,256]{2,1,0:T(8,128)(2,1)S(1)} collective-permute-done((bf16[8,112,256]{2,1,0:T(8,128)(2,1)S(1)}, bf16[8,112,256]{2,1,0:T(8,128)(2,1)S(1)}, u32[]{:S(2)}, u32[]{:S(2)}) %collective-permute-start.7) | collective-permute-done | bytes 458784 | tf_op jit(solution)/shard_map/ppermute | solution.py:53
  62.4 2.5 %collective-permute-start.8 = (bf16[16,112,256]{2,1,0:T(8,128)(2,1)S(1)}, bf16[16,112,256]{2,1,0:T(8,128)(2,1)}, u32[]{:S(2)}, u32[]{:S(2)}) collective-permute-start(bf16[16,112,256]{2,1,0:T(8,128)(2,1)S(1)} %constant_dynamic-update-slice_fusion.refs_0_), channel_id=1, source_target_pairs={{0,4},{1,13},{2,6},{3,15},{4,0},{5,9},{6,2},{7,11},{8,12},{9,5},{1... | collective-permute-start | bytes 2752520 | tf_op jit(solution)/shard_map/ppermute | solution.py:53
  64.9 3.5 %collective-permute-done.22.refs_1_ = bf16[16,112,256]{2,1,0:T(8,128)(2,1)} collective-permute-done((bf16[16,112,256]{2,1,0:T(8,128)(2,1)S(1)}, bf16[16,112,256]{2,1,0:T(8,128)(2,1)}, u32[]{:S(2)}, u32[]{:S(2)}) %collective-permute-start.22) | collective-permute-done | bytes 917536 | tf_op jit(solution)/shard_map/ppermute | solution.py:53
  68.4 4.7 %collective-permute-done.23.refs_2_ = bf16[16,112,256]{2,1,0:T(8,128)(2,1)S(1)} collective-permute-done((bf16[16,112,256]{2,1,0:T(8,128)(2,1)S(1)}, bf16[16,112,256]{2,1,0:T(8,128)(2,1)S(1)}, u32[]{:S(2)}, u32[]{:S(2)}) %collective-permute-start.23) | collective-permute-done | bytes 917536 | tf_op jit(solution)/shard_map/ppermute | solution.py:53
  73.1 0.9 copy-done.10
  74.0 2.4 %collective-permute-start.16 = (bf16[16,112,256]{2,1,0:T(8,128)(2,1)}, bf16[16,112,256]{2,1,0:T(8,128)(2,1)}, u32[]{:S(2)}, u32[]{:S(2)}) collective-permute-start(bf16[16,112,256]{2,1,0:T(8,128)(2,1)} %constant_dynamic-update-slice_fusion.5.refs_0_), channel_id=1, source_target_pairs={{0,4},{1,13},{2,6},{3,15},{4,0},{5,9},{6,2},{7,11},{8,12},{9,5},{1... | collective-permute-start | bytes 2752520 | tf_op jit(solution)/shard_map/ppermute | solution.py:53
  76.4 8.6 %collective-permute-done.15.refs_1_ = bf16[16,112,256]{2,1,0:T(8,128)(2,1)} collective-permute-done((bf16[16,112,256]{2,1,0:T(8,128)(2,1)}, bf16[16,112,256]{2,1,0:T(8,128)(2,1)}, u32[]{:S(2)}, u32[]{:S(2)}) %collective-permute-start.15) | collective-permute-done | bytes 917536 | tf_op jit(solution)/shard_map/ppermute | solution.py:53
  85.0 2.4 %collective-permute-start.17 = (bf16[16,112,256]{2,1,0:T(8,128)(2,1)}, bf16[16,112,256]{2,1,0:T(8,128)(2,1)}, u32[]{:S(2)}, u32[]{:S(2)}) collective-permute-start(bf16[16,112,256]{2,1,0:T(8,128)(2,1)} %collective-permute-done.15.refs_1_), channel_id=1, source_target_pairs={{0,4},{1,13},{2,6},{3,15},{4,0},{5,9},{6,2},{7,11},{8,12},{9,5},{1... | collective-permute-start | bytes 2752520 | tf_op jit(solution)/shard_map/ppermute | solution.py:53
  87.5 2.7 %collective-permute-start.10 = (bf16[16,112,256]{2,1,0:T(8,128)(2,1)}, bf16[16,112,256]{2,1,0:T(8,128)(2,1)}, u32[]{:S(2)}, u32[]{:S(2)}) collective-permute-start(bf16[16,112,256]{2,1,0:T(8,128)(2,1)} %collective-permute-done.8.refs_1_), channel_id=1, source_target_pairs={{0,64},{1,67},{2,66},{3,65},{4,68},{5,71},{6,70},{7,69},{8,72},{9,... | collective-permute-start | bytes 2752520 | tf_op jit(solution)/shard_map/ppermute | solution.py:53
  90.1 4.9 %all-gather.3.cloned.1.call-done = bf16[1,3584,256]{2,1,0:T(8,128)(2,1)} async-done(((bf16[1,112,256]{2,1,0:T(8,128)(2,1)}), bf16[1,3584,256]{2,1,0:T(8,128)(2,1)}) %all-gather.3.cloned.1.call-update) | async-done | bytes 1835024 | tf_op jit(solution)/shard_map/all_gather | solution.py:305
  95.1 1.5 copy-done.6
  96.6 6.3 %shard_map.133 = (bf16[512,3584]{1,0:T(8,128)(2,1)}, bf16[512,256]{1,0:T(8,128)(2,1)S(1)}) custom-call(bf16[512,3584]{1,0:T(8,128)(2,1)} %mine_ref.7, bf16[512,3584]{1,0:T(8,128)(2,1)} %collective-permute-done.1.theirs_ref, bf16[3584,256]{1,0:T(8,128)(2,1)S(1)} %bitcast.1), custom_call_target="tpu_custom_call" | custom-call | flops 1879048192 | bytes 9175040 | tf_op jit(solution)/shard_map/pallas_call | solution.py:248
  102.9 0.6 collective-permute-start
  103.5 9.8 %shard_map.134 = (bf16[512,3584]{1,0:T(8,128)(2,1)}, bf16[512,512]{1,0:T(8,128)(2,1)S(1)}) custom-call(bf16[512,3584]{1,0:T(8,128)(2,1)} %mine_ref.7, bf16[512,3584]{1,0:T(8,128)(2,1)} %collective-permute-done.1.theirs_ref, bf16[16,112,256]{2,1,0:T(8,128)(2,1)S(1)} %copy-done.9, ...), custom_call_target="tpu_custom_call", output_to_operand_aliasing={{0}: (6, {})} | custom-call | flops 3758096384 | bytes 11010048 | tf_op jit(solution)/shard_map/pallas_call | solution.py:248
  113.3 10.0 %shard_map.135 = (bf16[512,3584]{1,0:T(8,128)(2,1)}, bf16[512,512]{1,0:T(8,128)(2,1)S(1)}) custom-call(bf16[512,3584]{1,0:T(8,128)(2,1)} %mine_ref.7, bf16[512,3584]{1,0:T(8,128)(2,1)} %collective-permute-done.1.theirs_ref, bf16[16,112,256]{2,1,0:T(8,128)(2,1)} %constant_dynamic-update-slice_fusion.5.refs_0_, ...), custom_call_target="tpu_custom_call", output_to_operand_aliasing={{0}: (6, {})} | custom-call | flops 3758096384 | bytes 11010048 | tf_op jit(solution)/shard_map/pallas_call | solution.py:248
  123.3 0.0 copy-start.1
  123.3 0.0 copy-start.5
  123.4 0.0 copy-start.13
  123.4 10.8 %shard_map.136 = (bf16[512,3584]{1,0:T(8,128)(2,1)}, bf16[512,512]{1,0:T(8,128)(2,1)S(1)}) custom-call(bf16[512,3584]{1,0:T(8,128)(2,1)} %mine_ref.7, bf16[512,3584]{1,0:T(8,128)(2,1)} %collective-permute-done.1.theirs_ref, bf16[16,112,256]{2,1,0:T(8,128)(2,1)S(1)} %constant_dynamic-update-slice_fusion.refs_0_, ...), custom_call_target="tpu_custom_call", output_to_operand_aliasing={{0}: (6, {})} | custom-call | flops 3758096384 | bytes 11010048 | tf_op jit(solution)/shard_map/pallas_call | solution.py:248
  134.2 2.6 %collective-permute-start.27 = (bf16[512,512]{1,0:T(8,128)(2,1)S(1)}, bf16[512,512]{1,0:T(8,128)(2,1)S(1)}, u32[]{:S(2)}, u32[]{:S(2)}) collective-permute-start(bf16[512,512]{1,0:T(8,128)(2,1)S(1)} %get-tuple-element.45), channel_id=1, source_target_pairs={{0,1},{1,0},{2,3},{3,2},{4,5},{5,4},{6,7},{7,6},{8,9},{9,8},{10,11... | collective-permute-start | bytes 1572872 | tf_op jit(solution)/shard_map/ppermute | solution.py:63
  136.8 0.1 collective-permute-start.26
  136.9 0.4 collective-permute-start.25
  137.3 0.1 collective-permute-start.28
  137.4 9.7 %shard_map.129 = (f32[1,3,56,3584]{3,2,1,0:T(8,128)}, f32[1,3,56,3584]{3,2,1,0:T(8,128)}, f32[1,3,56,3584]{3,2,1,0:T(8,128)}) custom-call(s32[1]{0:T(128)S(6)} %copy.36.frag_ref, s32[3]{0:T(128)S(1)} %copy-done.13, f32[1,3,56,3584]{3,2,1,0:T(8,128)S(1)} %copy-done.1, bf16[1,3,56,3584]{3,2,1,0:T(8,128)(2,1)S(1)} %copy-done.7, ...), custom_call_target="tpu_custom_call" | custom-call | flops 12042240 | bytes 15654912 | tf_op jit(solution)/shard_map/pallas_call | solution.py:316
  147.1 1.9 %shard_map.130 = (f32[56,3584]{1,0:T(8,128)}, f32[1,3,56,3584]{3,2,1,0:T(8,128)}) custom-call(s32[1]{0:T(128)S(6)} %copy.36.frag_ref, s32[3]{0:T(128)S(1)} %copy-done.13, f32[56,3584]{1,0:T(8,128)S(1)} %copy-done.3, f32[56,3584]{1,0:T(8,128)S(1)} %copy-done.4, f32[56,3584]{1,0:T(8,128)S(1)} %get-tuple-element.26.diff_ref, ...), custom_call_target="tpu_custom_call", output_to_operand_aliasing={{1}: (6, {})} | custom-call | tf_op jit(solution)/shard_map/pallas_call | solution.py:330
  149.0 1.3 shard_map.137
  (58 shorter events, 0.5 us)
Async XLA Ops:
  7.2 87.9 %all-gather.3.cloned.1.call-start = ((), (), s32[]{:S(2)}) async-start(), calls=%async_computation | async-start | bytes 1892352 | tf_op jit(solution)/shard_map/all_gather | solution.py:305
  7.9 1.7 %copy-start = (f32[1,3,56,3584]{3,2,1,0:T(8,128)S(1)}, f32[1,3,56,3584]{3,2,1,0:T(8,128)}, u32[]{:S(2)}) copy-start(f32[1,3,56,3584]{3,2,1,0:T(8,128)} %p_ref.1) | copy-start | bytes 7225348
  9.5 1.1 copy-start.2
  10.7 0.7 copy-start.12
  11.3 7.8 %copy-start.3 = (f32[56,3584]{1,0:T(8,128)S(1)}, f32[56,3584]{1,0:T(8,128)}, u32[]{:S(2)}) copy-start(f32[56,3584]{1,0:T(8,128)} %anchor_ref.5) | copy-start | bytes 2408452
  11.3 7.8 %copy-start.4 = (f32[56,3584]{1,0:T(8,128)S(1)}, f32[56,3584]{1,0:T(8,128)}, u32[]{:S(2)}) copy-start(f32[56,3584]{1,0:T(8,128)} %momentum_ref.3) | copy-start | bytes 2408452
  12.0 7.1 %collective-permute-start.2 = (bf16[56,2048]{1,0:T(8,128)(2,1)S(1)}, bf16[56,2048]{1,0:T(8,128)(2,1)S(1)}, u32[]{:S(2)}, u32[]{:S(2)}) collective-permute-start(bf16[56,2048]{1,0:T(8,128)(2,1)S(1)} %get-tuple-element.32), channel_id=1, source_target_pairs={{0,64},{64,0},{1,65},{65,1},{2,66},{66,2},{3,67},{67,3},{4,68},{68... | collective-permute-start | bytes 688136 | tf_op jit(solution)/shard_map/ppermute | solution.py:287
  19.3 2.8 %collective-permute-start.3 = (f32[56,1024]{1,0:T(8,128)S(1)}, f32[56,1024]{1,0:T(8,128)S(1)}, u32[]{:S(2)}, u32[]{:S(2)}) collective-permute-start(f32[56,1024]{1,0:T(8,128)S(1)} %get-tuple-element.34), channel_id=1, source_target_pairs={{0,1},{1,0},{2,3},{3,2},{4,5},{5,4},{6,7},{7,6},{8,9},{9,8},{10,11... | collective-permute-start | bytes 688136 | tf_op jit(solution)/shard_map/ppermute | solution.py:63
  21.0 66.5 %collective-permute-start.1 = (bf16[512,3584]{1,0:T(8,128)(2,1)}, bf16[512,3584]{1,0:T(8,128)(2,1)}, u32[]{:S(2)}, u32[]{:S(2)}) collective-permute-start(bf16[512,3584]{1,0:T(8,128)(2,1)} %mine_ref.7), channel_id=1, source_target_pairs={{0,1},{1,0},{2,3},{3,2},{4,5},{5,4},{6,7},{7,6},{8,9},{9,8},{10,11... | collective-permute-start | bytes 11010056 | tf_op jit(solution)/shard_map/ppermute | solution.py:63
  22.8 11.7 %collective-permute-start.11 = (bf16[1,112,256]{2,1,0:T(8,128)(2,1)S(1)}, bf16[1,112,256]{2,1,0:T(8,128)(2,1)S(1)}, u32[]{:S(2)}, u32[]{:S(2)}) collective-permute-start(bf16[1,112,256]{2,1,0:T(8,128)(2,1)S(1)} %get-tuple-element.36), channel_id=1, source_target_pairs={{0,64},{1,67},{2,66},{3,65},{4,68},{5,71},{6,70},{7,69},{8,72},{9,... | collective-permute-start | bytes 172040 | tf_op jit(solution)/shard_map/ppermute | solution.py:53
  26.4 8.2 %collective-permute-start.4 = (bf16[1,112,256]{2,1,0:T(8,128)(2,1)S(1)}, bf16[1,112,256]{2,1,0:T(8,128)(2,1)S(1)}, u32[]{:S(2)}, u32[]{:S(2)}) collective-permute-start(bf16[1,112,256]{2,1,0:T(8,128)(2,1)S(1)} %get-tuple-element.35), channel_id=1, source_target_pairs={{0,16},{1,49},{2,18},{3,51},{4,20},{5,53},{6,22},{7,55},{8,24},{9,... | collective-permute-start | bytes 172040 | tf_op jit(solution)/shard_map/ppermute | solution.py:53
  30.2 4.2 %collective-permute-start.18 = (bf16[1,112,256]{2,1,0:T(8,128)(2,1)S(1)}, bf16[1,112,256]{2,1,0:T(8,128)(2,1)S(1)}, u32[]{:S(2)}, u32[]{:S(2)}) collective-permute-start(bf16[1,112,256]{2,1,0:T(8,128)(2,1)S(1)} %get-tuple-element.37), channel_id=1, source_target_pairs={{0,4},{1,13},{2,6},{3,15},{4,0},{5,9},{6,2},{7,11},{8,12},{9,5},{1... | collective-permute-start | bytes 172040 | tf_op jit(solution)/shard_map/ppermute | solution.py:53
  34.4 4.9 %collective-permute-start.19 = (bf16[2,112,256]{2,1,0:T(8,128)(2,1)S(1)}, bf16[2,112,256]{2,1,0:T(8,128)(2,1)S(1)}, u32[]{:S(2)}, u32[]{:S(2)}) collective-permute-start(bf16[2,112,256]{2,1,0:T(8,128)(2,1)S(1)} %pad_maximum_fusion.8), channel_id=1, source_target_pairs={{0,64},{1,67},{2,66},{3,65},{4,68},{5,71},{6,70},{7,69},{8,72},{9,... | collective-permute-start | bytes 344072 | tf_op jit(solution)/shard_map/ppermute | solution.py:53
  34.6 4.9 %collective-permute-start.12 = (bf16[2,112,256]{2,1,0:T(8,128)(2,1)S(1)}, bf16[2,112,256]{2,1,0:T(8,128)(2,1)S(1)}, u32[]{:S(2)}, u32[]{:S(2)}) collective-permute-start(bf16[2,112,256]{2,1,0:T(8,128)(2,1)S(1)} %pad_maximum_fusion.7), channel_id=1, source_target_pairs={{0,16},{1,49},{2,18},{3,51},{4,20},{5,53},{6,22},{7,55},{8,24},{9,... | collective-permute-start | bytes 344072 | tf_op jit(solution)/shard_map/ppermute | solution.py:53
  34.7 5.2 %collective-permute-start.5 = (bf16[2,112,256]{2,1,0:T(8,128)(2,1)S(1)}, bf16[2,112,256]{2,1,0:T(8,128)(2,1)S(1)}, u32[]{:S(2)}, u32[]{:S(2)}) collective-permute-start(bf16[2,112,256]{2,1,0:T(8,128)(2,1)S(1)} %pad_maximum_fusion.6), channel_id=1, source_target_pairs={{0,12},{1,5},{2,14},{3,7},{4,8},{5,1},{6,10},{7,3},{8,4},{9,13},{1... | collective-permute-start | bytes 344072 | tf_op jit(solution)/shard_map/ppermute | solution.py:53
  39.4 6.8 %collective-permute-start.20 = (bf16[4,112,256]{2,1,0:T(8,128)(2,1)S(1)}, bf16[4,112,256]{2,1,0:T(8,128)(2,1)S(1)}, u32[]{:S(2)}, u32[]{:S(2)}) collective-permute-start(bf16[4,112,256]{2,1,0:T(8,128)(2,1)S(1)} %pad_maximum_fusion.5), channel_id=1, source_target_pairs={{0,16},{1,49},{2,18},{3,51},{4,20},{5,53},{6,22},{7,55},{8,24},{9,... | collective-permute-start | bytes 688136 | tf_op jit(solution)/shard_map/ppermute | solution.py:53
  39.5 7.4 %collective-permute-start.13 = (bf16[4,112,256]{2,1,0:T(8,128)(2,1)S(1)}, bf16[4,112,256]{2,1,0:T(8,128)(2,1)S(1)}, u32[]{:S(2)}, u32[]{:S(2)}) collective-permute-start(bf16[4,112,256]{2,1,0:T(8,128)(2,1)S(1)} %pad_maximum_fusion.4), channel_id=1, source_target_pairs={{0,12},{1,5},{2,14},{3,7},{4,8},{5,1},{6,10},{7,3},{8,4},{9,13},{1... | collective-permute-start | bytes 688136 | tf_op jit(solution)/shard_map/ppermute | solution.py:53
  39.9 14.2 %collective-permute-start.6 = (bf16[4,112,256]{2,1,0:T(8,128)(2,1)S(1)}, bf16[4,112,256]{2,1,0:T(8,128)(2,1)S(1)}, u32[]{:S(2)}, u32[]{:S(2)}) collective-permute-start(bf16[4,112,256]{2,1,0:T(8,128)(2,1)S(1)} %pad_maximum_fusion.3), channel_id=1, source_target_pairs={{0,66},{1,65},{2,64},{3,67},{4,70},{5,69},{6,68},{7,71},{8,74},{9,... | collective-permute-start | bytes 688136 | tf_op jit(solution)/shard_map/ppermute | solution.py:53
  46.2 7.7 %collective-permute-start.21 = (bf16[8,112,256]{2,1,0:T(8,128)(2,1)S(1)}, bf16[8,112,256]{2,1,0:T(8,128)(2,1)S(1)}, u32[]{:S(2)}, u32[]{:S(2)}) collective-permute-start(bf16[8,112,256]{2,1,0:T(8,128)(2,1)S(1)} %pad_maximum_fusion.2), channel_id=1, source_target_pairs={{0,12},{1,5},{2,14},{3,7},{4,8},{5,1},{6,10},{7,3},{8,4},{9,13},{1... | collective-permute-start | bytes 1376264 | tf_op jit(solution)/shard_map/ppermute | solution.py:53
  47.0 9.4 %collective-permute-start.14 = (bf16[8,112,256]{2,1,0:T(8,128)(2,1)S(1)}, bf16[8,112,256]{2,1,0:T(8,128)(2,1)S(1)}, u32[]{:S(2)}, u32[]{:S(2)}) collective-permute-start(bf16[8,112,256]{2,1,0:T(8,128)(2,1)S(1)} %pad_maximum_fusion.1), channel_id=1, source_target_pairs={{0,66},{1,65},{2,64},{3,67},{4,70},{5,69},{6,68},{7,71},{8,74},{9,... | collective-permute-start | bytes 1376264 | tf_op jit(solution)/shard_map/ppermute | solution.py:53
  54.0 33.4 %copy-start.8 = (bf16[16,112,256]{2,1,0:T(8,128)(2,1)}, bf16[16,112,256]{2,1,0:T(8,128)(2,1)S(1)}, u32[]{:S(2)}) copy-start(bf16[16,112,256]{2,1,0:T(8,128)(2,1)S(1)} %constant_dynamic-update-slice_fusion.10.refs_0_) | copy-start | bytes 2752516
  54.0 14.4 %collective-permute-start.22 = (bf16[16,112,256]{2,1,0:T(8,128)(2,1)S(1)}, bf16[16,112,256]{2,1,0:T(8,128)(2,1)}, u32[]{:S(2)}, u32[]{:S(2)}) collective-permute-start(bf16[16,112,256]{2,1,0:T(8,128)(2,1)S(1)} %constant_dynamic-update-slice_fusion.10.refs_0_), channel_id=1, source_target_pairs={{0,66},{1,65},{2,64},{3,67},{4,70},{5,69},{6,68},{7,71},{8,74},{9,... | collective-permute-start | bytes 2752520 | tf_op jit(solution)/shard_map/ppermute | solution.py:53
  54.2 8.2 %collective-permute-start.7 = (bf16[8,112,256]{2,1,0:T(8,128)(2,1)S(1)}, bf16[8,112,256]{2,1,0:T(8,128)(2,1)S(1)}, u32[]{:S(2)}, u32[]{:S(2)}) collective-permute-start(bf16[8,112,256]{2,1,0:T(8,128)(2,1)S(1)} %pad_maximum_fusion), channel_id=1, source_target_pairs={{0,48},{1,17},{2,50},{3,19},{4,52},{5,21},{6,54},{7,23},{8,56},{9,... | collective-permute-start | bytes 1376264 | tf_op jit(solution)/shard_map/ppermute | solution.py:53
  55.0 18.1 %collective-permute-start.23 = (bf16[16,112,256]{2,1,0:T(8,128)(2,1)S(1)}, bf16[16,112,256]{2,1,0:T(8,128)(2,1)S(1)}, u32[]{:S(2)}, u32[]{:S(2)}) collective-permute-start(bf16[16,112,256]{2,1,0:T(8,128)(2,1)S(1)} %constant_dynamic-update-slice_fusion.10.refs_0_), channel_id=1, source_target_pairs={{0,48},{1,17},{2,50},{3,19},{4,52},{5,21},{6,54},{7,23},{8,56},{9,... | collective-permute-start | bytes 2752520 | tf_op jit(solution)/shard_map/ppermute | solution.py:53
  57.2 27.8 %collective-permute-start.15 = (bf16[16,112,256]{2,1,0:T(8,128)(2,1)}, bf16[16,112,256]{2,1,0:T(8,128)(2,1)}, u32[]{:S(2)}, u32[]{:S(2)}) collective-permute-start(bf16[16,112,256]{2,1,0:T(8,128)(2,1)} %constant_dynamic-update-slice_fusion.5.refs_0_), channel_id=1, source_target_pairs={{0,48},{1,17},{2,50},{3,19},{4,52},{5,21},{6,54},{7,23},{8,56},{9,... | collective-permute-start | bytes 2752520 | tf_op jit(solution)/shard_map/ppermute | solution.py:53
  62.4 25.0 %collective-permute-start.8 = (bf16[16,112,256]{2,1,0:T(8,128)(2,1)S(1)}, bf16[16,112,256]{2,1,0:T(8,128)(2,1)}, u32[]{:S(2)}, u32[]{:S(2)}) collective-permute-start(bf16[16,112,256]{2,1,0:T(8,128)(2,1)S(1)} %constant_dynamic-update-slice_fusion.refs_0_), channel_id=1, source_target_pairs={{0,4},{1,13},{2,6},{3,15},{4,0},{5,9},{6,2},{7,11},{8,12},{9,5},{1... | collective-permute-start | bytes 2752520 | tf_op jit(solution)/shard_map/ppermute | solution.py:53
  68.4 34.5 %collective-permute-start.24 = (bf16[16,112,256]{2,1,0:T(8,128)(2,1)}, bf16[16,112,256]{2,1,0:T(8,128)(2,1)}, u32[]{:S(2)}, u32[]{:S(2)}) collective-permute-start(bf16[16,112,256]{2,1,0:T(8,128)(2,1)} %collective-permute-done.22.refs_1_), channel_id=1, source_target_pairs={{0,48},{1,17},{2,50},{3,19},{4,52},{5,21},{6,54},{7,23},{8,56},{9,... | collective-permute-start | bytes 2752520 | tf_op jit(solution)/shard_map/ppermute | solution.py:53
  73.1 0.9 copy-start.10
  74.0 39.3 %collective-permute-start.16 = (bf16[16,112,256]{2,1,0:T(8,128)(2,1)}, bf16[16,112,256]{2,1,0:T(8,128)(2,1)}, u32[]{:S(2)}, u32[]{:S(2)}) collective-permute-start(bf16[16,112,256]{2,1,0:T(8,128)(2,1)} %constant_dynamic-update-slice_fusion.5.refs_0_), channel_id=1, source_target_pairs={{0,4},{1,13},{2,6},{3,15},{4,0},{5,9},{6,2},{7,11},{8,12},{9,5},{1... | collective-permute-start | bytes 2752520 | tf_op jit(solution)/shard_map/ppermute | solution.py:53
  85.0 28.3 %collective-permute-start.17 = (bf16[16,112,256]{2,1,0:T(8,128)(2,1)}, bf16[16,112,256]{2,1,0:T(8,128)(2,1)}, u32[]{:S(2)}, u32[]{:S(2)}) collective-permute-start(bf16[16,112,256]{2,1,0:T(8,128)(2,1)} %collective-permute-done.15.refs_1_), channel_id=1, source_target_pairs={{0,4},{1,13},{2,6},{3,15},{4,0},{5,9},{6,2},{7,11},{8,12},{9,5},{1... | collective-permute-start | bytes 2752520 | tf_op jit(solution)/shard_map/ppermute | solution.py:53
  87.4 35.9 %collective-permute-start.9 = (bf16[16,112,256]{2,1,0:T(8,128)(2,1)S(1)}, bf16[16,112,256]{2,1,0:T(8,128)(2,1)}, u32[]{:S(2)}, u32[]{:S(2)}) collective-permute-start(bf16[16,112,256]{2,1,0:T(8,128)(2,1)S(1)} %constant_dynamic-update-slice_fusion.refs_0_), channel_id=1, source_target_pairs={{0,64},{1,67},{2,66},{3,65},{4,68},{5,71},{6,70},{7,69},{8,72},{9,... | collective-permute-start | bytes 2752520 | tf_op jit(solution)/shard_map/ppermute | solution.py:53
  87.5 35.9 %collective-permute-start.10 = (bf16[16,112,256]{2,1,0:T(8,128)(2,1)}, bf16[16,112,256]{2,1,0:T(8,128)(2,1)}, u32[]{:S(2)}, u32[]{:S(2)}) collective-permute-start(bf16[16,112,256]{2,1,0:T(8,128)(2,1)} %collective-permute-done.8.refs_1_), channel_id=1, source_target_pairs={{0,64},{1,67},{2,66},{3,65},{4,68},{5,71},{6,70},{7,69},{8,72},{9,... | collective-permute-start | bytes 2752520 | tf_op jit(solution)/shard_map/ppermute | solution.py:53
  95.1 1.5 copy-start.6
  96.6 6.9 %copy-start.9 = (bf16[16,112,256]{2,1,0:T(8,128)(2,1)S(1)}, bf16[16,112,256]{2,1,0:T(8,128)(2,1)}, u32[]{:S(2)}) copy-start(bf16[16,112,256]{2,1,0:T(8,128)(2,1)} %copy-done.8) | copy-start | bytes 2752516
  96.6 6.9 %copy-start.11 = (bf16[16,112,256]{2,1,0:T(8,128)(2,1)S(1)}, bf16[16,112,256]{2,1,0:T(8,128)(2,1)}, u32[]{:S(2)}) copy-start(bf16[16,112,256]{2,1,0:T(8,128)(2,1)} %copy-done.10) | copy-start | bytes 2752516
  102.9 44.2 %collective-permute-start = (f32[56,3584]{1,0:T(8,128)S(1)}, f32[56,3584]{1,0:T(8,128)S(1)}, u32[]{:S(2)}, u32[]{:S(2)}) collective-permute-start(f32[56,3584]{1,0:T(8,128)S(1)} %get-tuple-element.26.diff_ref), channel_id=1, source_target_pairs={{0,64},{64,0},{1,65},{65,1},{2,66},{66,2},{3,67},{67,3},{4,68},{68... | collective-permute-start | bytes 2408456 | tf_op jit(solution)/shard_map/ppermute | solution.py:329
  123.3 14.1 %copy-start.1 = (f32[1,3,56,3584]{3,2,1,0:T(8,128)S(1)}, f32[1,3,56,3584]{3,2,1,0:T(8,128)}, u32[]{:S(2)}) copy-start(f32[1,3,56,3584]{3,2,1,0:T(8,128)} %p_ref.1) | copy-start | bytes 7225348
  123.3 14.1 %copy-start.5 = (f32[1,3,56,3584]{3,2,1,0:T(8,128)S(1)}, f32[1,3,56,3584]{3,2,1,0:T(8,128)}, u32[]{:S(2)}) copy-start(f32[1,3,56,3584]{3,2,1,0:T(8,128)} %m_ref.1) | copy-start | bytes 7225348
  123.3 14.1 %copy-start.7 = (bf16[1,3,56,3584]{3,2,1,0:T(8,128)(2,1)S(1)}, bf16[1,3,56,3584]{3,2,1,0:T(8,128)(2,1)}, u32[]{:S(2)}) copy-start(bf16[1,3,56,3584]{3,2,1,0:T(8,128)(2,1)} %g_ref.1) | copy-start | bytes 3612676
  123.4 14.1 %copy-start.13 = (s32[3]{0:T(128)S(1)}, s32[3]{0:T(128)}, u32[]{:S(2)}) copy-start(s32[3]{0:T(128)} %plan_ref.5) | copy-start | bytes 40
  134.2 14.8 %collective-permute-start.27 = (bf16[512,512]{1,0:T(8,128)(2,1)S(1)}, bf16[512,512]{1,0:T(8,128)(2,1)S(1)}, u32[]{:S(2)}, u32[]{:S(2)}) collective-permute-start(bf16[512,512]{1,0:T(8,128)(2,1)S(1)} %get-tuple-element.45), channel_id=1, source_target_pairs={{0,1},{1,0},{2,3},{3,2},{4,5},{5,4},{6,7},{7,6},{8,9},{9,8},{10,11... | collective-permute-start | bytes 1572872 | tf_op jit(solution)/shard_map/ppermute | solution.py:63
  136.8 12.2 %collective-permute-start.26 = (bf16[512,512]{1,0:T(8,128)(2,1)S(1)}, bf16[512,512]{1,0:T(8,128)(2,1)S(1)}, u32[]{:S(2)}, u32[]{:S(2)}) collective-permute-start(bf16[512,512]{1,0:T(8,128)(2,1)S(1)} %get-tuple-element.44), channel_id=1, source_target_pairs={{0,1},{1,0},{2,3},{3,2},{4,5},{5,4},{6,7},{7,6},{8,9},{9,8},{10,11... | collective-permute-start | bytes 1572872 | tf_op jit(solution)/shard_map/ppermute | solution.py:63
  136.9 12.1 %collective-permute-start.25 = (bf16[512,512]{1,0:T(8,128)(2,1)S(1)}, bf16[512,512]{1,0:T(8,128)(2,1)S(1)}, u32[]{:S(2)}, u32[]{:S(2)}) collective-permute-start(bf16[512,512]{1,0:T(8,128)(2,1)S(1)} %get-tuple-element.43), channel_id=1, source_target_pairs={{0,1},{1,0},{2,3},{3,2},{4,5},{5,4},{6,7},{7,6},{8,9},{9,8},{10,11... | collective-permute-start | bytes 1572872 | tf_op jit(solution)/shard_map/ppermute | solution.py:63
  137.3 11.7 %collective-permute-start.28 = (bf16[512,256]{1,0:T(8,128)(2,1)S(1)}, bf16[512,256]{1,0:T(8,128)(2,1)S(1)}, u32[]{:S(2)}, u32[]{:S(2)}) collective-permute-start(bf16[512,256]{1,0:T(8,128)(2,1)S(1)} %get-tuple-element.46), channel_id=1, source_target_pairs={{0,1},{1,0},{2,3},{3,2},{4,5},{5,4},{6,7},{7,6},{8,9},{9,8},{10,11... | collective-permute-start | bytes 786440 | tf_op jit(solution)/shard_map/ppermute | solution.py:63
Sparse Core Ops, SparseCore 0:
  22.9 72.0 all-gather.2

commit v2 on v0

v2 whole, which is shorter than its diff:
```python
import functools

import jax
import jax.numpy as jnp
import numpy as np
from jax import lax
from jax.experimental import pallas as pl
from jax.experimental.pallas import tpu as pltpu
from jax.sharding import Mesh
from jax.sharding import PartitionSpec as P

STEP = 40
LAYERS = 3
outer_rate = 0.7
outer_mu = 0.9
inner_rate = 0.01
decay_rate = 0.1
beta_one = 0.9
beta_two = 0.95
adam_eps = 1e-08

ROWS = 56
CHIP = 2 * ROWS
D = 3584
HALF = D // 2
PART = HALF // 2
TILE = 128
GROUPS = 3
SHARE = (48, 32, 32)
ROOM = max(SHARE)
TOK = 512

ALL = ("yl", "z", "x", "yh", "core")
CHIPS = ("z", "x", "yh")
FLIPS = (("x", 1), ("y", 1), ("z", 1), ("x", 3), ("y", 3), ("z", 3))


def order(group, core):
    s = (group + 3 * core) % 6
    return FLIPS[s:] + FLIPS[:s]


def flipped(i, flip):
    core, yh, x, z, yl = i % 2, i // 2 % 2, i // 4 % 4, i // 16 % 4, i // 64
    y = yh * 2 + yl
    axis, mask = flip
    x, y, z = (v ^ mask if name == axis else v for name, v in (("x", x), ("y", y), ("z", z)))
    return ((y % 2 * 4 + z) * 4 + x) * 4 + y // 2 * 2 + core


def exchange(value, group, step):
    flips = [order(group, core)[step] for core in (0, 1)]
    return lax.ppermute(value, ALL, [(i, flipped(i, flips[i % 2])) for i in range(128)])


def code_masks(group, core):
    shift = {"z": 4, "x": 2, "y": 0}
    bits = [mask << shift[axis] for axis, mask in order(group, core)]
    return [functools.reduce(lambda a, b: a ^ b, [bits[k] for k in range(6) if r >> k & 1], 0) for r in range(64)]


def swap_cores(value):
    return lax.ppermute(value, "core", [(0, 1), (1, 0)])


def chosen_of(frag_ref, plan_ref):
    current = lax.rem(frag_ref[0], LAYERS)
    return jnp.where(plan_ref[0] == current, 0, jnp.where(plan_ref[1] == current, 1, 2))


def lanes(start, size):
    return pl.ds(pl.multiple_of(start, 128), size)


def outer(anchor, momentum, summed):
    pseudo = summed * 0.5
    momentum_new = outer_mu * momentum + pseudo
    return anchor - outer_rate * (pseudo + outer_mu * momentum_new), momentum_new


def fetch(jobs, sem):
    copies = [
        pltpu.make_async_copy(src.at[(*index, slice(None), lanes(at, PART))], to, sem.at[i])
        for i, (src, index, at, to) in enumerate(jobs)
    ]
    for copy in copies:
        copy.start()
    for copy in copies:
        copy.wait()


OLD = outer_rate * outer_mu * outer_mu
NEW = outer_rate * (1.0 + outer_mu) * 0.5


def first_kernel(
    frag_ref, plan_ref, anchor_ref, momentum_ref, params_ref, same_ref, cross_ref, keep_ref, give_ref, rest_ref, held, sem
):
    island, core, layer = lax.axis_index("yl"), lax.axis_index("core"), chosen_of(frag_ref, plan_ref)
    jobs = []
    for part in (1 - island, island):
        for half in (core, 1 - core):
            at = half * HALF + part * PART
            jobs += [(anchor_ref, (), at, held.at[len(jobs)]), (params_ref, (0, layer), at, held.at[len(jobs) + 1])]
    for half in (core, 1 - core):
        jobs.append((momentum_ref, (), half * HALF + island * PART, held.at[len(jobs)]))
    fetch(jobs, sem)
    same_ref[...] = (held[0] - held[1]).astype(jnp.bfloat16)
    cross_ref[...] = (held[2] - held[3]).astype(jnp.bfloat16)
    for i, (out_ref, half) in enumerate(((keep_ref, core), (give_ref, 1 - core))):
        anchor = held[4 + 2 * i]
        diff = anchor - held[5 + 2 * i]
        out_ref[...] = anchor - OLD * held[8 + i] - NEW * diff
        rest_ref[:, lanes(half * PART, PART)] = diff.astype(jnp.bfloat16)


def join_kernel(keep_ref, got_ref, same_ref, cross_ref, after_ref, *refs):
    outs, rows_ref = refs[:-1], refs[-1]
    core = lax.axis_index("core")
    for at, base_ref, term_ref in ((core, keep_ref, same_ref), (1 - core, got_ref, cross_ref)):
        rows = pl.ds(pl.multiple_of(at * ROWS, 8), ROWS)
        rows_ref[rows, :] = base_ref[...] - NEW * term_ref[...].astype(jnp.float32)
    done = 0
    for q, out_ref in enumerate(outs):
        share = SHARE[q]
        if share < ROOM:
            out_ref[0, CHIP + share : CHIP + ROOM] = jnp.zeros((ROOM - share, TILE), jnp.bfloat16)
        for at, tile, start, size in (
            (0, q, 0, CHIP),
            (CHIP, 2 * GROUPS, done, share),
            (CHIP + ROOM, GROUPS + q, 0, CHIP),
        ):
            value = rows_ref[start : start + size, tile * TILE : (tile + 1) * TILE]
            out_ref[0, at : at + size] = value.astype(jnp.bfloat16)
        done += share


def layers_kernel(
    frag_ref, plan_ref, p_ref, g_ref, m_ref, v_ref, anchor_ref, momentum_ref, same_ref, cross_ref, rest_ref, *refs
):
    p_out, m_out, v_out, momentum_out, done_ref = refs[-5:]
    chosen = pl.program_id(0) == LAYERS - 1

    @pl.when(jnp.logical_not(chosen))
    def _():
        grad = g_ref[...].astype(jnp.float32)
        first = beta_one * m_ref[...] + (1.0 - beta_one) * grad
        second = beta_two * v_ref[...] + (1.0 - beta_two) * grad * grad
        first_hat = first * (1.0 / (1.0 - beta_one**STEP))
        second_hat = second * (1.0 / (1.0 - beta_two**STEP))
        p_out[...] = p_ref[...] * (1.0 - inner_rate * decay_rate) - inner_rate * first_hat / (
            jnp.sqrt(second_hat) + adam_eps
        )
        m_out[...] = first
        v_out[...] = second

    @pl.when(chosen)
    def _():
        core, island = lax.axis_index("core"), lax.axis_index("yl")
        for half in (0, 1):
            for part in (0, 1):
                at = half * HALF + part * PART
                cols = slice(at, at + PART)
                got = jnp.where(
                    half == core, same_ref[...].astype(jnp.float32), cross_ref[...].astype(jnp.float32)
                )
                rest = rest_ref[:, half * PART : (half + 1) * PART].astype(jnp.float32)
                anchor = anchor_ref[:, cols]
                summed = (anchor - p_ref[0, 0, :, cols]).astype(jnp.bfloat16).astype(jnp.float32) + jnp.where(
                    part == island, got, rest
                )
                new, momentum_new = outer(anchor, momentum_ref[:, cols], summed)
                p_out[0, 0, :, cols] = new
                momentum_out[:, cols] = momentum_new
        m_out[...] = m_ref[...]
        v_out[...] = v_ref[...]

    done_ref[...] = jnp.zeros_like(done_ref)


STEP_ROWS = 512


def result_columns(tiles, half):
    return [half * HALF + part * PART + tile * TILE for tile in tiles for part in (0, 1)]


def piece_of(pieces, r, tile, q, size):
    at = CHIP if tile == 2 * GROUPS else 0 if tile < GROUPS else CHIP + ROOM
    return pieces[r // 32].at[r % 32, pl.ds(at, size)]


def multiply_kernel(tiles, n_pieces, has_buffer, mine_ref, theirs_ref, *refs):
    pieces, refs = refs[:n_pieces], refs[n_pieces + 1 + has_buffer :]
    result_ref, out_ref, weight, staged, load_sem, out_sem, result_sem = refs
    core = lax.axis_index("core")
    here = lax.axis_index("z") * 16 + lax.axis_index("x") * 4 + lax.axis_index("yh") * 2 + lax.axis_index("yl")

    def load_weight(g):
        done = 0
        tile = tiles[g]
        for q in (tile % GROUPS,) if tile < 2 * GROUPS else range(GROUPS):
            size = CHIP if tile < 2 * GROUPS else SHARE[q]
            masks = [code_masks(q, c) for c in (0, 1)]
            own = pieces if n_pieces == 2 else pieces[2 * q : 2 * q + 2]
            for r in range(64):
                code = here ^ jnp.where(core == 0, masks[0][r], masks[1][r])
                pltpu.make_async_copy(
                    piece_of(own, r, tile, q, size),
                    weight.at[g, code // 2, pl.ds(done, size), lanes(code % 2 * TILE, TILE)],
                    load_sem.at[g],
                ).start()
            done += SHARE[q]

    for g in range(len(tiles)):
        load_weight(g)
    columns = result_columns(tiles, core)
    for g in range(len(tiles)):
        pltpu.make_async_copy(weight.at[g], weight.at[g], load_sem.at[g]).wait()
        for i, rows_ref in enumerate((theirs_ref, mine_ref)):
            for at in range(0, TOK, STEP_ROWS):
                staged[i, at : at + STEP_ROWS, 2 * TILE * g : 2 * TILE * (g + 1)] = jnp.dot(
                    rows_ref[at : at + STEP_ROWS], weight[g].reshape(D, 2 * TILE), preferred_element_type=jnp.float32
                ).astype(jnp.bfloat16)
        cols = slice(2 * TILE * g, 2 * TILE * (g + 1))
        pltpu.make_async_copy(staged.at[0, :, cols], out_ref.at[:, cols], out_sem).start()
        for k in (2 * g, 2 * g + 1):
            pltpu.make_async_copy(
                staged.at[1, :, k * TILE : (k + 1) * TILE], result_ref.at[:, lanes(columns[k], TILE)], result_sem
            ).start()
    pltpu.make_async_copy(staged.at[0], staged.at[0], out_sem).wait()
    pltpu.make_async_copy(staged.at[1], staged.at[1], result_sem).wait()


TILES = ((0, 3), (2, 5), (1, 4, 6))


def place_kernel(buffer_ref, *refs):
    received, result_ref, sem = refs[:-2], refs[-2], refs[-1]
    half = 1 - lax.axis_index("core")
    copies = []
    for got, tiles in zip(received, TILES):
        for i, at in enumerate(result_columns(tiles, half)):
            copies.append(
                pltpu.make_async_copy(
                    got.at[:, i * TILE : (i + 1) * TILE], result_ref.at[:, lanes(at, TILE)], sem.at[len(copies)]
                )
            )
    for copy in copies:
        copy.start()
    for copy in copies:
        copy.wait()


ANY = pl.BlockSpec(memory_space=pl.ANY)
VMEM = pl.BlockSpec(memory_space=pltpu.VMEM)
SMEM = pl.BlockSpec(memory_space=pltpu.SMEM)
LIMIT = pltpu.CompilerParams(vmem_limit_bytes=24 * 2**20)
FULL = pltpu.CompilerParams(vmem_limit_bytes=60 * 2**20)
SMALL = pltpu.CompilerParams(vmem_limit_bytes=16 * 2**20)


def shape(dims, dtype):
    return jax.ShapeDtypeStruct(dims, dtype)


def cost(flops, moved):
    return pl.CostEstimate(flops=flops, bytes_accessed=moved, transcendentals=0)


def layers_call(scalars, inner, flat, parts, rest, after):
    def layer(i, frag_ref, plan_ref):
        return (0, lax.rem(chosen_of(frag_ref, plan_ref) + 1 + i, LAYERS), 0, 0)

    def whole(dims):
        return pl.BlockSpec(dims, lambda i, *_: (0, 0))

    stepped = pl.BlockSpec((1, 1, ROWS, D), layer)
    state = shape((1, LAYERS, ROWS, D), jnp.float32)
    return pl.pallas_call(
        layers_kernel,
        grid_spec=pltpu.PrefetchScalarGridSpec(
            num_scalar_prefetch=2,
            grid=(LAYERS,),
            in_specs=[stepped] * 4 + [whole((ROWS, D))] * 2 + [whole((ROWS, PART))] * 2 + [whole((ROWS, 2 * PART))] + [ANY] * len(after),
            out_specs=[stepped] * 3 + [whole((ROWS, D)), whole((8, 128))],
        ),
        out_shape=[state] * 3 + [shape((ROWS, D), jnp.float32), shape((8, 128), jnp.int32)],
        compiler_params=LIMIT,
        cost_estimate=cost(20 * LAYERS * ROWS * D, 30 * LAYERS * ROWS * D),
    )(*scalars, *inner, *flat, *parts, rest, *after)


def multiply_call(tiles, tokens, others, pieces, after, buffer):
    width = 2 * TILE * len(tiles)
    args = [tokens, others, *pieces, after] + ([] if buffer is None else [buffer])
    return pl.pallas_call(
        functools.partial(multiply_kernel, tiles, len(pieces), buffer is not None),
        in_specs=[VMEM] * 2 + [ANY] * (len(args) - 2),
        out_specs=[ANY, ANY],
        out_shape=[shape((TOK, D), jnp.bfloat16), shape((TOK, width), jnp.bfloat16)],
        scratch_shapes=[
            pltpu.VMEM((len(tiles), D // CHIP, CHIP, 2 * TILE), jnp.bfloat16),
            pltpu.VMEM((2, TOK, width), jnp.bfloat16),
            pltpu.SemaphoreType.DMA((len(tiles),)),
            pltpu.SemaphoreType.DMA,
            pltpu.SemaphoreType.DMA,
        ],
        input_output_aliases={} if buffer is None else {len(args) - 1: 0},
        compiler_params=LIMIT,
        cost_estimate=cost(2 * 2 * TOK * D * width, 4 * TOK * D + 2 * D * width),
    )(*args)


def body(inner_params, inner_grads, adam_first, adam_second, anchor, momentum, tokens, frag_index, plan):
    f32, bf16 = jnp.float32, jnp.bfloat16
    scalars = (frag_index, plan)
    others = swap_cores(tokens)

    send_same, send_cross, keep, give, rest = pl.pallas_call(
        first_kernel,
        in_specs=[SMEM] * 2 + [ANY] * 3,
        out_specs=[VMEM] * 5,
        out_shape=[shape((ROWS, PART), bf16)] * 2 + [shape((ROWS, PART), f32)] * 2 + [shape((ROWS, 2 * PART), bf16)],
        scratch_shapes=[pltpu.VMEM((10, ROWS, PART), f32), pltpu.SemaphoreType.DMA((10,))],
        compiler_params=FULL,
    )(*scalars, anchor, momentum, inner_params)
    same = lax.ppermute(send_same, "yl", [(0, 1), (1, 0)])
    cross = lax.ppermute(send_cross, ("yl", "core"), [(i, 3 - i) for i in range(4)])
    got = swap_cores(give)
    cur = pl.pallas_call(
        join_kernel,
        in_specs=[VMEM] * 4 + [ANY],
        out_specs=[VMEM] * GROUPS,
        out_shape=[shape((1, 2 * CHIP + ROOM, TILE), bf16)] * GROUPS,
        scratch_shapes=[pltpu.VMEM((CHIP, PART), f32)],
        compiler_params=SMALL,
    )(keep, got, same, cross, others)
    rest_received = lax.ppermute(rest, "yl", [(0, 1), (1, 0)])

    late = rest_received[0, 0] != rest_received[0, 0]

    def doubled(value, step, before):
        out, arrivals = [], []
        for q in range(GROUPS):
            arrived = exchange(value[q], q, step)
            ahead = (arrivals[q - 1] if q else before)[0]
            waits = (ahead != ahead)[None]
            if step == 2 and q == 0:
                waits = waits | late
            out.append(jnp.concatenate([value[q], jnp.where(waits, value[q], arrived)], axis=0))
            arrivals.append(arrived)
        return out, arrivals[1], arrivals[-1]

    before = jnp.zeros((1, 2 * CHIP + ROOM, TILE), bf16)
    for step in range(4):
        cur, before, _ = doubled(cur, step, before)
    both, _, before = doubled(cur, 4, before)
    params_out, first_out, second_out, momentum_out, done = layers_call(
        (frag_index, plan), (inner_params, inner_grads, adam_first, adam_second), (anchor, momentum), (same, swap_cores(cross)),
        rest_received, (before,),
    )
    sixth = [exchange(both[q], q, 5) for q in range(GROUPS)]
    pieces = [[both[q], sixth[q]] for q in range(GROUPS)]
    swapped, result = [], None
    for tiles in TILES:
        needed = pieces[tiles[0]] if len(tiles) == 2 else sum(pieces, [])
        result, out = multiply_call(tiles, tokens, others, needed, done, result)
        swapped.append(swap_cores(out))
    projected = pl.pallas_call(
        place_kernel,
        in_specs=[ANY] + [VMEM] * GROUPS,
        out_specs=ANY,
        out_shape=shape((TOK, D), bf16),
        scratch_shapes=[pltpu.SemaphoreType.DMA((14,))],
        input_output_aliases={0: 0},
        compiler_params=pltpu.CompilerParams(vmem_limit_bytes=4 * 2**20),
    )(result, *swapped)
    return (params_out, first_out, second_out, momentum_out, projected)


def solution(mesh):
    torus = Mesh(np.asarray(mesh.devices).reshape(2, 4, 4, 2, 2), ALL)
    fsdp = ("z", "x", "yh", "core")
    state = P("yl", None, fsdp, None)
    rows = P(fsdp, None)
    tokens = P(ALL, None)
    return jax.shard_map(
        body,
        mesh=torus,
        in_specs=(state, state, state, state, rows, rows, tokens, P(), P()),
        out_specs=(state, state, state, rows, tokens),
        check_vma=False,
    )
```

time: 230 us -> 134 us (0.58)
  waiting for transfers between devices: 171 us -> 52.6 us
  starting transfers between devices: 0.08 us -> 41.3 us
  Pallas kernels: 0 us -> 30.8 us
  matrix products: 21 us -> 0 us
  between operations: 16.7 us -> 3.17 us
  other arithmetic: 15.6 us -> 3.1 us
  local copies, waits for them, and re-layouts: 5.92 us -> 1.74 us
    all_gather x1 -> x0, waiting for transfers between devices: 126 us -> none  [body(): lax.all_gather(weight_bf, 'fsdp', axis=0, tiled=True)]
    ppermute x0 -> x27, waiting for transfers between devices: none -> 52.6 us  [the longest x18 42.8 us: exchange(): lax.ppermute(value, ALL, [(i, flipped(i, flips[i % 2])) for i in range(12...]
    psum x1 -> x0, waiting for transfers between devices: 44.6 us -> none  [body(): summed = lax.psum(local_diff, 'island')]
    ppermute x0 -> x27, starting transfers between devices: none -> 41.3 us  [the longest x6 20.3 us: swap_cores(): return lax.ppermute(value, 'core', [(0, 1), (1, 0)])]
    pallas_call x0 -> x7, Pallas kernels: none -> 30.8 us  [the longest x3 21.2 us: multiply_call(): pl.pallas_call(functools.partial(multiply_kernel, tiles, len(pieces), buf...]
    dot_general x1 -> x0, matrix products: 21 us -> none  [body(): jnp.dot(tokens, lax.all_gather(weight_bf, 'fsdp', axis=0, tiled=True), pr...]
    select_n x1 -> x0, other arithmetic: 8.37 us -> none  [body(): second_out = jnp.where(is_frag, adam_second, second_new)]
    unnamed x5 -> x28, local copies, waits for them, and re-layouts: 5.92 us -> 1.23 us
  transfers between devices with their start and end apart: 2 -> 27, of which waited for: 2 -> 15; matrix products, arithmetic and copies ran while one was open for 4% -> 3% of each run, Pallas kernels for 0% -> 16%
where the time goes in v2:
time: 134 us; the launch traced here: 133 us
  waiting for transfers between devices  52.6 us (39%)
  starting transfers between devices  41.3 us (31%)
  Pallas kernels  30.8 us (23%)
  between operations  3.17 us (2%)
  other arithmetic  3.1 us (2%)
  local copies, waits for them, and re-layouts  1.74 us (1%)
    ppermute x18, waiting for transfers between devices, exchange(): lax.ppermute(value, ALL, [(i, flipped(i, flips[i % 2])) for i in range(12...  42.8 us
    pallas_call x3, Pallas kernels, multiply_call(): pl.pallas_call(functools.partial(multiply_kernel, tiles, len(pieces), buf...  21.2 us
    ppermute x6, starting transfers between devices, swap_cores(): return lax.ppermute(value, 'core', [(0, 1), (1, 0)])  20.3 us
    ppermute x18, starting transfers between devices, exchange(): lax.ppermute(value, ALL, [(i, flipped(i, flips[i % 2])) for i in range(12...  17.6 us
    pallas_call x1, Pallas kernels, layers_call(): pl.pallas_call(layers_kernel, grid_spec=pltpu.PrefetchScalarGridSpec(num_...  4.86 us
    ppermute x6, waiting for transfers between devices, swap_cores(): return lax.ppermute(value, 'core', [(0, 1), (1, 0)])  3.85 us
    pallas_call x1, Pallas kernels, body(): pl.pallas_call(first_kernel, in_specs=[SMEM] * 2 + [ANY] * 3, out_specs=[...  3.3 us
    ppermute x1, waiting for transfers between devices, body(): rest_received = lax.ppermute(rest, 'yl', [(0, 1), (1, 0)])  3.29 us
  transfers between devices with their start and end apart: 27, of which 15 were waited for; matrix products, arithmetic and copies ran while one was open for 3% of the time, Pallas kernels for 16%

profile of v2, /device:TPU:1, one launch (start us, length us, event | category | flops | bytes accessed | tf_op | source)
XLA Modules:
  0.0 132.6 jit_solution(3160803034479375050)
XLA Ops:
  0.6 1.5 %collective-permute-start.5 = (bf16[512,3584]{1,0:T(8,128)(2,1)}, bf16[512,3584]{1,0:T(8,128)(2,1)S(1)}, u32[]{:S(2)}, u32[]{:S(2)}) collective-permute-start(bf16[512,3584]{1,0:T(8,128)(2,1)} %mine_ref.5), channel_id=1, source_target_pairs={{0,1},{1,0},{2,3},{3,2},{4,5},{5,4},{6,7},{7,6},{8,9},{9,8},{10,11... | collective-permute-start | bytes 11010056 | tf_op jit(solution)/shard_map/ppermute | solution.py:63
  2.8 3.3 %shard_map.128 = (bf16[56,896]{1,0:T(8,128)(2,1)}, bf16[56,896]{1,0:T(8,128)(2,1)}, f32[56,896]{1,0:T(8,128)}, f32[56,896]{1,0:T(8,128)}, bf16[56,1792]{1,0:T(8,128)(2,1)}) custom-call(s32[1]{0:T(128)S(6)} %copy.48.frag_ref, s32[3]{0:T(128)} %plan_ref.3, f32[56,3584]{1,0:T(8,128)} %anchor_ref.3, f32[56,3584]{1,0:T(8,128)} %momentum_ref.3, ...), custom_call_target="tpu_custom_call" | custom-call | tf_op jit(solution)/shard_map/pallas_call | solution.py:320
  6.1 1.5 %collective-permute-start.3 = (bf16[56,1792]{1,0:T(8,128)(2,1)}, bf16[56,1792]{1,0:T(8,128)(2,1)S(1)}, u32[]{:S(2)}, u32[]{:S(2)}) collective-permute-start(bf16[56,1792]{1,0:T(8,128)(2,1)} %get-tuple-element.26), channel_id=1, source_target_pairs={{0,64},{64,0},{1,65},{65,1},{2,66},{66,2},{3,67},{67,3},{4,68},{68... | collective-permute-start | bytes 602120 | tf_op jit(solution)/shard_map/ppermute | solution.py:339
  7.6 0.3 collective-permute-start.4
  7.8 0.1 collective-permute-start
  7.9 1.8 %collective-permute-start.1 = (bf16[56,896]{1,0:T(8,128)(2,1)}, bf16[56,896]{1,0:T(8,128)(2,1)S(1)}, u32[]{:S(2)}, u32[]{:S(2)}) collective-permute-start(bf16[56,896]{1,0:T(8,128)(2,1)} %get-tuple-element.25), channel_id=1, source_target_pairs={{0,65},{1,64},{64,1},{65,0},{2,67},{3,66},{66,3},{67,2},{4,69},{5,... | collective-permute-start | bytes 301064 | tf_op jit(solution)/shard_map/ppermute | solution.py:329
  9.7 3.3 %collective-permute-done.3.rest_ref = bf16[56,1792]{1,0:T(8,128)(2,1)S(1)} collective-permute-done((bf16[56,1792]{1,0:T(8,128)(2,1)}, bf16[56,1792]{1,0:T(8,128)(2,1)S(1)}, u32[]{:S(2)}, u32[]{:S(2)}) %collective-permute-start.3) | collective-permute-done | bytes 200736 | tf_op jit(solution)/shard_map/ppermute | solution.py:339
  13.0 0.5 slice.45
  14.8 0.3 collective-permute-done.same_ref
  15.2 2.2 %collective-permute-done.1.cross_ref = bf16[56,896]{1,0:T(8,128)(2,1)S(1)} collective-permute-done((bf16[56,896]{1,0:T(8,128)(2,1)}, bf16[56,896]{1,0:T(8,128)(2,1)S(1)}, u32[]{:S(2)}, u32[]{:S(2)}) %collective-permute-start.1) | collective-permute-done | bytes 100384 | tf_op jit(solution)/shard_map/ppermute | solution.py:329
  17.4 0.9 copy-done.7
  18.3 0.1 shard_map.129
  18.4 2.6 %collective-permute-start.8 = (bf16[1,272,128]{2,1,0:T(8,128)(2,1)S(1)}, bf16[1,272,128]{2,1,0:T(8,128)(2,1)S(1)}, u32[]{:S(2)}, u32[]{:S(2)}) collective-permute-start(bf16[1,272,128]{2,1,0:T(8,128)(2,1)S(1)} %get-tuple-element.31), channel_id=1, source_target_pairs={{0,4},{1,13},{2,6},{3,15},{4,0},{5,9},{6,2},{7,11},{8,12},{9,5},{1... | collective-permute-start | bytes 208904 | tf_op jit(solution)/shard_map/ppermute | solution.py:53
  21.1 2.7 %collective-permute-start.6 = (bf16[1,272,128]{2,1,0:T(8,128)(2,1)S(1)}, bf16[1,272,128]{2,1,0:T(8,128)(2,1)S(1)}, u32[]{:S(2)}, u32[]{:S(2)}) collective-permute-start(bf16[1,272,128]{2,1,0:T(8,128)(2,1)S(1)} %get-tuple-element.30), channel_id=1, source_target_pairs={{0,64},{1,67},{2,66},{3,65},{4,68},{5,71},{6,70},{7,69},{8,72},{9,... | collective-permute-start | bytes 208904 | tf_op jit(solution)/shard_map/ppermute | solution.py:53
  23.8 3.8 %collective-permute-start.7 = (bf16[1,272,128]{2,1,0:T(8,128)(2,1)S(1)}, bf16[1,272,128]{2,1,0:T(8,128)(2,1)S(1)}, u32[]{:S(2)}, u32[]{:S(2)}) collective-permute-start(bf16[1,272,128]{2,1,0:T(8,128)(2,1)S(1)} %get-tuple-element.29), channel_id=1, source_target_pairs={{0,16},{1,49},{2,18},{3,51},{4,20},{5,53},{6,22},{7,55},{8,24},{9,... | collective-permute-start | bytes 208904 | tf_op jit(solution)/shard_map/ppermute | solution.py:53
  27.7 1.7 %collective-permute-done.7 = bf16[1,272,128]{2,1,0:T(8,128)(2,1)S(1)} collective-permute-done((bf16[1,272,128]{2,1,0:T(8,128)(2,1)S(1)}, bf16[1,272,128]{2,1,0:T(8,128)(2,1)S(1)}, u32[]{:S(2)}, u32[]{:S(2)}) %collective-permute-start.7) | collective-permute-done | bytes 69664 | tf_op jit(solution)/shard_map/ppermute | solution.py:53
  29.4 0.1 constant_dynamic-update-slice_fusion.12
  29.6 0.1 collective-permute-start.10
  29.6 2.8 %collective-permute-start.9 = (bf16[2,272,128]{2,1,0:T(8,128)(2,1)S(1)}, bf16[2,272,128]{2,1,0:T(8,128)(2,1)S(1)}, u32[]{:S(2)}, u32[]{:S(2)}) collective-permute-start(bf16[2,272,128]{2,1,0:T(8,128)(2,1)S(1)} %pad_maximum_fusion.6), channel_id=1, source_target_pairs={{0,16},{1,49},{2,18},{3,51},{4,20},{5,53},{6,22},{7,55},{8,24},{9,... | collective-permute-start | bytes 417800 | tf_op jit(solution)/shard_map/ppermute | solution.py:53
  32.5 5.0 %collective-permute-done.11 = bf16[2,272,128]{2,1,0:T(8,128)(2,1)S(1)} collective-permute-done((bf16[2,272,128]{2,1,0:T(8,128)(2,1)S(1)}, bf16[2,272,128]{2,1,0:T(8,128)(2,1)S(1)}, u32[]{:S(2)}, u32[]{:S(2)}) %collective-permute-start.11) | collective-permute-done | bytes 139296 | tf_op jit(solution)/shard_map/ppermute | solution.py:53
  37.6 0.1 constant_dynamic-update-slice_fusion.15
  37.8 0.1 constant_dynamic-update-slice_fusion.23
  37.9 0.1 collective-permute-start.13
  38.0 1.5 %collective-permute-start.12 = (bf16[4,272,128]{2,1,0:T(8,128)(2,1)S(1)}, bf16[4,272,128]{2,1,0:T(8,128)(2,1)S(1)}, u32[]{:S(2)}, u32[]{:S(2)}) collective-permute-start(bf16[4,272,128]{2,1,0:T(8,128)(2,1)S(1)} %pad_maximum_fusion.3), channel_id=1, source_target_pairs={{0,12},{1,5},{2,14},{3,7},{4,8},{5,1},{6,10},{7,3},{8,4},{9,13},{1... | collective-permute-start | bytes 835592 | tf_op jit(solution)/shard_map/ppermute | solution.py:53
  39.4 0.1 constant_dynamic-update-slice_fusion.7
  39.6 0.1 collective-permute-start.14
  39.7 4.1 %collective-permute-done.12 = bf16[4,272,128]{2,1,0:T(8,128)(2,1)S(1)} collective-permute-done((bf16[4,272,128]{2,1,0:T(8,128)(2,1)S(1)}, bf16[4,272,128]{2,1,0:T(8,128)(2,1)S(1)}, u32[]{:S(2)}, u32[]{:S(2)}) %collective-permute-start.12) | collective-permute-done | bytes 278560 | tf_op jit(solution)/shard_map/ppermute | solution.py:53
  43.8 0.1 constant_dynamic-update-slice_fusion.22
  43.9 0.1 pad_maximum_fusion.1
  44.0 0.1 collective-permute-start.16
  44.1 2.2 %collective-permute-done.14 = bf16[4,272,128]{2,1,0:T(8,128)(2,1)S(1)} collective-permute-done((bf16[4,272,128]{2,1,0:T(8,128)(2,1)S(1)}, bf16[4,272,128]{2,1,0:T(8,128)(2,1)S(1)}, u32[]{:S(2)}, u32[]{:S(2)}) %collective-permute-start.14) | collective-permute-done | bytes 278560 | tf_op jit(solution)/shard_map/ppermute | solution.py:53
  46.3 0.1 constant_dynamic-update-slice_fusion.6
  46.5 0.2 collective-permute-start.18
  46.7 0.1 constant_dynamic-update-slice_fusion.14
  46.9 1.5 %collective-permute-start.15 = (bf16[8,272,128]{2,1,0:T(8,128)(2,1)S(1)}, bf16[8,272,128]{2,1,0:T(8,128)(2,1)S(1)}, u32[]{:S(2)}, u32[]{:S(2)}) collective-permute-start(bf16[8,272,128]{2,1,0:T(8,128)(2,1)S(1)} %pad_maximum_fusion), channel_id=1, source_target_pairs={{0,66},{1,65},{2,64},{3,67},{4,70},{5,69},{6,68},{7,71},{8,74},{9,... | collective-permute-start | bytes 1671176 | tf_op jit(solution)/shard_map/ppermute | solution.py:53
  48.5 6.8 %collective-permute-done.18 = bf16[8,272,128]{2,1,0:T(8,128)(2,1)S(1)} collective-permute-done((bf16[8,272,128]{2,1,0:T(8,128)(2,1)S(1)}, bf16[8,272,128]{2,1,0:T(8,128)(2,1)S(1)}, u32[]{:S(2)}, u32[]{:S(2)}) %collective-permute-start.18) | collective-permute-done | bytes 557088 | tf_op jit(solution)/shard_map/ppermute | solution.py:53
  55.2 0.3 fusion.3
  55.5 1.5 %collective-permute-start.19 = (bf16[16,272,128]{2,1,0:T(8,128)(2,1)S(1)}, bf16[16,272,128]{2,1,0:T(8,128)(2,1)S(1)}, u32[]{:S(2)}, u32[]{:S(2)}) collective-permute-start(bf16[16,272,128]{2,1,0:T(8,128)(2,1)S(1)} %get-tuple-element.63), channel_id=1, source_target_pairs={{0,66},{1,65},{2,64},{3,67},{4,70},{5,69},{6,68},{7,71},{8,74},{9,... | collective-permute-start | bytes 3342344 | tf_op jit(solution)/shard_map/ppermute | solution.py:53
  57.0 0.3 fusion.5
  57.2 0.1 collective-permute-start.21
  57.4 0.3 fusion
  57.6 0.3 collective-permute-start.17
  57.9 12.3 %collective-permute-done.19 = bf16[16,272,128]{2,1,0:T(8,128)(2,1)S(1)} collective-permute-done((bf16[16,272,128]{2,1,0:T(8,128)(2,1)S(1)}, bf16[16,272,128]{2,1,0:T(8,128)(2,1)S(1)}, u32[]{:S(2)}, u32[]{:S(2)}) %collective-permute-start.19) | collective-permute-done | bytes 1114144 | tf_op jit(solution)/shard_map/ppermute | solution.py:53
  70.2 0.4 select_dynamic-update-slice_fusion.2.refs_0_
  70.6 0.1 collective-permute-start.20
  70.7 1.3 collective-permute-done.21
  72.0 1.6 %collective-permute-done.17.refs_0_ = bf16[16,272,128]{2,1,0:T(8,128)(2,1)S(1)} collective-permute-done((bf16[16,272,128]{2,1,0:T(8,128)(2,1)S(1)}, bf16[16,272,128]{2,1,0:T(8,128)(2,1)S(1)}, u32[]{:S(2)}, u32[]{:S(2)}) %collective-permute-start.17) | collective-permute-done | bytes 1114144 | tf_op jit(solution)/shard_map/ppermute | solution.py:53
  73.6 0.4 select_dynamic-update-slice_fusion.refs_0_.refs_4_
  73.9 0.1 collective-permute-start.23
  74.1 0.4 select_dynamic-update-slice_fusion.1.refs_2_
  74.5 0.3 collective-permute-start.22
  74.7 8.8 %collective-permute-start.2 = (bf16[56,896]{1,0:T(8,128)(2,1)S(1)}, bf16[56,896]{1,0:T(8,128)(2,1)S(1)}, u32[]{:S(2)}, u32[]{:S(2)}) collective-permute-start(bf16[56,896]{1,0:T(8,128)(2,1)S(1)} %collective-permute-done.1.cross_ref), channel_id=1, source_target_pairs={{0,1},{1,0},{2,3},{3,2},{4,5},{5,4},{6,7},{7,6},{8,9},{9,8},{10,11... | collective-permute-start | bytes 301064 | tf_op jit(solution)/shard_map/ppermute | solution.py:63
  83.5 0.9 collective-permute-done.2.cross_ref
  84.5 4.9 %shard_map.130 = (f32[1,3,56,3584]{3,2,1,0:T(8,128)}, f32[1,3,56,3584]{3,2,1,0:T(8,128)}, f32[1,3,56,3584]{3,2,1,0:T(8,128)}, f32[56,3584]{1,0:T(8,128)}, s32[8,128]{1,0:T(8,128)S(1)}) custom-call(s32[1]{0:T(128)S(6)} %copy.48.frag_ref, s32[3]{0:T(128)S(1)} %copy-done.8, f32[1,3,56,3584]{3,2,1,0:T(8,128)S(1)} %copy-done.1, ...), custom_call_target="tpu_custom_call" | custom-call | flops 12042240 | bytes 18063360 | tf_op jit(solution)/shard_map/pallas_call | solution.py:280
  89.4 7.9 %collective-permute-done.20.refs_1_ = bf16[32,272,128]{2,1,0:T(8,128)(2,1)S(1)} collective-permute-done((bf16[32,272,128]{2,1,0:T(8,128)(2,1)S(1)}, bf16[32,272,128]{2,1,0:T(8,128)(2,1)S(1)}, u32[]{:S(2)}, u32[]{:S(2)}) %collective-permute-start.20) | collective-permute-done | bytes 2228256 | tf_op jit(solution)/shard_map/ppermute | solution.py:53
  97.2 6.2 %shard_map.131 = (bf16[512,3584]{1,0:T(8,128)(2,1)}, bf16[512,512]{1,0:T(8,128)(2,1)S(1)}) custom-call(bf16[512,3584]{1,0:T(8,128)(2,1)S(1)} %copy-done, bf16[512,3584]{1,0:T(8,128)(2,1)S(1)} %collective-permute-done.5.after_ref.theirs_ref, bf16[32,272,128]{2,1,0:T(8,128)(2,1)S(1)} %select_dynamic-update-slice_fusion.2.refs_0_, ...), custom_call_target="tpu_custom_call" | custom-call | flops 3758096384 | bytes 11010048 | tf_op jit(solution)/shard_map/pallas_call | solution.py:297
  103.5 6.2 %shard_map.132 = (bf16[512,3584]{1,0:T(8,128)(2,1)}, bf16[512,512]{1,0:T(8,128)(2,1)S(1)}) custom-call(bf16[512,3584]{1,0:T(8,128)(2,1)S(1)} %copy-done, bf16[512,3584]{1,0:T(8,128)(2,1)S(1)} %collective-permute-done.5.after_ref.theirs_ref, ...), custom_call_target="tpu_custom_call", output_to_operand_aliasing={{0}: (5, {})} | custom-call | flops 3758096384 | bytes 11010048 | tf_op jit(solution)/shard_map/pallas_call | solution.py:297
  109.7 8.8 %shard_map.133 = (bf16[512,3584]{1,0:T(8,128)(2,1)}, bf16[512,768]{1,0:T(8,128)(2,1)S(1)}) custom-call(bf16[512,3584]{1,0:T(8,128)(2,1)S(1)} %copy-done, bf16[512,3584]{1,0:T(8,128)(2,1)S(1)} %collective-permute-done.5.after_ref.theirs_ref, bf16[32,272,128]{2,1,0:T(8,128)(2,1)S(1)} %select_dynamic-update-slice_fusion.2.refs_0_, ...), custom_call_target="tpu_custom_call", output_to_operand_aliasing={{0}: (9, {})} | custom-call | flops 5637144576 | bytes 12845056 | tf_op jit(solution)/shard_map/pallas_call | solution.py:297
  118.5 9.2 %collective-permute-start.26 = (bf16[512,768]{1,0:T(8,128)(2,1)S(1)}, bf16[512,768]{1,0:T(8,128)(2,1)S(1)}, u32[]{:S(2)}, u32[]{:S(2)}) collective-permute-start(bf16[512,768]{1,0:T(8,128)(2,1)S(1)} %get-tuple-element.42), channel_id=1, source_target_pairs={{0,1},{1,0},{2,3},{3,2},{4,5},{5,4},{6,7},{7,6},{8,9},{9,8},{10,11... | collective-permute-start | bytes 2359304 | tf_op jit(solution)/shard_map/ppermute | solution.py:63
  127.7 0.1 collective-permute-start.25
  127.8 0.4 collective-permute-start.24
  128.2 2.2 %collective-permute-done.25.refs_1_ = bf16[512,512]{1,0:T(8,128)(2,1)S(1)} collective-permute-done((bf16[512,512]{1,0:T(8,128)(2,1)S(1)}, bf16[512,512]{1,0:T(8,128)(2,1)S(1)}, u32[]{:S(2)}, u32[]{:S(2)}) %collective-permute-start.25) | collective-permute-done | bytes 524320 | tf_op jit(solution)/shard_map/ppermute | solution.py:63
  130.4 0.7 collective-permute-done.24.refs_0_
  131.1 1.3 %shard_map.134 = bf16[512,3584]{1,0:T(8,128)(2,1)} custom-call(bf16[512,3584]{1,0:T(8,128)(2,1)} %get-tuple-element.39.buffer_ref, bf16[512,512]{1,0:T(8,128)(2,1)S(1)} %collective-permute-done.24.refs_0_, bf16[512,512]{1,0:T(8,128)(2,1)S(1)} %collective-permute-done.25.refs_1_, ...), custom_call_target="tpu_custom_call", output_to_operand_aliasing={{}: (0, {})} | custom-call | tf_op jit(solution)/shard_map/pallas_call | solution.py:370
  (56 shorter events, 0.8 us)
Async XLA Ops:
  0.6 16.8 %collective-permute-start.5 = (bf16[512,3584]{1,0:T(8,128)(2,1)}, bf16[512,3584]{1,0:T(8,128)(2,1)S(1)}, u32[]{:S(2)}, u32[]{:S(2)}) collective-permute-start(bf16[512,3584]{1,0:T(8,128)(2,1)} %mine_ref.5), channel_id=1, source_target_pairs={{0,1},{1,0},{2,3},{3,2},{4,5},{5,4},{6,7},{7,6},{8,9},{9,8},{10,11... | collective-permute-start | bytes 11010056 | tf_op jit(solution)/shard_map/ppermute | solution.py:63
  6.1 6.9 %collective-permute-start.3 = (bf16[56,1792]{1,0:T(8,128)(2,1)}, bf16[56,1792]{1,0:T(8,128)(2,1)S(1)}, u32[]{:S(2)}, u32[]{:S(2)}) collective-permute-start(bf16[56,1792]{1,0:T(8,128)(2,1)} %get-tuple-element.26), channel_id=1, source_target_pairs={{0,64},{64,0},{1,65},{65,1},{2,66},{66,2},{3,67},{67,3},{4,68},{68... | collective-permute-start | bytes 602120 | tf_op jit(solution)/shard_map/ppermute | solution.py:339
  7.6 9.8 %collective-permute-start.4 = (f32[56,896]{1,0:T(8,128)}, f32[56,896]{1,0:T(8,128)S(1)}, u32[]{:S(2)}, u32[]{:S(2)}) collective-permute-start(f32[56,896]{1,0:T(8,128)} %get-tuple-element.28), channel_id=1, source_target_pairs={{0,1},{1,0},{2,3},{3,2},{4,5},{5,4},{6,7},{7,6},{8,9},{9,8},{10,11... | collective-permute-start | bytes 602120 | tf_op jit(solution)/shard_map/ppermute | solution.py:63
  7.8 7.3 %collective-permute-start = (bf16[56,896]{1,0:T(8,128)(2,1)}, bf16[56,896]{1,0:T(8,128)(2,1)S(1)}, u32[]{:S(2)}, u32[]{:S(2)}) collective-permute-start(bf16[56,896]{1,0:T(8,128)(2,1)} %get-tuple-element.24), channel_id=1, source_target_pairs={{0,64},{64,0},{1,65},{65,1},{2,66},{66,2},{3,67},{67,3},{4,68},{68... | collective-permute-start | bytes 301064 | tf_op jit(solution)/shard_map/ppermute | solution.py:328
  7.9 9.5 %collective-permute-start.1 = (bf16[56,896]{1,0:T(8,128)(2,1)}, bf16[56,896]{1,0:T(8,128)(2,1)S(1)}, u32[]{:S(2)}, u32[]{:S(2)}) collective-permute-start(bf16[56,896]{1,0:T(8,128)(2,1)} %get-tuple-element.25), channel_id=1, source_target_pairs={{0,65},{1,64},{64,1},{65,0},{2,67},{3,66},{66,3},{67,2},{4,69},{5,... | collective-permute-start | bytes 301064 | tf_op jit(solution)/shard_map/ppermute | solution.py:329
  17.4 0.9 copy-start.7
  18.4 9.3 %collective-permute-start.8 = (bf16[1,272,128]{2,1,0:T(8,128)(2,1)S(1)}, bf16[1,272,128]{2,1,0:T(8,128)(2,1)S(1)}, u32[]{:S(2)}, u32[]{:S(2)}) collective-permute-start(bf16[1,272,128]{2,1,0:T(8,128)(2,1)S(1)} %get-tuple-element.31), channel_id=1, source_target_pairs={{0,4},{1,13},{2,6},{3,15},{4,0},{5,9},{6,2},{7,11},{8,12},{9,5},{1... | collective-permute-start | bytes 208904 | tf_op jit(solution)/shard_map/ppermute | solution.py:53
  21.1 8.3 %collective-permute-start.6 = (bf16[1,272,128]{2,1,0:T(8,128)(2,1)S(1)}, bf16[1,272,128]{2,1,0:T(8,128)(2,1)S(1)}, u32[]{:S(2)}, u32[]{:S(2)}) collective-permute-start(bf16[1,272,128]{2,1,0:T(8,128)(2,1)S(1)} %get-tuple-element.30), channel_id=1, source_target_pairs={{0,64},{1,67},{2,66},{3,65},{4,68},{5,71},{6,70},{7,69},{8,72},{9,... | collective-permute-start | bytes 208904 | tf_op jit(solution)/shard_map/ppermute | solution.py:53
  23.8 5.5 %collective-permute-start.7 = (bf16[1,272,128]{2,1,0:T(8,128)(2,1)S(1)}, bf16[1,272,128]{2,1,0:T(8,128)(2,1)S(1)}, u32[]{:S(2)}, u32[]{:S(2)}) collective-permute-start(bf16[1,272,128]{2,1,0:T(8,128)(2,1)S(1)} %get-tuple-element.29), channel_id=1, source_target_pairs={{0,16},{1,49},{2,18},{3,51},{4,20},{5,53},{6,22},{7,55},{8,24},{9,... | collective-permute-start | bytes 208904 | tf_op jit(solution)/shard_map/ppermute | solution.py:53
  29.6 8.2 %collective-permute-start.10 = (bf16[2,272,128]{2,1,0:T(8,128)(2,1)S(1)}, bf16[2,272,128]{2,1,0:T(8,128)(2,1)S(1)}, u32[]{:S(2)}, u32[]{:S(2)}) collective-permute-start(bf16[2,272,128]{2,1,0:T(8,128)(2,1)S(1)} %pad_maximum_fusion.7), channel_id=1, source_target_pairs={{0,12},{1,5},{2,14},{3,7},{4,8},{5,1},{6,10},{7,3},{8,4},{9,13},{1... | collective-permute-start | bytes 417800 | tf_op jit(solution)/shard_map/ppermute | solution.py:53
  29.6 7.9 %collective-permute-start.9 = (bf16[2,272,128]{2,1,0:T(8,128)(2,1)S(1)}, bf16[2,272,128]{2,1,0:T(8,128)(2,1)S(1)}, u32[]{:S(2)}, u32[]{:S(2)}) collective-permute-start(bf16[2,272,128]{2,1,0:T(8,128)(2,1)S(1)} %pad_maximum_fusion.6), channel_id=1, source_target_pairs={{0,16},{1,49},{2,18},{3,51},{4,20},{5,53},{6,22},{7,55},{8,24},{9,... | collective-permute-start | bytes 417800 | tf_op jit(solution)/shard_map/ppermute | solution.py:53
  32.4 5.1 %collective-permute-start.11 = (bf16[2,272,128]{2,1,0:T(8,128)(2,1)S(1)}, bf16[2,272,128]{2,1,0:T(8,128)(2,1)S(1)}, u32[]{:S(2)}, u32[]{:S(2)}) collective-permute-start(bf16[2,272,128]{2,1,0:T(8,128)(2,1)S(1)} %get-tuple-element.71), channel_id=1, source_target_pairs={{0,64},{1,67},{2,66},{3,65},{4,68},{5,71},{6,70},{7,69},{8,72},{9,... | collective-permute-start | bytes 417800 | tf_op jit(solution)/shard_map/ppermute | solution.py:53
  37.9 5.9 %collective-permute-start.13 = (bf16[4,272,128]{2,1,0:T(8,128)(2,1)S(1)}, bf16[4,272,128]{2,1,0:T(8,128)(2,1)S(1)}, u32[]{:S(2)}, u32[]{:S(2)}) collective-permute-start(bf16[4,272,128]{2,1,0:T(8,128)(2,1)S(1)} %pad_maximum_fusion.4), channel_id=1, source_target_pairs={{0,66},{1,65},{2,64},{3,67},{4,70},{5,69},{6,68},{7,71},{8,74},{9,... | collective-permute-start | bytes 835592 | tf_op jit(solution)/shard_map/ppermute | solution.py:53
  38.0 5.8 %collective-permute-start.12 = (bf16[4,272,128]{2,1,0:T(8,128)(2,1)S(1)}, bf16[4,272,128]{2,1,0:T(8,128)(2,1)S(1)}, u32[]{:S(2)}, u32[]{:S(2)}) collective-permute-start(bf16[4,272,128]{2,1,0:T(8,128)(2,1)S(1)} %pad_maximum_fusion.3), channel_id=1, source_target_pairs={{0,12},{1,5},{2,14},{3,7},{4,8},{5,1},{6,10},{7,3},{8,4},{9,13},{1... | collective-permute-start | bytes 835592 | tf_op jit(solution)/shard_map/ppermute | solution.py:53
  39.6 6.7 %collective-permute-start.14 = (bf16[4,272,128]{2,1,0:T(8,128)(2,1)S(1)}, bf16[4,272,128]{2,1,0:T(8,128)(2,1)S(1)}, u32[]{:S(2)}, u32[]{:S(2)}) collective-permute-start(bf16[4,272,128]{2,1,0:T(8,128)(2,1)S(1)} %pad_maximum_fusion.5), channel_id=1, source_target_pairs={{0,16},{1,49},{2,18},{3,51},{4,20},{5,53},{6,22},{7,55},{8,24},{9,... | collective-permute-start | bytes 835592 | tf_op jit(solution)/shard_map/ppermute | solution.py:53
  44.0 13.4 %collective-permute-start.16 = (bf16[8,272,128]{2,1,0:T(8,128)(2,1)S(1)}, bf16[8,272,128]{2,1,0:T(8,128)(2,1)S(1)}, u32[]{:S(2)}, u32[]{:S(2)}) collective-permute-start(bf16[8,272,128]{2,1,0:T(8,128)(2,1)S(1)} %pad_maximum_fusion.1), channel_id=1, source_target_pairs={{0,48},{1,17},{2,50},{3,19},{4,52},{5,21},{6,54},{7,23},{8,56},{9,... | collective-permute-start | bytes 1671176 | tf_op jit(solution)/shard_map/ppermute | solution.py:53
  46.5 8.8 %collective-permute-start.18 = (bf16[8,272,128]{2,1,0:T(8,128)(2,1)S(1)}, bf16[8,272,128]{2,1,0:T(8,128)(2,1)S(1)}, u32[]{:S(2)}, u32[]{:S(2)}) collective-permute-start(bf16[8,272,128]{2,1,0:T(8,128)(2,1)S(1)} %pad_maximum_fusion.2), channel_id=1, source_target_pairs={{0,12},{1,5},{2,14},{3,7},{4,8},{5,1},{6,10},{7,3},{8,4},{9,13},{1... | collective-permute-start | bytes 1671176 | tf_op jit(solution)/shard_map/ppermute | solution.py:53
  46.9 10.1 %collective-permute-start.15 = (bf16[8,272,128]{2,1,0:T(8,128)(2,1)S(1)}, bf16[8,272,128]{2,1,0:T(8,128)(2,1)S(1)}, u32[]{:S(2)}, u32[]{:S(2)}) collective-permute-start(bf16[8,272,128]{2,1,0:T(8,128)(2,1)S(1)} %pad_maximum_fusion), channel_id=1, source_target_pairs={{0,66},{1,65},{2,64},{3,67},{4,70},{5,69},{6,68},{7,71},{8,74},{9,... | collective-permute-start | bytes 1671176 | tf_op jit(solution)/shard_map/ppermute | solution.py:53
  55.5 14.7 %collective-permute-start.19 = (bf16[16,272,128]{2,1,0:T(8,128)(2,1)S(1)}, bf16[16,272,128]{2,1,0:T(8,128)(2,1)S(1)}, u32[]{:S(2)}, u32[]{:S(2)}) collective-permute-start(bf16[16,272,128]{2,1,0:T(8,128)(2,1)S(1)} %get-tuple-element.63), channel_id=1, source_target_pairs={{0,66},{1,65},{2,64},{3,67},{4,70},{5,69},{6,68},{7,71},{8,74},{9,... | collective-permute-start | bytes 3342344 | tf_op jit(solution)/shard_map/ppermute | solution.py:53
  57.2 14.7 %collective-permute-start.21 = (bf16[16,272,128]{2,1,0:T(8,128)(2,1)S(1)}, bf16[16,272,128]{2,1,0:T(8,128)(2,1)S(1)}, u32[]{:S(2)}, u32[]{:S(2)}) collective-permute-start(bf16[16,272,128]{2,1,0:T(8,128)(2,1)S(1)} %get-tuple-element.61), channel_id=1, source_target_pairs={{0,48},{1,17},{2,50},{3,19},{4,52},{5,21},{6,54},{7,23},{8,56},{9,... | collective-permute-start | bytes 3342344 | tf_op jit(solution)/shard_map/ppermute | solution.py:53
  57.6 15.9 %collective-permute-start.17 = (bf16[16,272,128]{2,1,0:T(8,128)(2,1)S(1)}, bf16[16,272,128]{2,1,0:T(8,128)(2,1)S(1)}, u32[]{:S(2)}, u32[]{:S(2)}) collective-permute-start(bf16[16,272,128]{2,1,0:T(8,128)(2,1)S(1)} %get-tuple-element.60), channel_id=1, source_target_pairs={{0,4},{1,13},{2,6},{3,15},{4,0},{5,9},{6,2},{7,11},{8,12},{9,5},{1... | collective-permute-start | bytes 3342344 | tf_op jit(solution)/shard_map/ppermute | solution.py:53
  70.2 14.3 %copy-start.5 = (f32[1,3,56,3584]{3,2,1,0:T(8,128)S(1)}, f32[1,3,56,3584]{3,2,1,0:T(8,128)}, u32[]{:S(2)}) copy-start(f32[1,3,56,3584]{3,2,1,0:T(8,128)} %v_ref.1) | copy-start | bytes 7225348
  70.2 14.3 %copy-start.6 = (bf16[1,3,56,3584]{3,2,1,0:T(8,128)(2,1)S(1)}, bf16[1,3,56,3584]{3,2,1,0:T(8,128)(2,1)}, u32[]{:S(2)}) copy-start(bf16[1,3,56,3584]{3,2,1,0:T(8,128)(2,1)} %g_ref.1) | copy-start | bytes 3612676
  70.6 26.7 %collective-permute-start.20 = (bf16[32,272,128]{2,1,0:T(8,128)(2,1)S(1)}, bf16[32,272,128]{2,1,0:T(8,128)(2,1)S(1)}, u32[]{:S(2)}, u32[]{:S(2)}) collective-permute-start(bf16[32,272,128]{2,1,0:T(8,128)(2,1)S(1)} %select_dynamic-update-slice_fusion.2.refs_0_), channel_id=1, source_target_pairs={{0,48},{1,17},{2,50},{3,19},{4,52},{5,21},{6,54},{7,23},{8,56},{9,... | collective-permute-start | bytes 6684680 | tf_op jit(solution)/shard_map/ppermute | solution.py:53
  73.6 10.9 %copy-start.3 = (f32[56,3584]{1,0:T(8,128)S(1)}, f32[56,3584]{1,0:T(8,128)}, u32[]{:S(2)}) copy-start(f32[56,3584]{1,0:T(8,128)} %momentum_ref.3) | copy-start | bytes 2408452
  73.6 10.9 %copy-start.4 = (f32[1,3,56,3584]{3,2,1,0:T(8,128)S(1)}, f32[1,3,56,3584]{3,2,1,0:T(8,128)}, u32[]{:S(2)}) copy-start(f32[1,3,56,3584]{3,2,1,0:T(8,128)} %m_ref.1) | copy-start | bytes 7225348
  73.9 29.5 %collective-permute-start.23 = (bf16[32,272,128]{2,1,0:T(8,128)(2,1)S(1)}, bf16[32,272,128]{2,1,0:T(8,128)(2,1)S(1)}, u32[]{:S(2)}, u32[]{:S(2)}) collective-permute-start(bf16[32,272,128]{2,1,0:T(8,128)(2,1)S(1)} %select_dynamic-update-slice_fusion.refs_0_.refs_4_), channel_id=1, source_target_pairs={{0,64},{1,67},{2,66},{3,65},{4,68},{5,71},{6,70},{7,69},{8,72},{9,... | collective-permute-start | bytes 6684680 | tf_op jit(solution)/shard_map/ppermute | solution.py:53
  74.1 10.4 %copy-start.1 = (f32[1,3,56,3584]{3,2,1,0:T(8,128)S(1)}, f32[1,3,56,3584]{3,2,1,0:T(8,128)}, u32[]{:S(2)}) copy-start(f32[1,3,56,3584]{3,2,1,0:T(8,128)} %p_ref.1) | copy-start | bytes 7225348
  74.1 10.4 %copy-start.2 = (f32[56,3584]{1,0:T(8,128)S(1)}, f32[56,3584]{1,0:T(8,128)}, u32[]{:S(2)}) copy-start(f32[56,3584]{1,0:T(8,128)} %anchor_ref.3) | copy-start | bytes 2408452
  74.1 10.4 %copy-start.8 = (s32[3]{0:T(128)S(1)}, s32[3]{0:T(128)}, u32[]{:S(2)}) copy-start(s32[3]{0:T(128)} %plan_ref.3) | copy-start | bytes 40
  74.5 22.8 %copy-start = (bf16[512,3584]{1,0:T(8,128)(2,1)S(1)}, bf16[512,3584]{1,0:T(8,128)(2,1)}, u32[]{:S(2)}) copy-start(bf16[512,3584]{1,0:T(8,128)(2,1)} %mine_ref.5) | copy-start | bytes 11010052
  74.5 35.2 %collective-permute-start.22 = (bf16[32,272,128]{2,1,0:T(8,128)(2,1)S(1)}, bf16[32,272,128]{2,1,0:T(8,128)(2,1)S(1)}, u32[]{:S(2)}, u32[]{:S(2)}) collective-permute-start(bf16[32,272,128]{2,1,0:T(8,128)(2,1)S(1)} %select_dynamic-update-slice_fusion.1.refs_2_), channel_id=1, source_target_pairs={{0,4},{1,13},{2,6},{3,15},{4,0},{5,9},{6,2},{7,11},{8,12},{9,5},{1... | collective-permute-start | bytes 6684680 | tf_op jit(solution)/shard_map/ppermute | solution.py:53
  74.7 9.7 %collective-permute-start.2 = (bf16[56,896]{1,0:T(8,128)(2,1)S(1)}, bf16[56,896]{1,0:T(8,128)(2,1)S(1)}, u32[]{:S(2)}, u32[]{:S(2)}) collective-permute-start(bf16[56,896]{1,0:T(8,128)(2,1)S(1)} %collective-permute-done.1.cross_ref), channel_id=1, source_target_pairs={{0,1},{1,0},{2,3},{3,2},{4,5},{5,4},{6,7},{7,6},{8,9},{9,8},{10,11... | collective-permute-start | bytes 301064 | tf_op jit(solution)/shard_map/ppermute | solution.py:63
  118.5 12.7 %collective-permute-start.26 = (bf16[512,768]{1,0:T(8,128)(2,1)S(1)}, bf16[512,768]{1,0:T(8,128)(2,1)S(1)}, u32[]{:S(2)}, u32[]{:S(2)}) collective-permute-start(bf16[512,768]{1,0:T(8,128)(2,1)S(1)} %get-tuple-element.42), channel_id=1, source_target_pairs={{0,1},{1,0},{2,3},{3,2},{4,5},{5,4},{6,7},{7,6},{8,9},{9,8},{10,11... | collective-permute-start | bytes 2359304 | tf_op jit(solution)/shard_map/ppermute | solution.py:63
  127.7 2.7 %collective-permute-start.25 = (bf16[512,512]{1,0:T(8,128)(2,1)S(1)}, bf16[512,512]{1,0:T(8,128)(2,1)S(1)}, u32[]{:S(2)}, u32[]{:S(2)}) collective-permute-start(bf16[512,512]{1,0:T(8,128)(2,1)S(1)} %get-tuple-element.41), channel_id=1, source_target_pairs={{0,1},{1,0},{2,3},{3,2},{4,5},{5,4},{6,7},{7,6},{8,9},{9,8},{10,11... | collective-permute-start | bytes 1572872 | tf_op jit(solution)/shard_map/ppermute | solution.py:63
  127.8 3.3 %collective-permute-start.24 = (bf16[512,512]{1,0:T(8,128)(2,1)S(1)}, bf16[512,512]{1,0:T(8,128)(2,1)S(1)}, u32[]{:S(2)}, u32[]{:S(2)}) collective-permute-start(bf16[512,512]{1,0:T(8,128)(2,1)S(1)} %get-tuple-element.40), channel_id=1, source_target_pairs={{0,1},{1,0},{2,3},{3,2},{4,5},{5,4},{6,7},{7,6},{8,9},{9,8},{10,11... | collective-permute-start | bytes 1572872 | tf_op jit(solution)/shard_map/ppermute | solution.py:63

commit v3 on v2

--- a/solution.py
+++ b/solution.py
@@ -29,6 +29,7 @@
 SHARE = (48, 32, 32)
 ROOM = max(SHARE)
 TOK = 512
+PITCH = 64
 
 ALL = ("yl", "z", "x", "yh", "core")
 CHIPS = ("z", "x", "yh")
@@ -111,11 +112,14 @@
         anchor = held[4 + 2 * i]
         diff = anchor - held[5 + 2 * i]
         out_ref[...] = anchor - OLD * held[8 + i] - NEW * diff
-        rest_ref[:, lanes(half * PART, PART)] = diff.astype(jnp.bfloat16)
-
-
-def join_kernel(keep_ref, got_ref, same_ref, cross_ref, after_ref, *refs):
-    outs, rows_ref = refs[:-1], refs[-1]
+        for tile in range(PART // TILE):
+            rows = jnp.concatenate([diff[:, tile * TILE : (tile + 1) * TILE], jnp.zeros((PITCH - ROWS, TILE), jnp.float32)])
+            at = pl.multiple_of((half * (PART // TILE) + tile) * PITCH, PITCH)
+            rest_ref[pl.ds(at, PITCH), :] = rows.astype(jnp.bfloat16)
+
+
+def join_kernel(keep_ref, got_ref, same_ref, cross_ref, after_ref, rest_ref, *refs):
+    outs, rows_ref = refs[:GROUPS], refs[-1]
     core = lax.axis_index("core")
     for at, base_ref, term_ref in ((core, keep_ref, same_ref), (1 - core, got_ref, cross_ref)):
         rows = pl.ds(pl.multiple_of(at * ROWS, 8), ROWS)
@@ -164,7 +168,14 @@
                 got = jnp.where(
                     half == core, same_ref[...].astype(jnp.float32), cross_ref[...].astype(jnp.float32)
                 )
-                rest = rest_ref[:, half * PART : (half + 1) * PART].astype(jnp.float32)
+                first = half * (PART // TILE)
+                rest = jnp.concatenate(
+                    [
+                        rest_ref[(first + tile) * PITCH : (first + tile + 1) * PITCH].astype(jnp.float32)[:ROWS]
+                        for tile in range(PART // TILE)
+                    ],
+                    axis=1,
+                )
                 anchor = anchor_ref[:, cols]
                 summed = (anchor - p_ref[0, 0, :, cols]).astype(jnp.bfloat16).astype(jnp.float32) + jnp.where(
                     part == island, got, rest
@@ -185,13 +196,8 @@
     return [half * HALF + part * PART + tile * TILE for tile in tiles for part in (0, 1)]
 
 
-def piece_of(pieces, r, tile, q, size):
-    at = CHIP if tile == 2 * GROUPS else 0 if tile < GROUPS else CHIP + ROOM
-    return pieces[r // 32].at[r % 32, pl.ds(at, size)]
-
-
-def multiply_kernel(tiles, n_pieces, has_buffer, mine_ref, theirs_ref, *refs):
-    pieces, refs = refs[:n_pieces], refs[n_pieces + 1 + has_buffer :]
+def multiply_kernel(tiles, has_buffer, mine_ref, theirs_ref, *refs):
+    pieces, refs = refs[: 2 * GROUPS], refs[2 * GROUPS + 1 + has_buffer :]
     result_ref, out_ref, weight, staged, load_sem, out_sem, result_sem = refs
     core = lax.axis_index("core")
     here = lax.axis_index("z") * 16 + lax.axis_index("x") * 4 + lax.axis_index("yh") * 2 + lax.axis_index("yl")
@@ -202,11 +208,11 @@
         for q in (tile % GROUPS,) if tile < 2 * GROUPS else range(GROUPS):
             size = CHIP if tile < 2 * GROUPS else SHARE[q]
             masks = [code_masks(q, c) for c in (0, 1)]
-            own = pieces if n_pieces == 2 else pieces[2 * q : 2 * q + 2]
+            at = 0 if tile < 2 * GROUPS else CHIP
             for r in range(64):
                 code = here ^ jnp.where(core == 0, masks[0][r], masks[1][r])
                 pltpu.make_async_copy(
-                    piece_of(own, r, tile, q, size),
+                    pieces[2 * q + r // 32].at[r % 32, pl.ds(at, size)],
                     weight.at[g, code // 2, pl.ds(done, size), lanes(code % 2 * TILE, TILE)],
                     load_sem.at[g],
                 ).start()
@@ -232,7 +238,7 @@
     pltpu.make_async_copy(staged.at[1], staged.at[1], result_sem).wait()
 
 
-TILES = ((0, 3), (2, 5), (1, 4, 6))
+TILES = ((0, 1, 2, 6), (3, 4, 5))
 
 
 def place_kernel(buffer_ref, *refs):
@@ -282,7 +288,7 @@
         grid_spec=pltpu.PrefetchScalarGridSpec(
             num_scalar_prefetch=2,
             grid=(LAYERS,),
-            in_specs=[stepped] * 4 + [whole((ROWS, D))] * 2 + [whole((ROWS, PART))] * 2 + [whole((ROWS, 2 * PART))] + [ANY] * len(after),
+            in_specs=[stepped] * 4 + [whole((ROWS, D))] * 2 + [whole((ROWS, PART))] * 2 + [whole((D // 2 // TILE * PITCH, TILE))] + [ANY] * len(after),
             out_specs=[stepped] * 3 + [whole((ROWS, D)), whole((8, 128))],
         ),
         out_shape=[state] * 3 + [shape((ROWS, D), jnp.float32), shape((8, 128), jnp.int32)],
@@ -295,7 +301,7 @@
     width = 2 * TILE * len(tiles)
     args = [tokens, others, *pieces, after] + ([] if buffer is None else [buffer])
     return pl.pallas_call(
-        functools.partial(multiply_kernel, tiles, len(pieces), buffer is not None),
+        functools.partial(multiply_kernel, tiles, buffer is not None),
         in_specs=[VMEM] * 2 + [ANY] * (len(args) - 2),
         out_specs=[ANY, ANY],
         out_shape=[shape((TOK, D), jnp.bfloat16), shape((TOK, width), jnp.bfloat16)],
@@ -321,24 +327,23 @@
         first_kernel,
         in_specs=[SMEM] * 2 + [ANY] * 3,
         out_specs=[VMEM] * 5,
-        out_shape=[shape((ROWS, PART), bf16)] * 2 + [shape((ROWS, PART), f32)] * 2 + [shape((ROWS, 2 * PART), bf16)],
+        out_shape=[shape((ROWS, PART), bf16)] * 2 + [shape((ROWS, PART), f32)] * 2 + [shape((D // 2 // TILE * PITCH, TILE), bf16)],
         scratch_shapes=[pltpu.VMEM((10, ROWS, PART), f32), pltpu.SemaphoreType.DMA((10,))],
         compiler_params=FULL,
     )(*scalars, anchor, momentum, inner_params)
     same = lax.ppermute(send_same, "yl", [(0, 1), (1, 0)])
     cross = lax.ppermute(send_cross, ("yl", "core"), [(i, 3 - i) for i in range(4)])
     got = swap_cores(give)
-    cur = pl.pallas_call(
+    *cur, rest = pl.pallas_call(
         join_kernel,
-        in_specs=[VMEM] * 4 + [ANY],
-        out_specs=[VMEM] * GROUPS,
-        out_shape=[shape((1, 2 * CHIP + ROOM, TILE), bf16)] * GROUPS,
+        in_specs=[VMEM] * 4 + [ANY] * 2,
+        out_specs=[VMEM] * GROUPS + [ANY],
+        out_shape=[shape((1, 2 * CHIP + ROOM, TILE), bf16)] * GROUPS + [shape(rest.shape, bf16)],
+        input_output_aliases={5: GROUPS},
         scratch_shapes=[pltpu.VMEM((CHIP, PART), f32)],
         compiler_params=SMALL,
-    )(keep, got, same, cross, others)
+    )(keep, got, same, cross, others, rest)
     rest_received = lax.ppermute(rest, "yl", [(0, 1), (1, 0)])
-
-    late = rest_received[0, 0] != rest_received[0, 0]
 
     def doubled(value, step, before):
         out, arrivals = [], []
@@ -347,29 +352,34 @@
             ahead = (arrivals[q - 1] if q else before)[0]
             waits = (ahead != ahead)[None]
             if step == 2 and q == 0:
-                waits = waits | late
+                late = rest_received[: 2 * CHIP + ROOM]
+                waits = waits | (late != late)[None]
             out.append(jnp.concatenate([value[q], jnp.where(waits, value[q], arrived)], axis=0))
             arrivals.append(arrived)
-        return out, arrivals[1], arrivals[-1]
+        return out, arrivals[1]
 
     before = jnp.zeros((1, 2 * CHIP + ROOM, TILE), bf16)
     for step in range(4):
-        cur, before, _ = doubled(cur, step, before)
-    both, _, before = doubled(cur, 4, before)
+        cur, before = doubled(cur, step, before)
+    cut = CHIP + ROOM
+    fifth = [exchange(cur[q], q, 4) for q in range(GROUPS)]
+    both = [
+        [jnp.concatenate([cur[q][:, rows], fifth[q][:, rows]], axis=0) for q in range(GROUPS)]
+        for rows in (slice(0, cut), slice(cut, None))
+    ]
     params_out, first_out, second_out, momentum_out, done = layers_call(
         (frag_index, plan), (inner_params, inner_grads, adam_first, adam_second), (anchor, momentum), (same, swap_cores(cross)),
-        rest_received, (before,),
+        rest_received, (fifth[-1],),
     )
-    sixth = [exchange(both[q], q, 5) for q in range(GROUPS)]
-    pieces = [[both[q], sixth[q]] for q in range(GROUPS)]
+    sixth = [[exchange(value[q], q, 5) for q in range(GROUPS)] for value in both]
     swapped, result = [], None
-    for tiles in TILES:
-        needed = pieces[tiles[0]] if len(tiles) == 2 else sum(pieces, [])
-        result, out = multiply_call(tiles, tokens, others, needed, done, result)
+    for tiles, have, got in zip(TILES, both, sixth):
+        pieces = [piece for q in range(GROUPS) for piece in (have[q], got[q])]
+        result, out = multiply_call(tiles, tokens, others, pieces, done, result)
         swapped.append(swap_cores(out))
     projected = pl.pallas_call(
         place_kernel,
-        in_specs=[ANY] + [VMEM] * GROUPS,
+        in_specs=[ANY] + [VMEM] * len(TILES),
         out_specs=ANY,
         out_shape=shape((TOK, D), bf16),
         scratch_shapes=[pltpu.SemaphoreType.DMA((14,))],

time: 134 us -> 121 us (0.903)
  starting transfers between devices: 41.3 us -> 32.7 us
    ppermute x6 -> x5, starting transfers between devices: 20.3 us -> 6.48 us  [swap_cores(): return lax.ppermute(value, 'core', [(0, 1), (1, 0)])]
    ppermute x18 -> x21, starting transfers between devices: 17.6 us -> 24.1 us  [exchange(): lax.ppermute(value, ALL, [(i, flipped(i, flips[i % 2])) for i in range(12...]
    ppermute x1, waiting for transfers between devices: 3.29 us -> 0.01 us  [body(): rest_received = lax.ppermute(rest, 'yl', [(0, 1), (1, 0)])]
    ppermute x1, waiting for transfers between devices: 0.34 us -> 2.16 us  [body(): same = lax.ppermute(send_same, 'yl', [(0, 1), (1, 0)])]
    ppermute x18 -> x21, waiting for transfers between devices: 42.8 us -> 44.6 us  [exchange(): lax.ppermute(value, ALL, [(i, flipped(i, flips[i % 2])) for i in range(12...]
    ppermute x1, starting transfers between devices: 1.46 us -> 0.01 us  [body(): rest_received = lax.ppermute(rest, 'yl', [(0, 1), (1, 0)])]
    ppermute x1, starting transfers between devices: 0.09 us -> 1.46 us  [body(): same = lax.ppermute(send_same, 'yl', [(0, 1), (1, 0)])]
    ppermute x6 -> x5, waiting for transfers between devices: 3.85 us -> 2.5 us  [swap_cores(): return lax.ppermute(value, 'core', [(0, 1), (1, 0)])]
  transfers between devices with their start and end apart: 27 -> 29, of which waited for: 15 -> 14; matrix products, arithmetic and copies ran while one was open for 3% -> 2% of each run, Pallas kernels for 16% -> 23%
where the time goes in v3:
time: 121 us
  waiting for transfers between devices  52.1 us (43%)
  starting transfers between devices  32.7 us (27%)
  Pallas kernels  29.6 us (24%)
  local copies, waits for them, and re-layouts  2.39 us (2%)
  other arithmetic  2.3 us (2%)
  between operations  1.92 us (2%)
    ppermute x21, waiting for transfers between devices, exchange(): lax.ppermute(value, ALL, [(i, flipped(i, flips[i % 2])) for i in range(12...  44.6 us
    ppermute x21, starting transfers between devices, exchange(): lax.ppermute(value, ALL, [(i, flipped(i, flips[i % 2])) for i in range(12...  24.1 us
    pallas_call x2, Pallas kernels, multiply_call(): pl.pallas_call(functools.partial(multiply_kernel, tiles, buffer is not No...  20 us
    ppermute x5, starting transfers between devices, swap_cores(): return lax.ppermute(value, 'core', [(0, 1), (1, 0)])  6.48 us
    pallas_call x1, Pallas kernels, layers_call(): pl.pallas_call(layers_kernel, grid_spec=pltpu.PrefetchScalarGridSpec(num_...  4.85 us
    pallas_call x1, Pallas kernels, body(): pl.pallas_call(first_kernel, in_specs=[SMEM] * 2 + [ANY] * 3, out_specs=[...  3.3 us
    ppermute x1, waiting for transfers between devices, body(): lax.ppermute(send_cross, ('yl', 'core'), [(i, 3 - i) for i in range(4)])  2.83 us
    ppermute x5, waiting for transfers between devices, swap_cores(): return lax.ppermute(value, 'core', [(0, 1), (1, 0)])  2.5 us
  transfers between devices with their start and end apart: 29, of which 14 were waited for; matrix products, arithmetic and copies ran while one was open for 2% of the time, Pallas kernels for 23%

profile of v3, /device:TPU:1, one launch (start us, length us, event | category | flops | bytes accessed | tf_op | source)
XLA Modules:
  0.0 121.0 jit_solution(6101305143074313882)
XLA Ops:
  0.6 1.5 %collective-permute-start.4 = (bf16[512,3584]{1,0:T(8,128)(2,1)}, bf16[512,3584]{1,0:T(8,128)(2,1)S(1)}, u32[]{:S(2)}, u32[]{:S(2)}) collective-permute-start(bf16[512,3584]{1,0:T(8,128)(2,1)} %mine_ref.3), channel_id=1, source_target_pairs={{0,1},{1,0},{2,3},{3,2},{4,5},{5,4},{6,7},{7,6},{8,9},{9,8},{10,11... | collective-permute-start | bytes 11010056 | tf_op jit(solution)/shard_map/ppermute | solution.py:64
  2.8 3.3 %shard_map.128 = (bf16[56,896]{1,0:T(8,128)(2,1)}, bf16[56,896]{1,0:T(8,128)(2,1)}, f32[56,896]{1,0:T(8,128)}, f32[56,896]{1,0:T(8,128)}, bf16[896,128]{1,0:T(8,128)(2,1)}) custom-call(s32[1]{0:T(128)S(6)} %copy.33.frag_ref, s32[3]{0:T(128)} %plan_ref.3, f32[56,3584]{1,0:T(8,128)} %anchor_ref.3, f32[56,3584]{1,0:T(8,128)} %momentum_ref.3, ...), custom_call_target="tpu_custom_call" | custom-call | tf_op jit(solution)/shard_map/pallas_call | solution.py:326
  6.1 0.1 collective-permute-start.3
  6.2 1.5 %collective-permute-start = (bf16[56,896]{1,0:T(8,128)(2,1)}, bf16[56,896]{1,0:T(8,128)(2,1)S(1)}, u32[]{:S(2)}, u32[]{:S(2)}) collective-permute-start(bf16[56,896]{1,0:T(8,128)(2,1)} %get-tuple-element.23), channel_id=1, source_target_pairs={{0,64},{64,0},{1,65},{65,1},{2,66},{66,2},{3,67},{67,3},{4,68},{68... | collective-permute-start | bytes 301064 | tf_op jit(solution)/shard_map/ppermute | solution.py:334
  7.6 0.7 collective-permute-start.1
  8.3 2.2 %collective-permute-done.same_ref = bf16[56,896]{1,0:T(8,128)(2,1)S(1)} collective-permute-done((bf16[56,896]{1,0:T(8,128)(2,1)}, bf16[56,896]{1,0:T(8,128)(2,1)S(1)}, u32[]{:S(2)}, u32[]{:S(2)}) %collective-permute-start) | collective-permute-done | bytes 100384 | tf_op jit(solution)/shard_map/ppermute | solution.py:334
  10.5 2.8 %collective-permute-done.1.cross_ref = bf16[56,896]{1,0:T(8,128)(2,1)S(1)} collective-permute-done((bf16[56,896]{1,0:T(8,128)(2,1)}, bf16[56,896]{1,0:T(8,128)(2,1)S(1)}, u32[]{:S(2)}, u32[]{:S(2)}) %collective-permute-start.1) | collective-permute-done | bytes 100384 | tf_op jit(solution)/shard_map/ppermute | solution.py:335
  13.3 0.9 copy-done.6
  14.3 0.9 copy-done.7
  15.2 0.1 shard_map.129
  15.3 2.5 %collective-permute-start.8 = (bf16[1,272,128]{2,1,0:T(8,128)(2,1)S(1)}, bf16[1,272,128]{2,1,0:T(8,128)(2,1)S(1)}, u32[]{:S(2)}, u32[]{:S(2)}) collective-permute-start(bf16[1,272,128]{2,1,0:T(8,128)(2,1)S(1)} %get-tuple-element.31), channel_id=1, source_target_pairs={{0,4},{1,13},{2,6},{3,15},{4,0},{5,9},{6,2},{7,11},{8,12},{9,5},{1... | collective-permute-start | bytes 208904 | tf_op jit(solution)/shard_map/ppermute | solution.py:54
  17.8 2.7 %collective-permute-start.6 = (bf16[1,272,128]{2,1,0:T(8,128)(2,1)S(1)}, bf16[1,272,128]{2,1,0:T(8,128)(2,1)S(1)}, u32[]{:S(2)}, u32[]{:S(2)}) collective-permute-start(bf16[1,272,128]{2,1,0:T(8,128)(2,1)S(1)} %get-tuple-element.30), channel_id=1, source_target_pairs={{0,64},{1,67},{2,66},{3,65},{4,68},{5,71},{6,70},{7,69},{8,72},{9,... | collective-permute-start | bytes 208904 | tf_op jit(solution)/shard_map/ppermute | solution.py:54
  20.6 3.8 %collective-permute-start.7 = (bf16[1,272,128]{2,1,0:T(8,128)(2,1)S(1)}, bf16[1,272,128]{2,1,0:T(8,128)(2,1)S(1)}, u32[]{:S(2)}, u32[]{:S(2)}) collective-permute-start(bf16[1,272,128]{2,1,0:T(8,128)(2,1)S(1)} %get-tuple-element.29), channel_id=1, source_target_pairs={{0,16},{1,49},{2,18},{3,51},{4,20},{5,53},{6,22},{7,55},{8,24},{9,... | collective-permute-start | bytes 208904 | tf_op jit(solution)/shard_map/ppermute | solution.py:54
  24.3 1.7 %collective-permute-done.7 = bf16[1,272,128]{2,1,0:T(8,128)(2,1)S(1)} collective-permute-done((bf16[1,272,128]{2,1,0:T(8,128)(2,1)S(1)}, bf16[1,272,128]{2,1,0:T(8,128)(2,1)S(1)}, u32[]{:S(2)}, u32[]{:S(2)}) %collective-permute-start.7) | collective-permute-done | bytes 69664 | tf_op jit(solution)/shard_map/ppermute | solution.py:54
  26.0 0.1 constant_dynamic-update-slice_fusion.8
  26.1 0.1 collective-permute-start.10
  26.2 2.8 %collective-permute-start.9 = (bf16[2,272,128]{2,1,0:T(8,128)(2,1)S(1)}, bf16[2,272,128]{2,1,0:T(8,128)(2,1)S(1)}, u32[]{:S(2)}, u32[]{:S(2)}) collective-permute-start(bf16[2,272,128]{2,1,0:T(8,128)(2,1)S(1)} %pad_maximum_fusion.12), channel_id=1, source_target_pairs={{0,16},{1,49},{2,18},{3,51},{4,20},{5,53},{6,22},{7,55},{8,24},{9,... | collective-permute-start | bytes 417800 | tf_op jit(solution)/shard_map/ppermute | solution.py:54
  29.0 0.6 collective-permute-start.11
  29.7 4.5 %collective-permute-done.11 = bf16[2,272,128]{2,1,0:T(8,128)(2,1)S(1)} collective-permute-done((bf16[2,272,128]{2,1,0:T(8,128)(2,1)S(1)}, bf16[2,272,128]{2,1,0:T(8,128)(2,1)S(1)}, u32[]{:S(2)}, u32[]{:S(2)}) %collective-permute-start.11) | collective-permute-done | bytes 139296 | tf_op jit(solution)/shard_map/ppermute | solution.py:54
  34.3 1.5 %collective-permute-start.12 = (bf16[4,272,128]{2,1,0:T(8,128)(2,1)S(1)}, bf16[4,272,128]{2,1,0:T(8,128)(2,1)S(1)}, u32[]{:S(2)}, u32[]{:S(2)}) collective-permute-start(bf16[4,272,128]{2,1,0:T(8,128)(2,1)S(1)} %pad_maximum_fusion.9), channel_id=1, source_target_pairs={{0,12},{1,5},{2,14},{3,7},{4,8},{5,1},{6,10},{7,3},{8,4},{9,13},{1... | collective-permute-start | bytes 835592 | tf_op jit(solution)/shard_map/ppermute | solution.py:54
  35.9 0.2 collective-permute-start.14
  36.1 0.1 constant_dynamic-update-slice_fusion.3
  36.3 1.4 %collective-permute-start.13 = (bf16[4,272,128]{2,1,0:T(8,128)(2,1)S(1)}, bf16[4,272,128]{2,1,0:T(8,128)(2,1)S(1)}, u32[]{:S(2)}, u32[]{:S(2)}) collective-permute-start(bf16[4,272,128]{2,1,0:T(8,128)(2,1)S(1)} %pad_maximum_fusion.10), channel_id=1, source_target_pairs={{0,66},{1,65},{2,64},{3,67},{4,70},{5,69},{6,68},{7,71},{8,74},{9,... | collective-permute-start | bytes 835592 | tf_op jit(solution)/shard_map/ppermute | solution.py:54
  37.7 4.9 %collective-permute-done.14 = bf16[4,272,128]{2,1,0:T(8,128)(2,1)S(1)} collective-permute-done((bf16[4,272,128]{2,1,0:T(8,128)(2,1)S(1)}, bf16[4,272,128]{2,1,0:T(8,128)(2,1)S(1)}, u32[]{:S(2)}, u32[]{:S(2)}) %collective-permute-start.14) | collective-permute-done | bytes 278560 | tf_op jit(solution)/shard_map/ppermute | solution.py:54
  42.6 0.1 constant_dynamic-update-slice_fusion.6
  42.8 0.1 collective-permute-start.18
  42.9 0.1 constant_dynamic-update-slice_fusion.10
  43.1 0.3 collective-permute-start.15
  43.5 0.1 constant_dynamic-update-slice_fusion.2
  43.6 7.9 %collective-permute-done.18 = bf16[8,272,128]{2,1,0:T(8,128)(2,1)S(1)} collective-permute-done((bf16[8,272,128]{2,1,0:T(8,128)(2,1)S(1)}, bf16[8,272,128]{2,1,0:T(8,128)(2,1)S(1)}, u32[]{:S(2)}, u32[]{:S(2)}) %collective-permute-start.18) | collective-permute-done | bytes 557088 | tf_op jit(solution)/shard_map/ppermute | solution.py:54
  51.5 0.2 pad_maximum_fusion.7
  51.8 0.1 collective-permute-start.16
  51.8 0.3 collective-permute-start.19
  52.2 0.2 select_dynamic-update-slice_fusion
  52.4 1.5 %collective-permute-start.21 = (bf16[16,272,128]{2,1,0:T(8,128)(2,1)S(1)}, bf16[16,272,128]{2,1,0:T(8,128)(2,1)S(1)}, u32[]{:S(2)}, u32[]{:S(2)}) collective-permute-start(bf16[16,272,128]{2,1,0:T(8,128)(2,1)S(1)} %select_dynamic-update-slice_fusion), channel_id=1, source_target_pairs={{0,48},{1,17},{2,50},{3,19},{4,52},{5,21},{6,54},{7,23},{8,56},{9,... | collective-permute-start | bytes 3342344 | tf_op jit(solution)/shard_map/ppermute | solution.py:54
  53.9 6.6 %collective-permute-done.16 = bf16[8,272,128]{2,1,0:T(8,128)(2,1)S(1)} collective-permute-done((bf16[8,272,128]{2,1,0:T(8,128)(2,1)S(1)}, bf16[8,272,128]{2,1,0:T(8,128)(2,1)S(1)}, u32[]{:S(2)}, u32[]{:S(2)}) %collective-permute-start.16) | collective-permute-done | bytes 557088 | tf_op jit(solution)/shard_map/ppermute | solution.py:54
  60.5 0.2 select_dynamic-update-slice_fusion.2
  60.7 0.6 collective-permute-start.17
  61.4 5.1 %collective-permute-done.19 = bf16[16,272,128]{2,1,0:T(8,128)(2,1)S(1)} collective-permute-done((bf16[16,272,128]{2,1,0:T(8,128)(2,1)S(1)}, bf16[16,272,128]{2,1,0:T(8,128)(2,1)S(1)}, u32[]{:S(2)}, u32[]{:S(2)}) %collective-permute-start.19) | collective-permute-done | bytes 1114144 | tf_op jit(solution)/shard_map/ppermute | solution.py:54
  66.6 0.1 pad_maximum_fusion.refs_0_
  66.7 1.5 %collective-permute-start.24 = (bf16[32,160,128]{2,1,0:T(8,128)(2,1)S(1)}, bf16[32,160,128]{2,1,0:T(8,128)(2,1)S(1)}, u32[]{:S(2)}, u32[]{:S(2)}) collective-permute-start(bf16[32,160,128]{2,1,0:T(8,128)(2,1)S(1)} %pad_maximum_fusion.refs_0_), channel_id=1, source_target_pairs={{0,48},{1,17},{2,50},{3,19},{4,52},{5,21},{6,54},{7,23},{8,56},{9,... | collective-permute-start | bytes 3932168 | tf_op jit(solution)/shard_map/ppermute | solution.py:54
  68.2 4.3 %collective-permute-done.21 = bf16[16,272,128]{2,1,0:T(8,128)(2,1)S(1)} collective-permute-done((bf16[16,272,128]{2,1,0:T(8,128)(2,1)S(1)}, bf16[16,272,128]{2,1,0:T(8,128)(2,1)S(1)}, u32[]{:S(2)}, u32[]{:S(2)}) %collective-permute-start.21) | collective-permute-done | bytes 1114144 | tf_op jit(solution)/shard_map/ppermute | solution.py:54
  72.5 0.1 pad_maximum_fusion.1.refs_2_
  72.6 0.6 collective-permute-start.25
  73.2 3.4 %collective-permute-done.17.refs_0_ = bf16[16,272,128]{2,1,0:T(8,128)(2,1)S(1)} collective-permute-done((bf16[16,272,128]{2,1,0:T(8,128)(2,1)S(1)}, bf16[16,272,128]{2,1,0:T(8,128)(2,1)S(1)}, u32[]{:S(2)}, u32[]{:S(2)}) %collective-permute-start.17) | collective-permute-done | bytes 1114144 | tf_op jit(solution)/shard_map/ppermute | solution.py:54
  76.7 0.1 pad_maximum_fusion.2.refs_4_
  76.8 0.7 collective-permute-start.26
  77.5 2.6 %collective-permute-start.2 = (bf16[56,896]{1,0:T(8,128)(2,1)S(1)}, bf16[56,896]{1,0:T(8,128)(2,1)S(1)}, u32[]{:S(2)}, u32[]{:S(2)}) collective-permute-start(bf16[56,896]{1,0:T(8,128)(2,1)S(1)} %collective-permute-done.1.cross_ref), channel_id=1, source_target_pairs={{0,1},{1,0},{2,3},{3,2},{4,5},{5,4},{6,7},{7,6},{8,9},{9,8},{10,11... | collective-permute-start | bytes 301064 | tf_op jit(solution)/shard_map/ppermute | solution.py:64
  80.3 0.1 pad_maximum_fusion.3.refs_0_
  80.4 0.1 collective-permute-start.20
  80.6 0.1 pad_maximum_fusion.4.refs_2_
  80.7 0.1 pad_maximum_fusion.5.refs_4_
  80.8 0.2 collective-permute-done.2.cross_ref
  81.1 1.8 %collective-permute-start.22 = (bf16[32,112,128]{2,1,0:T(8,128)(2,1)S(1)}, bf16[32,112,128]{2,1,0:T(8,128)(2,1)S(1)}, u32[]{:S(2)}, u32[]{:S(2)}) collective-permute-start(bf16[32,112,128]{2,1,0:T(8,128)(2,1)S(1)} %pad_maximum_fusion.4.refs_2_), channel_id=1, source_target_pairs={{0,4},{1,13},{2,6},{3,15},{4,0},{5,9},{6,2},{7,11},{8,12},{9,5},{1... | collective-permute-start | bytes 2752520 | tf_op jit(solution)/shard_map/ppermute | solution.py:54
  82.9 3.6 %collective-permute-done.24.refs_1_ = bf16[32,160,128]{2,1,0:T(8,128)(2,1)S(1)} collective-permute-done((bf16[32,160,128]{2,1,0:T(8,128)(2,1)S(1)}, bf16[32,160,128]{2,1,0:T(8,128)(2,1)S(1)}, u32[]{:S(2)}, u32[]{:S(2)}) %collective-permute-start.24) | collective-permute-done | bytes 1310752 | tf_op jit(solution)/shard_map/ppermute | solution.py:54
  86.5 0.9 collective-permute-start.23
  87.5 4.9 %shard_map.130 = (f32[1,3,56,3584]{3,2,1,0:T(8,128)}, f32[1,3,56,3584]{3,2,1,0:T(8,128)}, f32[1,3,56,3584]{3,2,1,0:T(8,128)}, f32[56,3584]{1,0:T(8,128)}, s32[8,128]{1,0:T(8,128)S(1)}) custom-call(s32[1]{0:T(128)S(6)} %copy.33.frag_ref, s32[3]{0:T(128)S(1)} %copy-done.8, f32[1,3,56,3584]{3,2,1,0:T(8,128)S(1)} %copy-done, ...), custom_call_target="tpu_custom_call" | custom-call | flops 12042240 | bytes 18063360 | tf_op jit(solution)/shard_map/pallas_call | solution.py:286
  92.3 2.5 %collective-permute-done.26.refs_5_ = bf16[32,160,128]{2,1,0:T(8,128)(2,1)S(1)} collective-permute-done((bf16[32,160,128]{2,1,0:T(8,128)(2,1)S(1)}, bf16[32,160,128]{2,1,0:T(8,128)(2,1)S(1)}, u32[]{:S(2)}, u32[]{:S(2)}) %collective-permute-start.26) | collective-permute-done | bytes 1310752 | tf_op jit(solution)/shard_map/ppermute | solution.py:54
  94.9 11.3 %shard_map.131 = (bf16[512,3584]{1,0:T(8,128)(2,1)}, bf16[512,1024]{1,0:T(8,128)(2,1)S(1)}) custom-call(bf16[512,3584]{1,0:T(8,128)(2,1)S(1)} %copy-done.9, bf16[512,3584]{1,0:T(8,128)(2,1)S(1)} %collective-permute-done.4.after_ref.theirs_ref, bf16[32,160,128]{2,1,0:T(8,128)(2,1)S(1)} %pad_maximum_fusion.refs_0_, ...), custom_call_target="tpu_custom_call" | custom-call | flops 7516192768 | bytes 14680064 | tf_op jit(solution)/shard_map/pallas_call | solution.py:303
  106.2 2.2 %collective-permute-start.27 = (bf16[512,1024]{1,0:T(8,128)(2,1)S(1)}, bf16[512,1024]{1,0:T(8,128)(2,1)S(1)}, u32[]{:S(2)}, u32[]{:S(2)}) collective-permute-start(bf16[512,1024]{1,0:T(8,128)(2,1)S(1)} %get-tuple-element.39), channel_id=1, source_target_pairs={{0,1},{1,0},{2,3},{3,2},{4,5},{5,4},{6,7},{7,6},{8,9},{9,8},{10,11... | collective-permute-start | bytes 3145736 | tf_op jit(solution)/shard_map/ppermute | solution.py:64
  108.4 8.7 %shard_map.132 = (bf16[512,3584]{1,0:T(8,128)(2,1)}, bf16[512,768]{1,0:T(8,128)(2,1)S(1)}) custom-call(bf16[512,3584]{1,0:T(8,128)(2,1)S(1)} %copy-done.9, bf16[512,3584]{1,0:T(8,128)(2,1)S(1)} %collective-permute-done.4.after_ref.theirs_ref, bf16[32,112,128]{2,1,0:T(8,128)(2,1)S(1)} %pad_maximum_fusion.3.refs_0_, ...), custom_call_target="tpu_custom_call", output_to_operand_aliasing={{0}: (9, {})} | custom-call | flops 5637144576 | bytes 12845056 | tf_op jit(solution)/shard_map/pallas_call | solution.py:303
  117.1 0.1 collective-permute-start.28
  117.2 2.3 %collective-permute-done.28.refs_1_ = bf16[512,768]{1,0:T(8,128)(2,1)S(1)} collective-permute-done((bf16[512,768]{1,0:T(8,128)(2,1)S(1)}, bf16[512,768]{1,0:T(8,128)(2,1)S(1)}, u32[]{:S(2)}, u32[]{:S(2)}) %collective-permute-start.28) | collective-permute-done | bytes 786464 | tf_op jit(solution)/shard_map/ppermute | solution.py:64
  119.5 1.3 %shard_map.133 = bf16[512,3584]{1,0:T(8,128)(2,1)} custom-call(bf16[512,3584]{1,0:T(8,128)(2,1)} %get-tuple-element.38.buffer_ref, bf16[512,1024]{1,0:T(8,128)(2,1)S(1)} %collective-permute-done.27.refs_0_, bf16[512,768]{1,0:T(8,128)(2,1)S(1)} %collective-permute-done.28.refs_1_), custom_call_target="tpu_custom_call", output_to_operand_aliasing={{}: (0, {})} | custom-call | tf_op jit(solution)/shard_map/pallas_call | solution.py:380
  (65 shorter events, 1.1 us)
Async XLA Ops:
  0.6 12.7 %collective-permute-start.4 = (bf16[512,3584]{1,0:T(8,128)(2,1)}, bf16[512,3584]{1,0:T(8,128)(2,1)S(1)}, u32[]{:S(2)}, u32[]{:S(2)}) collective-permute-start(bf16[512,3584]{1,0:T(8,128)(2,1)} %mine_ref.3), channel_id=1, source_target_pairs={{0,1},{1,0},{2,3},{3,2},{4,5},{5,4},{6,7},{7,6},{8,9},{9,8},{10,11... | collective-permute-start | bytes 11010056 | tf_op jit(solution)/shard_map/ppermute | solution.py:64
  6.1 7.2 %collective-permute-start.3 = (f32[56,896]{1,0:T(8,128)}, f32[56,896]{1,0:T(8,128)S(1)}, u32[]{:S(2)}, u32[]{:S(2)}) collective-permute-start(f32[56,896]{1,0:T(8,128)} %get-tuple-element.26), channel_id=1, source_target_pairs={{0,1},{1,0},{2,3},{3,2},{4,5},{5,4},{6,7},{7,6},{8,9},{9,8},{10,11... | collective-permute-start | bytes 602120 | tf_op jit(solution)/shard_map/ppermute | solution.py:64
  6.2 4.3 %collective-permute-start = (bf16[56,896]{1,0:T(8,128)(2,1)}, bf16[56,896]{1,0:T(8,128)(2,1)S(1)}, u32[]{:S(2)}, u32[]{:S(2)}) collective-permute-start(bf16[56,896]{1,0:T(8,128)(2,1)} %get-tuple-element.23), channel_id=1, source_target_pairs={{0,64},{64,0},{1,65},{65,1},{2,66},{66,2},{3,67},{67,3},{4,68},{68... | collective-permute-start | bytes 301064 | tf_op jit(solution)/shard_map/ppermute | solution.py:334
  7.6 5.7 %collective-permute-start.1 = (bf16[56,896]{1,0:T(8,128)(2,1)}, bf16[56,896]{1,0:T(8,128)(2,1)S(1)}, u32[]{:S(2)}, u32[]{:S(2)}) collective-permute-start(bf16[56,896]{1,0:T(8,128)(2,1)} %get-tuple-element.24), channel_id=1, source_target_pairs={{0,65},{1,64},{64,1},{65,0},{2,67},{3,66},{66,3},{67,2},{4,69},{5,... | collective-permute-start | bytes 301064 | tf_op jit(solution)/shard_map/ppermute | solution.py:335
  13.3 0.9 copy-start.6
  14.3 0.9 copy-start.7
  15.3 9.0 %collective-permute-start.8 = (bf16[1,272,128]{2,1,0:T(8,128)(2,1)S(1)}, bf16[1,272,128]{2,1,0:T(8,128)(2,1)S(1)}, u32[]{:S(2)}, u32[]{:S(2)}) collective-permute-start(bf16[1,272,128]{2,1,0:T(8,128)(2,1)S(1)} %get-tuple-element.31), channel_id=1, source_target_pairs={{0,4},{1,13},{2,6},{3,15},{4,0},{5,9},{6,2},{7,11},{8,12},{9,5},{1... | collective-permute-start | bytes 208904 | tf_op jit(solution)/shard_map/ppermute | solution.py:54
  17.8 6.5 %collective-permute-start.6 = (bf16[1,272,128]{2,1,0:T(8,128)(2,1)S(1)}, bf16[1,272,128]{2,1,0:T(8,128)(2,1)S(1)}, u32[]{:S(2)}, u32[]{:S(2)}) collective-permute-start(bf16[1,272,128]{2,1,0:T(8,128)(2,1)S(1)} %get-tuple-element.30), channel_id=1, source_target_pairs={{0,64},{1,67},{2,66},{3,65},{4,68},{5,71},{6,70},{7,69},{8,72},{9,... | collective-permute-start | bytes 208904 | tf_op jit(solution)/shard_map/ppermute | solution.py:54
  20.6 15.5 %collective-permute-start.5 = (bf16[896,128]{1,0:T(8,128)(2,1)S(1)}, bf16[896,128]{1,0:T(8,128)(2,1)S(1)}, u32[]{:S(2)}, u32[]{:S(2)}) collective-permute-start(bf16[896,128]{1,0:T(8,128)(2,1)S(1)} %get-tuple-element.28), channel_id=1, source_target_pairs={{0,64},{64,0},{1,65},{65,1},{2,66},{66,2},{3,67},{67,3},{4,68},{68... | collective-permute-start | bytes 688136 | tf_op jit(solution)/shard_map/ppermute | solution.py:346
  20.6 5.5 %collective-permute-start.7 = (bf16[1,272,128]{2,1,0:T(8,128)(2,1)S(1)}, bf16[1,272,128]{2,1,0:T(8,128)(2,1)S(1)}, u32[]{:S(2)}, u32[]{:S(2)}) collective-permute-start(bf16[1,272,128]{2,1,0:T(8,128)(2,1)S(1)} %get-tuple-element.29), channel_id=1, source_target_pairs={{0,16},{1,49},{2,18},{3,51},{4,20},{5,53},{6,22},{7,55},{8,24},{9,... | collective-permute-start | bytes 208904 | tf_op jit(solution)/shard_map/ppermute | solution.py:54
  26.1 10.0 %collective-permute-start.10 = (bf16[2,272,128]{2,1,0:T(8,128)(2,1)S(1)}, bf16[2,272,128]{2,1,0:T(8,128)(2,1)S(1)}, u32[]{:S(2)}, u32[]{:S(2)}) collective-permute-start(bf16[2,272,128]{2,1,0:T(8,128)(2,1)S(1)} %pad_maximum_fusion.13), channel_id=1, source_target_pairs={{0,12},{1,5},{2,14},{3,7},{4,8},{5,1},{6,10},{7,3},{8,4},{9,13},{1... | collective-permute-start | bytes 417800 | tf_op jit(solution)/shard_map/ppermute | solution.py:54
  26.2 7.9 %collective-permute-start.9 = (bf16[2,272,128]{2,1,0:T(8,128)(2,1)S(1)}, bf16[2,272,128]{2,1,0:T(8,128)(2,1)S(1)}, u32[]{:S(2)}, u32[]{:S(2)}) collective-permute-start(bf16[2,272,128]{2,1,0:T(8,128)(2,1)S(1)} %pad_maximum_fusion.12), channel_id=1, source_target_pairs={{0,16},{1,49},{2,18},{3,51},{4,20},{5,53},{6,22},{7,55},{8,24},{9,... | collective-permute-start | bytes 417800 | tf_op jit(solution)/shard_map/ppermute | solution.py:54
  29.0 5.1 %collective-permute-start.11 = (bf16[2,272,128]{2,1,0:T(8,128)(2,1)S(1)}, bf16[2,272,128]{2,1,0:T(8,128)(2,1)S(1)}, u32[]{:S(2)}, u32[]{:S(2)}) collective-permute-start(bf16[2,272,128]{2,1,0:T(8,128)(2,1)S(1)} %get-tuple-element.60), channel_id=1, source_target_pairs={{0,64},{1,67},{2,66},{3,65},{4,68},{5,71},{6,70},{7,69},{8,72},{9,... | collective-permute-start | bytes 417800 | tf_op jit(solution)/shard_map/ppermute | solution.py:54
  34.3 8.7 %collective-permute-start.12 = (bf16[4,272,128]{2,1,0:T(8,128)(2,1)S(1)}, bf16[4,272,128]{2,1,0:T(8,128)(2,1)S(1)}, u32[]{:S(2)}, u32[]{:S(2)}) collective-permute-start(bf16[4,272,128]{2,1,0:T(8,128)(2,1)S(1)} %pad_maximum_fusion.9), channel_id=1, source_target_pairs={{0,12},{1,5},{2,14},{3,7},{4,8},{5,1},{6,10},{7,3},{8,4},{9,13},{1... | collective-permute-start | bytes 835592 | tf_op jit(solution)/shard_map/ppermute | solution.py:54
  35.9 6.7 %collective-permute-start.14 = (bf16[4,272,128]{2,1,0:T(8,128)(2,1)S(1)}, bf16[4,272,128]{2,1,0:T(8,128)(2,1)S(1)}, u32[]{:S(2)}, u32[]{:S(2)}) collective-permute-start(bf16[4,272,128]{2,1,0:T(8,128)(2,1)S(1)} %pad_maximum_fusion.11), channel_id=1, source_target_pairs={{0,16},{1,49},{2,18},{3,51},{4,20},{5,53},{6,22},{7,55},{8,24},{9,... | collective-permute-start | bytes 835592 | tf_op jit(solution)/shard_map/ppermute | solution.py:54
  36.3 7.2 %collective-permute-start.13 = (bf16[4,272,128]{2,1,0:T(8,128)(2,1)S(1)}, bf16[4,272,128]{2,1,0:T(8,128)(2,1)S(1)}, u32[]{:S(2)}, u32[]{:S(2)}) collective-permute-start(bf16[4,272,128]{2,1,0:T(8,128)(2,1)S(1)} %pad_maximum_fusion.10), channel_id=1, source_target_pairs={{0,66},{1,65},{2,64},{3,67},{4,70},{5,69},{6,68},{7,71},{8,74},{9,... | collective-permute-start | bytes 835592 | tf_op jit(solution)/shard_map/ppermute | solution.py:54
  42.8 8.8 %collective-permute-start.18 = (bf16[8,272,128]{2,1,0:T(8,128)(2,1)S(1)}, bf16[8,272,128]{2,1,0:T(8,128)(2,1)S(1)}, u32[]{:S(2)}, u32[]{:S(2)}) collective-permute-start(bf16[8,272,128]{2,1,0:T(8,128)(2,1)S(1)} %pad_maximum_fusion.8), channel_id=1, source_target_pairs={{0,12},{1,5},{2,14},{3,7},{4,8},{5,1},{6,10},{7,3},{8,4},{9,13},{1... | collective-permute-start | bytes 1671176 | tf_op jit(solution)/shard_map/ppermute | solution.py:54
  43.1 9.1 %collective-permute-start.15 = (bf16[8,272,128]{2,1,0:T(8,128)(2,1)S(1)}, bf16[8,272,128]{2,1,0:T(8,128)(2,1)S(1)}, u32[]{:S(2)}, u32[]{:S(2)}) collective-permute-start(bf16[8,272,128]{2,1,0:T(8,128)(2,1)S(1)} %pad_maximum_fusion.6), channel_id=1, source_target_pairs={{0,66},{1,65},{2,64},{3,67},{4,70},{5,69},{6,68},{7,71},{8,74},{9,... | collective-permute-start | bytes 1671176 | tf_op jit(solution)/shard_map/ppermute | solution.py:54
  51.8 8.8 %collective-permute-start.16 = (bf16[8,272,128]{2,1,0:T(8,128)(2,1)S(1)}, bf16[8,272,128]{2,1,0:T(8,128)(2,1)S(1)}, u32[]{:S(2)}, u32[]{:S(2)}) collective-permute-start(bf16[8,272,128]{2,1,0:T(8,128)(2,1)S(1)} %get-tuple-element.67), channel_id=1, source_target_pairs={{0,48},{1,17},{2,50},{3,19},{4,52},{5,21},{6,54},{7,23},{8,56},{9,... | collective-permute-start | bytes 1671176 | tf_op jit(solution)/shard_map/ppermute | solution.py:54
  51.8 14.7 %collective-permute-start.19 = (bf16[16,272,128]{2,1,0:T(8,128)(2,1)S(1)}, bf16[16,272,128]{2,1,0:T(8,128)(2,1)S(1)}, u32[]{:S(2)}, u32[]{:S(2)}) collective-permute-start(bf16[16,272,128]{2,1,0:T(8,128)(2,1)S(1)} %get-tuple-element.68), channel_id=1, source_target_pairs={{0,66},{1,65},{2,64},{3,67},{4,70},{5,69},{6,68},{7,71},{8,74},{9,... | collective-permute-start | bytes 3342344 | tf_op jit(solution)/shard_map/ppermute | solution.py:54
  52.4 20.0 %collective-permute-start.21 = (bf16[16,272,128]{2,1,0:T(8,128)(2,1)S(1)}, bf16[16,272,128]{2,1,0:T(8,128)(2,1)S(1)}, u32[]{:S(2)}, u32[]{:S(2)}) collective-permute-start(bf16[16,272,128]{2,1,0:T(8,128)(2,1)S(1)} %select_dynamic-update-slice_fusion), channel_id=1, source_target_pairs={{0,48},{1,17},{2,50},{3,19},{4,52},{5,21},{6,54},{7,23},{8,56},{9,... | collective-permute-start | bytes 3342344 | tf_op jit(solution)/shard_map/ppermute | solution.py:54
  60.7 15.9 %collective-permute-start.17 = (bf16[16,272,128]{2,1,0:T(8,128)(2,1)S(1)}, bf16[16,272,128]{2,1,0:T(8,128)(2,1)S(1)}, u32[]{:S(2)}, u32[]{:S(2)}) collective-permute-start(bf16[16,272,128]{2,1,0:T(8,128)(2,1)S(1)} %select_dynamic-update-slice_fusion.2), channel_id=1, source_target_pairs={{0,4},{1,13},{2,6},{3,15},{4,0},{5,9},{6,2},{7,11},{8,12},{9,5},{1... | collective-permute-start | bytes 3342344 | tf_op jit(solution)/shard_map/ppermute | solution.py:54
  66.7 19.7 %collective-permute-start.24 = (bf16[32,160,128]{2,1,0:T(8,128)(2,1)S(1)}, bf16[32,160,128]{2,1,0:T(8,128)(2,1)S(1)}, u32[]{:S(2)}, u32[]{:S(2)}) collective-permute-start(bf16[32,160,128]{2,1,0:T(8,128)(2,1)S(1)} %pad_maximum_fusion.refs_0_), channel_id=1, source_target_pairs={{0,48},{1,17},{2,50},{3,19},{4,52},{5,21},{6,54},{7,23},{8,56},{9,... | collective-permute-start | bytes 3932168 | tf_op jit(solution)/shard_map/ppermute | solution.py:54
  72.6 19.7 %collective-permute-start.25 = (bf16[32,160,128]{2,1,0:T(8,128)(2,1)S(1)}, bf16[32,160,128]{2,1,0:T(8,128)(2,1)S(1)}, u32[]{:S(2)}, u32[]{:S(2)}) collective-permute-start(bf16[32,160,128]{2,1,0:T(8,128)(2,1)S(1)} %pad_maximum_fusion.1.refs_2_), channel_id=1, source_target_pairs={{0,4},{1,13},{2,6},{3,15},{4,0},{5,9},{6,2},{7,11},{8,12},{9,5},{1... | collective-permute-start | bytes 3932168 | tf_op jit(solution)/shard_map/ppermute | solution.py:54
  76.8 18.0 %collective-permute-start.26 = (bf16[32,160,128]{2,1,0:T(8,128)(2,1)S(1)}, bf16[32,160,128]{2,1,0:T(8,128)(2,1)S(1)}, u32[]{:S(2)}, u32[]{:S(2)}) collective-permute-start(bf16[32,160,128]{2,1,0:T(8,128)(2,1)S(1)} %pad_maximum_fusion.2.refs_4_), channel_id=1, source_target_pairs={{0,64},{1,67},{2,66},{3,65},{4,68},{5,71},{6,70},{7,69},{8,72},{9,... | collective-permute-start | bytes 3932168 | tf_op jit(solution)/shard_map/ppermute | solution.py:54
  77.5 3.5 %collective-permute-start.2 = (bf16[56,896]{1,0:T(8,128)(2,1)S(1)}, bf16[56,896]{1,0:T(8,128)(2,1)S(1)}, u32[]{:S(2)}, u32[]{:S(2)}) collective-permute-start(bf16[56,896]{1,0:T(8,128)(2,1)S(1)} %collective-permute-done.1.cross_ref), channel_id=1, source_target_pairs={{0,1},{1,0},{2,3},{3,2},{4,5},{5,4},{6,7},{7,6},{8,9},{9,8},{10,11... | collective-permute-start | bytes 301064 | tf_op jit(solution)/shard_map/ppermute | solution.py:64
  80.1 7.3 %copy-start.5 = (bf16[1,3,56,3584]{3,2,1,0:T(8,128)(2,1)S(1)}, bf16[1,3,56,3584]{3,2,1,0:T(8,128)(2,1)}, u32[]{:S(2)}) copy-start(bf16[1,3,56,3584]{3,2,1,0:T(8,128)(2,1)} %g_ref.1) | copy-start | bytes 3612676
  80.2 7.2 %copy-start.4 = (f32[1,3,56,3584]{3,2,1,0:T(8,128)S(1)}, f32[1,3,56,3584]{3,2,1,0:T(8,128)}, u32[]{:S(2)}) copy-start(f32[1,3,56,3584]{3,2,1,0:T(8,128)} %v_ref.1) | copy-start | bytes 7225348
  80.3 7.1 %copy-start.3 = (f32[1,3,56,3584]{3,2,1,0:T(8,128)S(1)}, f32[1,3,56,3584]{3,2,1,0:T(8,128)}, u32[]{:S(2)}) copy-start(f32[1,3,56,3584]{3,2,1,0:T(8,128)} %m_ref.1) | copy-start | bytes 7225348
  80.4 28.0 %collective-permute-start.20 = (bf16[32,112,128]{2,1,0:T(8,128)(2,1)S(1)}, bf16[32,112,128]{2,1,0:T(8,128)(2,1)S(1)}, u32[]{:S(2)}, u32[]{:S(2)}) collective-permute-start(bf16[32,112,128]{2,1,0:T(8,128)(2,1)S(1)} %pad_maximum_fusion.3.refs_0_), channel_id=1, source_target_pairs={{0,48},{1,17},{2,50},{3,19},{4,52},{5,21},{6,54},{7,23},{8,56},{9,... | collective-permute-start | bytes 2752520 | tf_op jit(solution)/shard_map/ppermute | solution.py:54
  80.5 6.9 %copy-start.1 = (f32[56,3584]{1,0:T(8,128)S(1)}, f32[56,3584]{1,0:T(8,128)}, u32[]{:S(2)}) copy-start(f32[56,3584]{1,0:T(8,128)} %anchor_ref.3) | copy-start | bytes 2408452
  80.6 6.9 %copy-start.2 = (f32[56,3584]{1,0:T(8,128)S(1)}, f32[56,3584]{1,0:T(8,128)}, u32[]{:S(2)}) copy-start(f32[56,3584]{1,0:T(8,128)} %momentum_ref.3) | copy-start | bytes 2408452
  80.7 6.8 %copy-start = (f32[1,3,56,3584]{3,2,1,0:T(8,128)S(1)}, f32[1,3,56,3584]{3,2,1,0:T(8,128)}, u32[]{:S(2)}) copy-start(f32[1,3,56,3584]{3,2,1,0:T(8,128)} %p_ref.1) | copy-start | bytes 7225348
  80.7 6.7 %copy-start.8 = (s32[3]{0:T(128)S(1)}, s32[3]{0:T(128)}, u32[]{:S(2)}) copy-start(s32[3]{0:T(128)} %plan_ref.3) | copy-start | bytes 40
  80.8 14.0 %copy-start.9 = (bf16[512,3584]{1,0:T(8,128)(2,1)S(1)}, bf16[512,3584]{1,0:T(8,128)(2,1)}, u32[]{:S(2)}) copy-start(bf16[512,3584]{1,0:T(8,128)(2,1)} %mine_ref.3) | copy-start | bytes 11010052
  81.1 27.3 %collective-permute-start.22 = (bf16[32,112,128]{2,1,0:T(8,128)(2,1)S(1)}, bf16[32,112,128]{2,1,0:T(8,128)(2,1)S(1)}, u32[]{:S(2)}, u32[]{:S(2)}) collective-permute-start(bf16[32,112,128]{2,1,0:T(8,128)(2,1)S(1)} %pad_maximum_fusion.4.refs_2_), channel_id=1, source_target_pairs={{0,4},{1,13},{2,6},{3,15},{4,0},{5,9},{6,2},{7,11},{8,12},{9,5},{1... | collective-permute-start | bytes 2752520 | tf_op jit(solution)/shard_map/ppermute | solution.py:54
  86.5 21.9 %collective-permute-start.23 = (bf16[32,112,128]{2,1,0:T(8,128)(2,1)S(1)}, bf16[32,112,128]{2,1,0:T(8,128)(2,1)S(1)}, u32[]{:S(2)}, u32[]{:S(2)}) collective-permute-start(bf16[32,112,128]{2,1,0:T(8,128)(2,1)S(1)} %pad_maximum_fusion.5.refs_4_), channel_id=1, source_target_pairs={{0,64},{1,67},{2,66},{3,65},{4,68},{5,71},{6,70},{7,69},{8,72},{9,... | collective-permute-start | bytes 2752520 | tf_op jit(solution)/shard_map/ppermute | solution.py:54
  106.2 13.3 %collective-permute-start.27 = (bf16[512,1024]{1,0:T(8,128)(2,1)S(1)}, bf16[512,1024]{1,0:T(8,128)(2,1)S(1)}, u32[]{:S(2)}, u32[]{:S(2)}) collective-permute-start(bf16[512,1024]{1,0:T(8,128)(2,1)S(1)} %get-tuple-element.39), channel_id=1, source_target_pairs={{0,1},{1,0},{2,3},{3,2},{4,5},{5,4},{6,7},{7,6},{8,9},{9,8},{10,11... | collective-permute-start | bytes 3145736 | tf_op jit(solution)/shard_map/ppermute | solution.py:64
  117.1 2.4 %collective-permute-start.28 = (bf16[512,768]{1,0:T(8,128)(2,1)S(1)}, bf16[512,768]{1,0:T(8,128)(2,1)S(1)}, u32[]{:S(2)}, u32[]{:S(2)}) collective-permute-start(bf16[512,768]{1,0:T(8,128)(2,1)S(1)} %get-tuple-element.40), channel_id=1, source_target_pairs={{0,1},{1,0},{2,3},{3,2},{4,5},{5,4},{6,7},{7,6},{8,9},{9,8},{10,11... | collective-permute-start | bytes 2359304 | tf_op jit(solution)/shard_map/ppermute | solution.py:64

commit v4 on v3

--- a/solution.py
+++ b/solution.py
@@ -26,8 +26,7 @@
 PART = HALF // 2
 TILE = 128
 GROUPS = 3
-SHARE = (48, 32, 32)
-ROOM = max(SHARE)
+SHARE = (32, 48, 32)
 TOK = 512
 PITCH = 64
 
@@ -118,21 +117,23 @@
             rest_ref[pl.ds(at, PITCH), :] = rows.astype(jnp.bfloat16)
 
 
-def join_kernel(keep_ref, got_ref, same_ref, cross_ref, after_ref, rest_ref, *refs):
-    outs, rows_ref = refs[:GROUPS], refs[-1]
+def join_kernel(keep_hbm, got_ref, same_ref, cross_ref, after_ref, rest_ref, *refs):
+    outs, (rows_ref, keep_ref, sem) = refs[:GROUPS], refs[-3:]
     core = lax.axis_index("core")
-    for at, base_ref, term_ref in ((core, keep_ref, same_ref), (1 - core, got_ref, cross_ref)):
+    copy = pltpu.make_async_copy(keep_hbm, keep_ref, sem)
+    copy.start()
+    for at, base_ref, term_ref in ((1 - core, got_ref, cross_ref), (core, keep_ref, same_ref)):
+        if base_ref is keep_ref:
+            copy.wait()
         rows = pl.ds(pl.multiple_of(at * ROWS, 8), ROWS)
         rows_ref[rows, :] = base_ref[...] - NEW * term_ref[...].astype(jnp.float32)
     done = 0
     for q, out_ref in enumerate(outs):
         share = SHARE[q]
-        if share < ROOM:
-            out_ref[0, CHIP + share : CHIP + ROOM] = jnp.zeros((ROOM - share, TILE), jnp.bfloat16)
         for at, tile, start, size in (
             (0, q, 0, CHIP),
             (CHIP, 2 * GROUPS, done, share),
-            (CHIP + ROOM, GROUPS + q, 0, CHIP),
+            (CHIP + share, GROUPS + q, 0, CHIP),
         ):
             value = rows_ref[start : start + size, tile * TILE : (tile + 1) * TILE]
             out_ref[0, at : at + size] = value.astype(jnp.bfloat16)
@@ -261,6 +262,7 @@
 ANY = pl.BlockSpec(memory_space=pl.ANY)
 VMEM = pl.BlockSpec(memory_space=pltpu.VMEM)
 SMEM = pl.BlockSpec(memory_space=pltpu.SMEM)
+HBM = pl.BlockSpec(memory_space=pltpu.HBM)
 LIMIT = pltpu.CompilerParams(vmem_limit_bytes=24 * 2**20)
 FULL = pltpu.CompilerParams(vmem_limit_bytes=60 * 2**20)
 SMALL = pltpu.CompilerParams(vmem_limit_bytes=16 * 2**20)
@@ -336,36 +338,38 @@
     got = swap_cores(give)
     *cur, rest = pl.pallas_call(
         join_kernel,
-        in_specs=[VMEM] * 4 + [ANY] * 2,
-        out_specs=[VMEM] * GROUPS + [ANY],
-        out_shape=[shape((1, 2 * CHIP + ROOM, TILE), bf16)] * GROUPS + [shape(rest.shape, bf16)],
+        in_specs=[HBM] + [VMEM] * 3 + [ANY, HBM],
+        out_specs=[VMEM] * GROUPS + [HBM],
+        out_shape=[shape((1, 2 * CHIP + share, TILE), bf16) for share in SHARE] + [shape(rest.shape, bf16)],
         input_output_aliases={5: GROUPS},
-        scratch_shapes=[pltpu.VMEM((CHIP, PART), f32)],
+        scratch_shapes=[pltpu.VMEM((CHIP, PART), f32), pltpu.VMEM((ROWS, PART), f32), pltpu.SemaphoreType.DMA],
         compiler_params=SMALL,
     )(keep, got, same, cross, others, rest)
     rest_received = lax.ppermute(rest, "yl", [(0, 1), (1, 0)])
+
+    def differs(held, like):
+        rows = min(held.shape[0], like.shape[1])
+        return jnp.pad(held[:rows] != held[:rows], ((0, like.shape[1] - rows), (0, 0)))[None]
 
     def doubled(value, step, before):
         out, arrivals = [], []
         for q in range(GROUPS):
             arrived = exchange(value[q], q, step)
             ahead = (arrivals[q - 1] if q else before)[0]
-            waits = (ahead != ahead)[None]
+            waits = differs(ahead, value[q])
             if step == 2 and q == 0:
-                late = rest_received[: 2 * CHIP + ROOM]
-                waits = waits | (late != late)[None]
+                waits = waits | differs(rest_received, value[q])
             out.append(jnp.concatenate([value[q], jnp.where(waits, value[q], arrived)], axis=0))
             arrivals.append(arrived)
         return out, arrivals[1]
 
-    before = jnp.zeros((1, 2 * CHIP + ROOM, TILE), bf16)
+    before = jnp.zeros((1, CHIP, TILE), bf16)
     for step in range(4):
         cur, before = doubled(cur, step, before)
-    cut = CHIP + ROOM
     fifth = [exchange(cur[q], q, 4) for q in range(GROUPS)]
     both = [
-        [jnp.concatenate([cur[q][:, rows], fifth[q][:, rows]], axis=0) for q in range(GROUPS)]
-        for rows in (slice(0, cut), slice(cut, None))
+        [jnp.concatenate([cur[q][:, rows(q)], fifth[q][:, rows(q)]], axis=0) for q in range(GROUPS)]
+        for rows in (lambda q: slice(0, CHIP + SHARE[q]), lambda q: slice(CHIP + SHARE[q], None))
     ]
     params_out, first_out, second_out, momentum_out, done = layers_call(
         (frag_index, plan), (inner_params, inner_grads, adam_first, adam_second), (anchor, momentum), (same, swap_cores(cross)),

time: 121 us -> 113 us (0.934)
  waiting for transfers between devices: 52.1 us -> 39.3 us
  starting transfers between devices: 32.7 us -> 36.5 us
    ppermute x21, waiting for transfers between devices: 44.6 us -> 32.1 us  [exchange(): lax.ppermute(value, ALL, [(i, flipped(i, flips[i % 2])) for i in range(12...]
    ppermute x21, starting transfers between devices: 24.1 us -> 26.8 us  [exchange(): lax.ppermute(value, ALL, [(i, flipped(i, flips[i % 2])) for i in range(12...]
  transfers between devices with their start and end apart: 29 -> 29, of which waited for: 14 -> 13; matrix products, arithmetic and copies ran while one was open for 2% -> 3% of each run, Pallas kernels for 23% -> 25%
where the time goes in v4:
time: 113 us
  waiting for transfers between devices  39.3 us (35%)
  starting transfers between devices  36.5 us (32%)
  Pallas kernels  29.8 us (26%)
  other arithmetic  2.45 us (2%)
  local copies, waits for them, and re-layouts  2.43 us (2%)
  between operations  2.02 us (2%)
    ppermute x21, waiting for transfers between devices, exchange(): lax.ppermute(value, ALL, [(i, flipped(i, flips[i % 2])) for i in range(12...  32.1 us
    ppermute x21, starting transfers between devices, exchange(): lax.ppermute(value, ALL, [(i, flipped(i, flips[i % 2])) for i in range(12...  26.8 us
    pallas_call x2, Pallas kernels, multiply_call(): pl.pallas_call(functools.partial(multiply_kernel, tiles, buffer is not No...  20 us
    ppermute x5, starting transfers between devices, swap_cores(): return lax.ppermute(value, 'core', [(0, 1), (1, 0)])  7.6 us
    pallas_call x1, Pallas kernels, layers_call(): pl.pallas_call(layers_kernel, grid_spec=pltpu.PrefetchScalarGridSpec(num_...  4.85 us
    pallas_call x1, Pallas kernels, body(): pl.pallas_call(first_kernel, in_specs=[SMEM] * 2 + [ANY] * 3, out_specs=[...  3.3 us
    ppermute x1, waiting for transfers between devices, body(): lax.ppermute(send_cross, ('yl', 'core'), [(i, 3 - i) for i in range(4)])  2.83 us
    ppermute x5, waiting for transfers between devices, swap_cores(): return lax.ppermute(value, 'core', [(0, 1), (1, 0)])  2.26 us
  transfers between devices with their start and end apart: 29, of which 13 were waited for; matrix products, arithmetic and copies ran while one was open for 3% of the time, Pallas kernels for 25%

profile of v4, /device:TPU:1, one launch (start us, length us, event | category | flops | bytes accessed | tf_op | source)
XLA Modules:
  0.0 112.6 jit_solution(7110347484694787657)
XLA Ops:
  0.6 1.5 %collective-permute-start.4 = (bf16[512,3584]{1,0:T(8,128)(2,1)}, bf16[512,3584]{1,0:T(8,128)(2,1)S(1)}, u32[]{:S(2)}, u32[]{:S(2)}) collective-permute-start(bf16[512,3584]{1,0:T(8,128)(2,1)} %mine_ref.3), channel_id=1, source_target_pairs={{0,1},{1,0},{2,3},{3,2},{4,5},{5,4},{6,7},{7,6},{8,9},{9,8},{10,11... | collective-permute-start | bytes 11010056 | tf_op jit(solution)/shard_map/ppermute | solution.py:63
  2.8 3.3 %shard_map.128 = (bf16[56,896]{1,0:T(8,128)(2,1)}, bf16[56,896]{1,0:T(8,128)(2,1)}, f32[56,896]{1,0:T(8,128)}, f32[56,896]{1,0:T(8,128)}, bf16[896,128]{1,0:T(8,128)(2,1)}) custom-call(s32[1]{0:T(128)S(6)} %copy.32.frag_ref, s32[3]{0:T(128)} %plan_ref.3, f32[56,3584]{1,0:T(8,128)} %anchor_ref.3, f32[56,3584]{1,0:T(8,128)} %momentum_ref.3, ...), custom_call_target="tpu_custom_call" | custom-call | tf_op jit(solution)/shard_map/pallas_call | solution.py:328
  6.1 0.1 collective-permute-start.3
  6.2 1.5 %collective-permute-start = (bf16[56,896]{1,0:T(8,128)(2,1)}, bf16[56,896]{1,0:T(8,128)(2,1)S(1)}, u32[]{:S(2)}, u32[]{:S(2)}) collective-permute-start(bf16[56,896]{1,0:T(8,128)(2,1)} %get-tuple-element.23), channel_id=1, source_target_pairs={{0,64},{64,0},{1,65},{65,1},{2,66},{66,2},{3,67},{67,3},{4,68},{68... | collective-permute-start | bytes 301064 | tf_op jit(solution)/shard_map/ppermute | solution.py:336
  7.6 0.7 collective-permute-start.1
  8.3 2.1 %collective-permute-done.same_ref = bf16[56,896]{1,0:T(8,128)(2,1)S(1)} collective-permute-done((bf16[56,896]{1,0:T(8,128)(2,1)}, bf16[56,896]{1,0:T(8,128)(2,1)S(1)}, u32[]{:S(2)}, u32[]{:S(2)}) %collective-permute-start) | collective-permute-done | bytes 100384 | tf_op jit(solution)/shard_map/ppermute | solution.py:336
  10.5 2.8 %collective-permute-done.1.cross_ref = bf16[56,896]{1,0:T(8,128)(2,1)S(1)} collective-permute-done((bf16[56,896]{1,0:T(8,128)(2,1)}, bf16[56,896]{1,0:T(8,128)(2,1)S(1)}, u32[]{:S(2)}, u32[]{:S(2)}) %collective-permute-start.1) | collective-permute-done | bytes 100384 | tf_op jit(solution)/shard_map/ppermute | solution.py:337
  13.3 0.9 copy-done.6
  14.3 0.9 copy-done.7
  15.2 0.3 shard_map.129
  15.5 3.8 %collective-permute-start.7 = (bf16[1,256,128]{2,1,0:T(8,128)(2,1)S(1)}, bf16[1,256,128]{2,1,0:T(8,128)(2,1)S(1)}, u32[]{:S(2)}, u32[]{:S(2)}) collective-permute-start(bf16[1,256,128]{2,1,0:T(8,128)(2,1)S(1)} %get-tuple-element.29), channel_id=1, source_target_pairs={{0,16},{1,49},{2,18},{3,51},{4,20},{5,53},{6,22},{7,55},{8,24},{9,... | collective-permute-start | bytes 196616 | tf_op jit(solution)/shard_map/ppermute | solution.py:53
  19.3 2.7 %collective-permute-start.6 = (bf16[1,272,128]{2,1,0:T(8,128)(2,1)S(1)}, bf16[1,272,128]{2,1,0:T(8,128)(2,1)S(1)}, u32[]{:S(2)}, u32[]{:S(2)}) collective-permute-start(bf16[1,272,128]{2,1,0:T(8,128)(2,1)S(1)} %get-tuple-element.30), channel_id=1, source_target_pairs={{0,64},{1,67},{2,66},{3,65},{4,68},{5,71},{6,70},{7,69},{8,72},{9,... | collective-permute-start | bytes 208904 | tf_op jit(solution)/shard_map/ppermute | solution.py:53
  22.1 2.6 %collective-permute-start.8 = (bf16[1,256,128]{2,1,0:T(8,128)(2,1)S(1)}, bf16[1,256,128]{2,1,0:T(8,128)(2,1)S(1)}, u32[]{:S(2)}, u32[]{:S(2)}) collective-permute-start(bf16[1,256,128]{2,1,0:T(8,128)(2,1)S(1)} %get-tuple-element.31), channel_id=1, source_target_pairs={{0,4},{1,13},{2,6},{3,15},{4,0},{5,9},{6,2},{7,11},{8,12},{9,5},{1... | collective-permute-start | bytes 196616 | tf_op jit(solution)/shard_map/ppermute | solution.py:53
  24.6 1.8 %collective-permute-done.8 = bf16[1,256,128]{2,1,0:T(8,128)(2,1)S(1)} collective-permute-done((bf16[1,256,128]{2,1,0:T(8,128)(2,1)S(1)}, bf16[1,256,128]{2,1,0:T(8,128)(2,1)S(1)}, u32[]{:S(2)}, u32[]{:S(2)}) %collective-permute-start.8) | collective-permute-done | bytes 65568 | tf_op jit(solution)/shard_map/ppermute | solution.py:53
  26.5 0.1 constant_dynamic-update-slice_fusion.6
  26.6 0.6 collective-permute-start.11
  27.4 0.4 collective-permute-start.10
  27.8 0.2 collective-permute-start.9
  28.0 3.7 %collective-permute-done.11 = bf16[2,256,128]{2,1,0:T(8,128)(2,1)S(1)} collective-permute-done((bf16[2,256,128]{2,1,0:T(8,128)(2,1)S(1)}, bf16[2,256,128]{2,1,0:T(8,128)(2,1)S(1)}, u32[]{:S(2)}, u32[]{:S(2)}) %collective-permute-start.11) | collective-permute-done | bytes 131104 | tf_op jit(solution)/shard_map/ppermute | solution.py:53
  31.7 0.1 constant_dynamic-update-slice_fusion.5
  31.9 0.2 collective-permute-start.14
  32.1 0.9 collective-permute-done.9
  33.0 0.1 constant_dynamic-update-slice_fusion.9
  33.1 1.2 %collective-permute-start.12 = (bf16[4,272,128]{2,1,0:T(8,128)(2,1)S(1)}, bf16[4,272,128]{2,1,0:T(8,128)(2,1)S(1)}, u32[]{:S(2)}, u32[]{:S(2)}) collective-permute-start(bf16[4,272,128]{2,1,0:T(8,128)(2,1)S(1)} %pad_maximum_fusion.9), channel_id=1, source_target_pairs={{0,12},{1,5},{2,14},{3,7},{4,8},{5,1},{6,10},{7,3},{8,4},{9,13},{1... | collective-permute-start | bytes 835592 | tf_op jit(solution)/shard_map/ppermute | solution.py:53
  34.5 0.9 collective-permute-start.13
  35.5 3.2 %collective-permute-done.14 = bf16[4,256,128]{2,1,0:T(8,128)(2,1)S(1)} collective-permute-done((bf16[4,256,128]{2,1,0:T(8,128)(2,1)S(1)}, bf16[4,256,128]{2,1,0:T(8,128)(2,1)S(1)}, u32[]{:S(2)}, u32[]{:S(2)}) %collective-permute-start.14) | collective-permute-done | bytes 262176 | tf_op jit(solution)/shard_map/ppermute | solution.py:53
  38.7 0.1 constant_dynamic-update-slice_fusion.4
  38.9 0.1 collective-permute-start.18
  39.0 0.1 constant_dynamic-update-slice_fusion.8
  39.2 0.5 collective-permute-start.15
  39.8 0.4 collective-permute-done.13
  40.1 0.1 constant_dynamic-update-slice_fusion
  40.3 0.1 collective-permute-start.16
  40.4 6.9 %collective-permute-done.18 = bf16[8,256,128]{2,1,0:T(8,128)(2,1)S(1)} collective-permute-done((bf16[8,256,128]{2,1,0:T(8,128)(2,1)S(1)}, bf16[8,256,128]{2,1,0:T(8,128)(2,1)S(1)}, u32[]{:S(2)}, u32[]{:S(2)}) %collective-permute-start.18) | collective-permute-done | bytes 524320 | tf_op jit(solution)/shard_map/ppermute | solution.py:53
  47.3 0.2 select_dynamic-update-slice_fusion.1
  47.5 0.5 collective-permute-start.19
  48.1 0.2 select_dynamic-update-slice_fusion
  48.3 0.1 collective-permute-start.21
  48.4 0.3 collective-permute-done.16
  48.7 0.2 select_dynamic-update-slice_fusion.2
  48.9 2.6 %collective-permute-start.17 = (bf16[16,256,128]{2,1,0:T(8,128)(2,1)S(1)}, bf16[16,256,128]{2,1,0:T(8,128)(2,1)S(1)}, u32[]{:S(2)}, u32[]{:S(2)}) collective-permute-start(bf16[16,256,128]{2,1,0:T(8,128)(2,1)S(1)} %select_dynamic-update-slice_fusion.2), channel_id=1, source_target_pairs={{0,4},{1,13},{2,6},{3,15},{4,0},{5,9},{6,2},{7,11},{8,12},{9,5},{1... | collective-permute-start | bytes 3145736 | tf_op jit(solution)/shard_map/ppermute | solution.py:53
  51.6 9.9 %collective-permute-done.19 = bf16[16,256,128]{2,1,0:T(8,128)(2,1)S(1)} collective-permute-done((bf16[16,256,128]{2,1,0:T(8,128)(2,1)S(1)}, bf16[16,256,128]{2,1,0:T(8,128)(2,1)S(1)}, u32[]{:S(2)}, u32[]{:S(2)}) %collective-permute-start.19) | collective-permute-done | bytes 1048608 | tf_op jit(solution)/shard_map/ppermute | solution.py:53
  61.6 0.1 pad_maximum_fusion.1.refs_0_
  61.7 0.1 collective-permute-start.24
  61.8 2.4 %collective-permute-done.17.refs_0_ = bf16[16,256,128]{2,1,0:T(8,128)(2,1)S(1)} collective-permute-done((bf16[16,256,128]{2,1,0:T(8,128)(2,1)S(1)}, bf16[16,256,128]{2,1,0:T(8,128)(2,1)S(1)}, u32[]{:S(2)}, u32[]{:S(2)}) %collective-permute-start.17) | collective-permute-done | bytes 1048608 | tf_op jit(solution)/shard_map/ppermute | solution.py:53
  64.3 0.1 pad_maximum_fusion.refs_2_
  64.4 2.6 %collective-permute-start.25 = (bf16[32,160,128]{2,1,0:T(8,128)(2,1)S(1)}, bf16[32,160,128]{2,1,0:T(8,128)(2,1)S(1)}, u32[]{:S(2)}, u32[]{:S(2)}) collective-permute-start(bf16[32,160,128]{2,1,0:T(8,128)(2,1)S(1)} %pad_maximum_fusion.refs_2_), channel_id=1, source_target_pairs={{0,4},{1,13},{2,6},{3,15},{4,0},{5,9},{6,2},{7,11},{8,12},{9,5},{1... | collective-permute-start | bytes 3932168 | tf_op jit(solution)/shard_map/ppermute | solution.py:53
  67.0 0.1 pad_maximum_fusion.2.refs_4_
  67.1 2.2 %collective-permute-start.26 = (bf16[32,144,128]{2,1,0:T(8,128)(2,1)S(1)}, bf16[32,144,128]{2,1,0:T(8,128)(2,1)S(1)}, u32[]{:S(2)}, u32[]{:S(2)}) collective-permute-start(bf16[32,144,128]{2,1,0:T(8,128)(2,1)S(1)} %pad_maximum_fusion.2.refs_4_), channel_id=1, source_target_pairs={{0,64},{1,67},{2,66},{3,65},{4,68},{5,71},{6,70},{7,69},{8,72},{9,... | collective-permute-start | bytes 3538952 | tf_op jit(solution)/shard_map/ppermute | solution.py:53
  69.3 1.8 %collective-permute-start.2 = (bf16[56,896]{1,0:T(8,128)(2,1)S(1)}, bf16[56,896]{1,0:T(8,128)(2,1)S(1)}, u32[]{:S(2)}, u32[]{:S(2)}) collective-permute-start(bf16[56,896]{1,0:T(8,128)(2,1)S(1)} %collective-permute-done.1.cross_ref), channel_id=1, source_target_pairs={{0,1},{1,0},{2,3},{3,2},{4,5},{5,4},{6,7},{7,6},{8,9},{9,8},{10,11... | collective-permute-start | bytes 301064 | tf_op jit(solution)/shard_map/ppermute | solution.py:63
  71.3 0.1 pad_maximum_fusion.3.refs_0_
  71.4 0.8 collective-permute-start.20
  72.2 0.1 pad_maximum_fusion.5.refs_4_
  72.4 0.1 pad_maximum_fusion.4.refs_2_
  72.5 2.2 %collective-permute-start.23 = (bf16[32,112,128]{2,1,0:T(8,128)(2,1)S(1)}, bf16[32,112,128]{2,1,0:T(8,128)(2,1)S(1)}, u32[]{:S(2)}, u32[]{:S(2)}) collective-permute-start(bf16[32,112,128]{2,1,0:T(8,128)(2,1)S(1)} %pad_maximum_fusion.5.refs_4_), channel_id=1, source_target_pairs={{0,64},{1,67},{2,66},{3,65},{4,68},{5,71},{6,70},{7,69},{8,72},{9,... | collective-permute-start | bytes 2752520 | tf_op jit(solution)/shard_map/ppermute | solution.py:53
  74.7 2.4 %collective-permute-done.24.refs_1_ = bf16[32,144,128]{2,1,0:T(8,128)(2,1)S(1)} collective-permute-done((bf16[32,144,128]{2,1,0:T(8,128)(2,1)S(1)}, bf16[32,144,128]{2,1,0:T(8,128)(2,1)S(1)}, u32[]{:S(2)}, u32[]{:S(2)}) %collective-permute-start.24) | collective-permute-done | bytes 1179680 | tf_op jit(solution)/shard_map/ppermute | solution.py:53
  77.2 2.5 %collective-permute-start.22 = (bf16[32,112,128]{2,1,0:T(8,128)(2,1)S(1)}, bf16[32,112,128]{2,1,0:T(8,128)(2,1)S(1)}, u32[]{:S(2)}, u32[]{:S(2)}) collective-permute-start(bf16[32,112,128]{2,1,0:T(8,128)(2,1)S(1)} %pad_maximum_fusion.4.refs_2_), channel_id=1, source_target_pairs={{0,4},{1,13},{2,6},{3,15},{4,0},{5,9},{6,2},{7,11},{8,12},{9,5},{1... | collective-permute-start | bytes 2752520 | tf_op jit(solution)/shard_map/ppermute | solution.py:53
  79.7 4.8 %shard_map.130 = (f32[1,3,56,3584]{3,2,1,0:T(8,128)}, f32[1,3,56,3584]{3,2,1,0:T(8,128)}, f32[1,3,56,3584]{3,2,1,0:T(8,128)}, f32[56,3584]{1,0:T(8,128)}, s32[8,128]{1,0:T(8,128)S(1)}) custom-call(s32[1]{0:T(128)S(6)} %copy.32.frag_ref, s32[3]{0:T(128)S(1)} %copy-done.8, f32[1,3,56,3584]{3,2,1,0:T(8,128)S(1)} %copy-done, ...), custom_call_target="tpu_custom_call" | custom-call | flops 12042240 | bytes 18063360 | tf_op jit(solution)/shard_map/pallas_call | solution.py:288
  84.5 11.3 %shard_map.131 = (bf16[512,3584]{1,0:T(8,128)(2,1)}, bf16[512,1024]{1,0:T(8,128)(2,1)S(1)}) custom-call(bf16[512,3584]{1,0:T(8,128)(2,1)S(1)} %copy-done.9, bf16[512,3584]{1,0:T(8,128)(2,1)S(1)} %collective-permute-done.4.after_ref.theirs_ref, bf16[32,144,128]{2,1,0:T(8,128)(2,1)S(1)} %pad_maximum_fusion.1.refs_0_, ...), custom_call_target="tpu_custom_call" | custom-call | flops 7516192768 | bytes 14680064 | tf_op jit(solution)/shard_map/pallas_call | solution.py:305
  95.9 4.1 %collective-permute-start.27 = (bf16[512,1024]{1,0:T(8,128)(2,1)S(1)}, bf16[512,1024]{1,0:T(8,128)(2,1)S(1)}, u32[]{:S(2)}, u32[]{:S(2)}) collective-permute-start(bf16[512,1024]{1,0:T(8,128)(2,1)S(1)} %get-tuple-element.39), channel_id=1, source_target_pairs={{0,1},{1,0},{2,3},{3,2},{4,5},{5,4},{6,7},{7,6},{8,9},{9,8},{10,11... | collective-permute-start | bytes 3145736 | tf_op jit(solution)/shard_map/ppermute | solution.py:63
  100.0 8.7 %shard_map.132 = (bf16[512,3584]{1,0:T(8,128)(2,1)}, bf16[512,768]{1,0:T(8,128)(2,1)S(1)}) custom-call(bf16[512,3584]{1,0:T(8,128)(2,1)S(1)} %copy-done.9, bf16[512,3584]{1,0:T(8,128)(2,1)S(1)} %collective-permute-done.4.after_ref.theirs_ref, bf16[32,112,128]{2,1,0:T(8,128)(2,1)S(1)} %pad_maximum_fusion.3.refs_0_, ...), custom_call_target="tpu_custom_call", output_to_operand_aliasing={{0}: (9, {})} | custom-call | flops 5637144576 | bytes 12845056 | tf_op jit(solution)/shard_map/pallas_call | solution.py:305
  108.7 0.1 collective-permute-start.28
  108.8 2.3 %collective-permute-done.28.refs_1_ = bf16[512,768]{1,0:T(8,128)(2,1)S(1)} collective-permute-done((bf16[512,768]{1,0:T(8,128)(2,1)S(1)}, bf16[512,768]{1,0:T(8,128)(2,1)S(1)}, u32[]{:S(2)}, u32[]{:S(2)}) %collective-permute-start.28) | collective-permute-done | bytes 786464 | tf_op jit(solution)/shard_map/ppermute | solution.py:63
  111.1 1.3 %shard_map.133 = bf16[512,3584]{1,0:T(8,128)(2,1)} custom-call(bf16[512,3584]{1,0:T(8,128)(2,1)} %get-tuple-element.38.buffer_ref, bf16[512,1024]{1,0:T(8,128)(2,1)S(1)} %collective-permute-done.27.refs_0_, bf16[512,768]{1,0:T(8,128)(2,1)S(1)} %collective-permute-done.28.refs_1_), custom_call_target="tpu_custom_call", output_to_operand_aliasing={{}: (0, {})} | custom-call | tf_op jit(solution)/shard_map/pallas_call | solution.py:384
  (75 shorter events, 1.3 us)
Async XLA Ops:
  0.6 12.7 %collective-permute-start.4 = (bf16[512,3584]{1,0:T(8,128)(2,1)}, bf16[512,3584]{1,0:T(8,128)(2,1)S(1)}, u32[]{:S(2)}, u32[]{:S(2)}) collective-permute-start(bf16[512,3584]{1,0:T(8,128)(2,1)} %mine_ref.3), channel_id=1, source_target_pairs={{0,1},{1,0},{2,3},{3,2},{4,5},{5,4},{6,7},{7,6},{8,9},{9,8},{10,11... | collective-permute-start | bytes 11010056 | tf_op jit(solution)/shard_map/ppermute | solution.py:63
  6.1 7.2 %collective-permute-start.3 = (f32[56,896]{1,0:T(8,128)}, f32[56,896]{1,0:T(8,128)S(1)}, u32[]{:S(2)}, u32[]{:S(2)}) collective-permute-start(f32[56,896]{1,0:T(8,128)} %get-tuple-element.26), channel_id=1, source_target_pairs={{0,1},{1,0},{2,3},{3,2},{4,5},{5,4},{6,7},{7,6},{8,9},{9,8},{10,11... | collective-permute-start | bytes 602120 | tf_op jit(solution)/shard_map/ppermute | solution.py:63
  6.2 4.3 %collective-permute-start = (bf16[56,896]{1,0:T(8,128)(2,1)}, bf16[56,896]{1,0:T(8,128)(2,1)S(1)}, u32[]{:S(2)}, u32[]{:S(2)}) collective-permute-start(bf16[56,896]{1,0:T(8,128)(2,1)} %get-tuple-element.23), channel_id=1, source_target_pairs={{0,64},{64,0},{1,65},{65,1},{2,66},{66,2},{3,67},{67,3},{4,68},{68... | collective-permute-start | bytes 301064 | tf_op jit(solution)/shard_map/ppermute | solution.py:336
  7.6 5.7 %collective-permute-start.1 = (bf16[56,896]{1,0:T(8,128)(2,1)}, bf16[56,896]{1,0:T(8,128)(2,1)S(1)}, u32[]{:S(2)}, u32[]{:S(2)}) collective-permute-start(bf16[56,896]{1,0:T(8,128)(2,1)} %get-tuple-element.24), channel_id=1, source_target_pairs={{0,65},{1,64},{64,1},{65,0},{2,67},{3,66},{66,3},{67,2},{4,69},{5,... | collective-permute-start | bytes 301064 | tf_op jit(solution)/shard_map/ppermute | solution.py:337
  13.3 0.9 copy-start.6
  14.3 0.9 copy-start.7
  15.5 11.8 %collective-permute-start.7 = (bf16[1,256,128]{2,1,0:T(8,128)(2,1)S(1)}, bf16[1,256,128]{2,1,0:T(8,128)(2,1)S(1)}, u32[]{:S(2)}, u32[]{:S(2)}) collective-permute-start(bf16[1,256,128]{2,1,0:T(8,128)(2,1)S(1)} %get-tuple-element.29), channel_id=1, source_target_pairs={{0,16},{1,49},{2,18},{3,51},{4,20},{5,53},{6,22},{7,55},{8,24},{9,... | collective-permute-start | bytes 196616 | tf_op jit(solution)/shard_map/ppermute | solution.py:53
  19.3 7.9 %collective-permute-start.6 = (bf16[1,272,128]{2,1,0:T(8,128)(2,1)S(1)}, bf16[1,272,128]{2,1,0:T(8,128)(2,1)S(1)}, u32[]{:S(2)}, u32[]{:S(2)}) collective-permute-start(bf16[1,272,128]{2,1,0:T(8,128)(2,1)S(1)} %get-tuple-element.30), channel_id=1, source_target_pairs={{0,64},{1,67},{2,66},{3,65},{4,68},{5,71},{6,70},{7,69},{8,72},{9,... | collective-permute-start | bytes 208904 | tf_op jit(solution)/shard_map/ppermute | solution.py:53
  22.1 12.3 %collective-permute-start.5 = (bf16[896,128]{1,0:T(8,128)(2,1)S(1)}, bf16[896,128]{1,0:T(8,128)(2,1)S(1)}, u32[]{:S(2)}, u32[]{:S(2)}) collective-permute-start(bf16[896,128]{1,0:T(8,128)(2,1)S(1)} %get-tuple-element.28), channel_id=1, source_target_pairs={{0,64},{64,0},{1,65},{65,1},{2,66},{66,2},{3,67},{67,3},{4,68},{68... | collective-permute-start | bytes 688136 | tf_op jit(solution)/shard_map/ppermute | solution.py:348
  22.1 4.4 %collective-permute-start.8 = (bf16[1,256,128]{2,1,0:T(8,128)(2,1)S(1)}, bf16[1,256,128]{2,1,0:T(8,128)(2,1)S(1)}, u32[]{:S(2)}, u32[]{:S(2)}) collective-permute-start(bf16[1,256,128]{2,1,0:T(8,128)(2,1)S(1)} %get-tuple-element.31), channel_id=1, source_target_pairs={{0,4},{1,13},{2,6},{3,15},{4,0},{5,9},{6,2},{7,11},{8,12},{9,5},{1... | collective-permute-start | bytes 196616 | tf_op jit(solution)/shard_map/ppermute | solution.py:53
  26.6 5.1 %collective-permute-start.11 = (bf16[2,256,128]{2,1,0:T(8,128)(2,1)S(1)}, bf16[2,256,128]{2,1,0:T(8,128)(2,1)S(1)}, u32[]{:S(2)}, u32[]{:S(2)}) collective-permute-start(bf16[2,256,128]{2,1,0:T(8,128)(2,1)S(1)} %pad_maximum_fusion.14), channel_id=1, source_target_pairs={{0,64},{1,67},{2,66},{3,65},{4,68},{5,71},{6,70},{7,69},{8,72},{9,... | collective-permute-start | bytes 393224 | tf_op jit(solution)/shard_map/ppermute | solution.py:53
  27.4 7.1 %collective-permute-start.10 = (bf16[2,256,128]{2,1,0:T(8,128)(2,1)S(1)}, bf16[2,256,128]{2,1,0:T(8,128)(2,1)S(1)}, u32[]{:S(2)}, u32[]{:S(2)}) collective-permute-start(bf16[2,256,128]{2,1,0:T(8,128)(2,1)S(1)} %pad_maximum_fusion.13), channel_id=1, source_target_pairs={{0,12},{1,5},{2,14},{3,7},{4,8},{5,1},{6,10},{7,3},{8,4},{9,13},{1... | collective-permute-start | bytes 393224 | tf_op jit(solution)/shard_map/ppermute | solution.py:53
  27.8 5.2 %collective-permute-start.9 = (bf16[2,272,128]{2,1,0:T(8,128)(2,1)S(1)}, bf16[2,272,128]{2,1,0:T(8,128)(2,1)S(1)}, u32[]{:S(2)}, u32[]{:S(2)}) collective-permute-start(bf16[2,272,128]{2,1,0:T(8,128)(2,1)S(1)} %pad_maximum_fusion.12), channel_id=1, source_target_pairs={{0,16},{1,49},{2,18},{3,51},{4,20},{5,53},{6,22},{7,55},{8,24},{9,... | collective-permute-start | bytes 417800 | tf_op jit(solution)/shard_map/ppermute | solution.py:53
  31.9 6.8 %collective-permute-start.14 = (bf16[4,256,128]{2,1,0:T(8,128)(2,1)S(1)}, bf16[4,256,128]{2,1,0:T(8,128)(2,1)S(1)}, u32[]{:S(2)}, u32[]{:S(2)}) collective-permute-start(bf16[4,256,128]{2,1,0:T(8,128)(2,1)S(1)} %pad_maximum_fusion.11), channel_id=1, source_target_pairs={{0,16},{1,49},{2,18},{3,51},{4,20},{5,53},{6,22},{7,55},{8,24},{9,... | collective-permute-start | bytes 786440 | tf_op jit(solution)/shard_map/ppermute | solution.py:53
  33.1 5.9 %collective-permute-start.12 = (bf16[4,272,128]{2,1,0:T(8,128)(2,1)S(1)}, bf16[4,272,128]{2,1,0:T(8,128)(2,1)S(1)}, u32[]{:S(2)}, u32[]{:S(2)}) collective-permute-start(bf16[4,272,128]{2,1,0:T(8,128)(2,1)S(1)} %pad_maximum_fusion.9), channel_id=1, source_target_pairs={{0,12},{1,5},{2,14},{3,7},{4,8},{5,1},{6,10},{7,3},{8,4},{9,13},{1... | collective-permute-start | bytes 835592 | tf_op jit(solution)/shard_map/ppermute | solution.py:53
  34.5 5.6 %collective-permute-start.13 = (bf16[4,256,128]{2,1,0:T(8,128)(2,1)S(1)}, bf16[4,256,128]{2,1,0:T(8,128)(2,1)S(1)}, u32[]{:S(2)}, u32[]{:S(2)}) collective-permute-start(bf16[4,256,128]{2,1,0:T(8,128)(2,1)S(1)} %pad_maximum_fusion.10), channel_id=1, source_target_pairs={{0,66},{1,65},{2,64},{3,67},{4,70},{5,69},{6,68},{7,71},{8,74},{9,... | collective-permute-start | bytes 786440 | tf_op jit(solution)/shard_map/ppermute | solution.py:53
  38.9 8.4 %collective-permute-start.18 = (bf16[8,256,128]{2,1,0:T(8,128)(2,1)S(1)}, bf16[8,256,128]{2,1,0:T(8,128)(2,1)S(1)}, u32[]{:S(2)}, u32[]{:S(2)}) collective-permute-start(bf16[8,256,128]{2,1,0:T(8,128)(2,1)S(1)} %pad_maximum_fusion.8), channel_id=1, source_target_pairs={{0,12},{1,5},{2,14},{3,7},{4,8},{5,1},{6,10},{7,3},{8,4},{9,13},{1... | collective-permute-start | bytes 1572872 | tf_op jit(solution)/shard_map/ppermute | solution.py:53
  39.2 8.8 %collective-permute-start.15 = (bf16[8,272,128]{2,1,0:T(8,128)(2,1)S(1)}, bf16[8,272,128]{2,1,0:T(8,128)(2,1)S(1)}, u32[]{:S(2)}, u32[]{:S(2)}) collective-permute-start(bf16[8,272,128]{2,1,0:T(8,128)(2,1)S(1)} %pad_maximum_fusion.6), channel_id=1, source_target_pairs={{0,66},{1,65},{2,64},{3,67},{4,70},{5,69},{6,68},{7,71},{8,74},{9,... | collective-permute-start | bytes 1671176 | tf_op jit(solution)/shard_map/ppermute | solution.py:53
  40.3 8.4 %collective-permute-start.16 = (bf16[8,256,128]{2,1,0:T(8,128)(2,1)S(1)}, bf16[8,256,128]{2,1,0:T(8,128)(2,1)S(1)}, u32[]{:S(2)}, u32[]{:S(2)}) collective-permute-start(bf16[8,256,128]{2,1,0:T(8,128)(2,1)S(1)} %pad_maximum_fusion.7), channel_id=1, source_target_pairs={{0,48},{1,17},{2,50},{3,19},{4,52},{5,21},{6,54},{7,23},{8,56},{9,... | collective-permute-start | bytes 1572872 | tf_op jit(solution)/shard_map/ppermute | solution.py:53
  47.5 14.0 %collective-permute-start.19 = (bf16[16,256,128]{2,1,0:T(8,128)(2,1)S(1)}, bf16[16,256,128]{2,1,0:T(8,128)(2,1)S(1)}, u32[]{:S(2)}, u32[]{:S(2)}) collective-permute-start(bf16[16,256,128]{2,1,0:T(8,128)(2,1)S(1)} %select_dynamic-update-slice_fusion.1), channel_id=1, source_target_pairs={{0,66},{1,65},{2,64},{3,67},{4,70},{5,69},{6,68},{7,71},{8,74},{9,... | collective-permute-start | bytes 3145736 | tf_op jit(solution)/shard_map/ppermute | solution.py:53
  48.3 15.9 %collective-permute-start.21 = (bf16[16,272,128]{2,1,0:T(8,128)(2,1)S(1)}, bf16[16,272,128]{2,1,0:T(8,128)(2,1)S(1)}, u32[]{:S(2)}, u32[]{:S(2)}) collective-permute-start(bf16[16,272,128]{2,1,0:T(8,128)(2,1)S(1)} %select_dynamic-update-slice_fusion), channel_id=1, source_target_pairs={{0,48},{1,17},{2,50},{3,19},{4,52},{5,21},{6,54},{7,23},{8,56},{9,... | collective-permute-start | bytes 3342344 | tf_op jit(solution)/shard_map/ppermute | solution.py:53
  48.9 15.2 %collective-permute-start.17 = (bf16[16,256,128]{2,1,0:T(8,128)(2,1)S(1)}, bf16[16,256,128]{2,1,0:T(8,128)(2,1)S(1)}, u32[]{:S(2)}, u32[]{:S(2)}) collective-permute-start(bf16[16,256,128]{2,1,0:T(8,128)(2,1)S(1)} %select_dynamic-update-slice_fusion.2), channel_id=1, source_target_pairs={{0,4},{1,13},{2,6},{3,15},{4,0},{5,9},{6,2},{7,11},{8,12},{9,5},{1... | collective-permute-start | bytes 3145736 | tf_op jit(solution)/shard_map/ppermute | solution.py:53
  61.7 15.4 %collective-permute-start.24 = (bf16[32,144,128]{2,1,0:T(8,128)(2,1)S(1)}, bf16[32,144,128]{2,1,0:T(8,128)(2,1)S(1)}, u32[]{:S(2)}, u32[]{:S(2)}) collective-permute-start(bf16[32,144,128]{2,1,0:T(8,128)(2,1)S(1)} %pad_maximum_fusion.1.refs_0_), channel_id=1, source_target_pairs={{0,48},{1,17},{2,50},{3,19},{4,52},{5,21},{6,54},{7,23},{8,56},{9,... | collective-permute-start | bytes 3538952 | tf_op jit(solution)/shard_map/ppermute | solution.py:53
  64.4 20.1 %collective-permute-start.25 = (bf16[32,160,128]{2,1,0:T(8,128)(2,1)S(1)}, bf16[32,160,128]{2,1,0:T(8,128)(2,1)S(1)}, u32[]{:S(2)}, u32[]{:S(2)}) collective-permute-start(bf16[32,160,128]{2,1,0:T(8,128)(2,1)S(1)} %pad_maximum_fusion.refs_2_), channel_id=1, source_target_pairs={{0,4},{1,13},{2,6},{3,15},{4,0},{5,9},{6,2},{7,11},{8,12},{9,5},{1... | collective-permute-start | bytes 3932168 | tf_op jit(solution)/shard_map/ppermute | solution.py:53
  67.1 17.5 %collective-permute-start.26 = (bf16[32,144,128]{2,1,0:T(8,128)(2,1)S(1)}, bf16[32,144,128]{2,1,0:T(8,128)(2,1)S(1)}, u32[]{:S(2)}, u32[]{:S(2)}) collective-permute-start(bf16[32,144,128]{2,1,0:T(8,128)(2,1)S(1)} %pad_maximum_fusion.2.refs_4_), channel_id=1, source_target_pairs={{0,64},{1,67},{2,66},{3,65},{4,68},{5,71},{6,70},{7,69},{8,72},{9,... | collective-permute-start | bytes 3538952 | tf_op jit(solution)/shard_map/ppermute | solution.py:53
  69.3 3.2 %collective-permute-start.2 = (bf16[56,896]{1,0:T(8,128)(2,1)S(1)}, bf16[56,896]{1,0:T(8,128)(2,1)S(1)}, u32[]{:S(2)}, u32[]{:S(2)}) collective-permute-start(bf16[56,896]{1,0:T(8,128)(2,1)S(1)} %collective-permute-done.1.cross_ref), channel_id=1, source_target_pairs={{0,1},{1,0},{2,3},{3,2},{4,5},{5,4},{6,7},{7,6},{8,9},{9,8},{10,11... | collective-permute-start | bytes 301064 | tf_op jit(solution)/shard_map/ppermute | solution.py:63
  71.1 8.5 %copy-start.5 = (bf16[1,3,56,3584]{3,2,1,0:T(8,128)(2,1)S(1)}, bf16[1,3,56,3584]{3,2,1,0:T(8,128)(2,1)}, u32[]{:S(2)}) copy-start(bf16[1,3,56,3584]{3,2,1,0:T(8,128)(2,1)} %g_ref.1) | copy-start | bytes 3612676
  71.2 8.5 %copy-start.4 = (f32[1,3,56,3584]{3,2,1,0:T(8,128)S(1)}, f32[1,3,56,3584]{3,2,1,0:T(8,128)}, u32[]{:S(2)}) copy-start(f32[1,3,56,3584]{3,2,1,0:T(8,128)} %v_ref.1) | copy-start | bytes 7225348
  71.3 8.4 %copy-start.3 = (f32[1,3,56,3584]{3,2,1,0:T(8,128)S(1)}, f32[1,3,56,3584]{3,2,1,0:T(8,128)}, u32[]{:S(2)}) copy-start(f32[1,3,56,3584]{3,2,1,0:T(8,128)} %m_ref.1) | copy-start | bytes 7225348
  71.4 28.6 %collective-permute-start.20 = (bf16[32,112,128]{2,1,0:T(8,128)(2,1)S(1)}, bf16[32,112,128]{2,1,0:T(8,128)(2,1)S(1)}, u32[]{:S(2)}, u32[]{:S(2)}) collective-permute-start(bf16[32,112,128]{2,1,0:T(8,128)(2,1)S(1)} %pad_maximum_fusion.3.refs_0_), channel_id=1, source_target_pairs={{0,48},{1,17},{2,50},{3,19},{4,52},{5,21},{6,54},{7,23},{8,56},{9,... | collective-permute-start | bytes 2752520 | tf_op jit(solution)/shard_map/ppermute | solution.py:53
  72.2 7.4 %copy-start.1 = (f32[56,3584]{1,0:T(8,128)S(1)}, f32[56,3584]{1,0:T(8,128)}, u32[]{:S(2)}) copy-start(f32[56,3584]{1,0:T(8,128)} %anchor_ref.3) | copy-start | bytes 2408452
  72.2 7.4 %copy-start.2 = (f32[56,3584]{1,0:T(8,128)S(1)}, f32[56,3584]{1,0:T(8,128)}, u32[]{:S(2)}) copy-start(f32[56,3584]{1,0:T(8,128)} %momentum_ref.3) | copy-start | bytes 2408452
  72.3 7.3 %copy-start = (f32[1,3,56,3584]{3,2,1,0:T(8,128)S(1)}, f32[1,3,56,3584]{3,2,1,0:T(8,128)}, u32[]{:S(2)}) copy-start(f32[1,3,56,3584]{3,2,1,0:T(8,128)} %p_ref.1) | copy-start | bytes 7225348
  72.3 7.3 %copy-start.8 = (s32[3]{0:T(128)S(1)}, s32[3]{0:T(128)}, u32[]{:S(2)}) copy-start(s32[3]{0:T(128)} %plan_ref.3) | copy-start | bytes 40
  72.5 12.1 %copy-start.9 = (bf16[512,3584]{1,0:T(8,128)(2,1)S(1)}, bf16[512,3584]{1,0:T(8,128)(2,1)}, u32[]{:S(2)}) copy-start(bf16[512,3584]{1,0:T(8,128)(2,1)} %mine_ref.3) | copy-start | bytes 11010052
  72.5 27.5 %collective-permute-start.23 = (bf16[32,112,128]{2,1,0:T(8,128)(2,1)S(1)}, bf16[32,112,128]{2,1,0:T(8,128)(2,1)S(1)}, u32[]{:S(2)}, u32[]{:S(2)}) collective-permute-start(bf16[32,112,128]{2,1,0:T(8,128)(2,1)S(1)} %pad_maximum_fusion.5.refs_4_), channel_id=1, source_target_pairs={{0,64},{1,67},{2,66},{3,65},{4,68},{5,71},{6,70},{7,69},{8,72},{9,... | collective-permute-start | bytes 2752520 | tf_op jit(solution)/shard_map/ppermute | solution.py:53
  77.2 22.8 %collective-permute-start.22 = (bf16[32,112,128]{2,1,0:T(8,128)(2,1)S(1)}, bf16[32,112,128]{2,1,0:T(8,128)(2,1)S(1)}, u32[]{:S(2)}, u32[]{:S(2)}) collective-permute-start(bf16[32,112,128]{2,1,0:T(8,128)(2,1)S(1)} %pad_maximum_fusion.4.refs_2_), channel_id=1, source_target_pairs={{0,4},{1,13},{2,6},{3,15},{4,0},{5,9},{6,2},{7,11},{8,12},{9,5},{1... | collective-permute-start | bytes 2752520 | tf_op jit(solution)/shard_map/ppermute | solution.py:53
  95.9 15.2 %collective-permute-start.27 = (bf16[512,1024]{1,0:T(8,128)(2,1)S(1)}, bf16[512,1024]{1,0:T(8,128)(2,1)S(1)}, u32[]{:S(2)}, u32[]{:S(2)}) collective-permute-start(bf16[512,1024]{1,0:T(8,128)(2,1)S(1)} %get-tuple-element.39), channel_id=1, source_target_pairs={{0,1},{1,0},{2,3},{3,2},{4,5},{5,4},{6,7},{7,6},{8,9},{9,8},{10,11... | collective-permute-start | bytes 3145736 | tf_op jit(solution)/shard_map/ppermute | solution.py:63
  108.7 2.4 %collective-permute-start.28 = (bf16[512,768]{1,0:T(8,128)(2,1)S(1)}, bf16[512,768]{1,0:T(8,128)(2,1)S(1)}, u32[]{:S(2)}, u32[]{:S(2)}) collective-permute-start(bf16[512,768]{1,0:T(8,128)(2,1)S(1)} %get-tuple-element.40), channel_id=1, source_target_pairs={{0,1},{1,0},{2,3},{3,2},{4,5},{5,4},{6,7},{7,6},{8,9},{9,8},{10,11... | collective-permute-start | bytes 2359304 | tf_op jit(solution)/shard_map/ppermute | solution.py:63

commit v5 on v4

--- a/solution.py
+++ b/solution.py
@@ -209,7 +209,7 @@
         for q in (tile % GROUPS,) if tile < 2 * GROUPS else range(GROUPS):
             size = CHIP if tile < 2 * GROUPS else SHARE[q]
             masks = [code_masks(q, c) for c in (0, 1)]
-            at = 0 if tile < 2 * GROUPS else CHIP
+            at = SHARE[tile % GROUPS] if GROUPS <= tile < 2 * GROUPS else 0
             for r in range(64):
                 code = here ^ jnp.where(core == 0, masks[0][r], masks[1][r])
                 pltpu.make_async_copy(
@@ -239,7 +239,7 @@
     pltpu.make_async_copy(staged.at[1], staged.at[1], result_sem).wait()
 
 
-TILES = ((0, 1, 2, 6), (3, 4, 5))
+TILES = ((0, 1, 2), (3, 4, 5, 6))
 
 
 def place_kernel(buffer_ref, *refs):
@@ -369,7 +369,7 @@
     fifth = [exchange(cur[q], q, 4) for q in range(GROUPS)]
     both = [
         [jnp.concatenate([cur[q][:, rows(q)], fifth[q][:, rows(q)]], axis=0) for q in range(GROUPS)]
-        for rows in (lambda q: slice(0, CHIP + SHARE[q]), lambda q: slice(CHIP + SHARE[q], None))
+        for rows in (lambda q: slice(0, CHIP), lambda q: slice(CHIP, None))
     ]
     params_out, first_out, second_out, momentum_out, done = layers_call(
         (frag_index, plan), (inner_params, inner_grads, adam_first, adam_second), (anchor, momentum), (same, swap_cores(cross)),

time: 113 us -> 113 us (level)
  waiting for transfers between devices: 39.3 us -> 43.6 us
  starting transfers between devices: 36.5 us -> 32.8 us
    ppermute x21, starting transfers between devices: 26.8 us -> 22.8 us  [exchange(): lax.ppermute(value, ALL, [(i, flipped(i, flips[i % 2])) for i in range(12...]
    ppermute x21, waiting for transfers between devices: 32.1 us -> 35.4 us  [exchange(): lax.ppermute(value, ALL, [(i, flipped(i, flips[i % 2])) for i in range(12...]
  transfers between devices with their start and end apart: 29 -> 29, of which waited for: 13 -> 14; matrix products, arithmetic and copies ran while one was open for 3% -> 3% of each run, Pallas kernels for 25% -> 15%
where the time goes in v5:
time: 113 us
  waiting for transfers between devices  43.6 us (39%)
  starting transfers between devices  32.8 us (29%)
  Pallas kernels  29.8 us (26%)
  other arithmetic  2.45 us (2%)
  local copies, waits for them, and re-layouts  2.4 us (2%)
  between operations  2 us (2%)
    ppermute x21, waiting for transfers between devices, exchange(): lax.ppermute(value, ALL, [(i, flipped(i, flips[i % 2])) for i in range(12...  35.4 us
    ppermute x21, starting transfers between devices, exchange(): lax.ppermute(value, ALL, [(i, flipped(i, flips[i % 2])) for i in range(12...  22.8 us
    pallas_call x2, Pallas kernels, multiply_call(): pl.pallas_call(functools.partial(multiply_kernel, tiles, buffer is not No...  20 us
    ppermute x5, starting transfers between devices, swap_cores(): return lax.ppermute(value, 'core', [(0, 1), (1, 0)])  7.91 us
    pallas_call x1, Pallas kernels, layers_call(): pl.pallas_call(layers_kernel, grid_spec=pltpu.PrefetchScalarGridSpec(num_...  4.86 us
    pallas_call x1, Pallas kernels, body(): pl.pallas_call(first_kernel, in_specs=[SMEM] * 2 + [ANY] * 3, out_specs=[...  3.3 us
    ppermute x5, waiting for transfers between devices, swap_cores(): return lax.ppermute(value, 'core', [(0, 1), (1, 0)])  3.28 us
    ppermute x1, waiting for transfers between devices, body(): lax.ppermute(send_cross, ('yl', 'core'), [(i, 3 - i) for i in range(4)])  2.83 us
  transfers between devices with their start and end apart: 29, of which 14 were waited for; matrix products, arithmetic and copies ran while one was open for 3% of the time, Pallas kernels for 15%

profile of v5, /device:TPU:1, one launch (start us, length us, event | category | flops | bytes accessed | tf_op | source)
XLA Modules:
  0.0 113.1 jit_solution(12991634845607956690)
XLA Ops:
  0.6 1.5 %collective-permute-start.4 = (bf16[512,3584]{1,0:T(8,128)(2,1)}, bf16[512,3584]{1,0:T(8,128)(2,1)S(1)}, u32[]{:S(2)}, u32[]{:S(2)}) collective-permute-start(bf16[512,3584]{1,0:T(8,128)(2,1)} %mine_ref.3), channel_id=1, source_target_pairs={{0,1},{1,0},{2,3},{3,2},{4,5},{5,4},{6,7},{7,6},{8,9},{9,8},{10,11... | collective-permute-start | bytes 11010056 | tf_op jit(solution)/shard_map/ppermute | solution.py:63
  2.8 3.3 %shard_map.128 = (bf16[56,896]{1,0:T(8,128)(2,1)}, bf16[56,896]{1,0:T(8,128)(2,1)}, f32[56,896]{1,0:T(8,128)}, f32[56,896]{1,0:T(8,128)}, bf16[896,128]{1,0:T(8,128)(2,1)}) custom-call(s32[1]{0:T(128)S(6)} %copy.32.frag_ref, s32[3]{0:T(128)} %plan_ref.3, f32[56,3584]{1,0:T(8,128)} %anchor_ref.3, f32[56,3584]{1,0:T(8,128)} %momentum_ref.3, ...), custom_call_target="tpu_custom_call" | custom-call | tf_op jit(solution)/shard_map/pallas_call | solution.py:328
  6.1 0.1 collective-permute-start.3
  6.2 1.5 %collective-permute-start = (bf16[56,896]{1,0:T(8,128)(2,1)}, bf16[56,896]{1,0:T(8,128)(2,1)S(1)}, u32[]{:S(2)}, u32[]{:S(2)}) collective-permute-start(bf16[56,896]{1,0:T(8,128)(2,1)} %get-tuple-element.23), channel_id=1, source_target_pairs={{0,64},{64,0},{1,65},{65,1},{2,66},{66,2},{3,67},{67,3},{4,68},{68... | collective-permute-start | bytes 301064 | tf_op jit(solution)/shard_map/ppermute | solution.py:336
  7.6 0.7 collective-permute-start.1
  8.3 2.1 %collective-permute-done.same_ref = bf16[56,896]{1,0:T(8,128)(2,1)S(1)} collective-permute-done((bf16[56,896]{1,0:T(8,128)(2,1)}, bf16[56,896]{1,0:T(8,128)(2,1)S(1)}, u32[]{:S(2)}, u32[]{:S(2)}) %collective-permute-start) | collective-permute-done | bytes 100384 | tf_op jit(solution)/shard_map/ppermute | solution.py:336
  10.5 2.8 %collective-permute-done.1.cross_ref = bf16[56,896]{1,0:T(8,128)(2,1)S(1)} collective-permute-done((bf16[56,896]{1,0:T(8,128)(2,1)}, bf16[56,896]{1,0:T(8,128)(2,1)S(1)}, u32[]{:S(2)}, u32[]{:S(2)}) %collective-permute-start.1) | collective-permute-done | bytes 100384 | tf_op jit(solution)/shard_map/ppermute | solution.py:337
  13.3 0.9 copy-done.8
  14.3 0.9 copy-done.9
  15.2 0.3 shard_map.129
  15.5 2.5 %collective-permute-start.8 = (bf16[1,256,128]{2,1,0:T(8,128)(2,1)S(1)}, bf16[1,256,128]{2,1,0:T(8,128)(2,1)S(1)}, u32[]{:S(2)}, u32[]{:S(2)}) collective-permute-start(bf16[1,256,128]{2,1,0:T(8,128)(2,1)S(1)} %get-tuple-element.31), channel_id=1, source_target_pairs={{0,4},{1,13},{2,6},{3,15},{4,0},{5,9},{6,2},{7,11},{8,12},{9,5},{1... | collective-permute-start | bytes 196616 | tf_op jit(solution)/shard_map/ppermute | solution.py:53
  18.1 2.7 %collective-permute-start.6 = (bf16[1,272,128]{2,1,0:T(8,128)(2,1)S(1)}, bf16[1,272,128]{2,1,0:T(8,128)(2,1)S(1)}, u32[]{:S(2)}, u32[]{:S(2)}) collective-permute-start(bf16[1,272,128]{2,1,0:T(8,128)(2,1)S(1)} %get-tuple-element.30), channel_id=1, source_target_pairs={{0,64},{1,67},{2,66},{3,65},{4,68},{5,71},{6,70},{7,69},{8,72},{9,... | collective-permute-start | bytes 208904 | tf_op jit(solution)/shard_map/ppermute | solution.py:53
  20.8 3.8 %collective-permute-start.7 = (bf16[1,256,128]{2,1,0:T(8,128)(2,1)S(1)}, bf16[1,256,128]{2,1,0:T(8,128)(2,1)S(1)}, u32[]{:S(2)}, u32[]{:S(2)}) collective-permute-start(bf16[1,256,128]{2,1,0:T(8,128)(2,1)S(1)} %get-tuple-element.29), channel_id=1, source_target_pairs={{0,16},{1,49},{2,18},{3,51},{4,20},{5,53},{6,22},{7,55},{8,24},{9,... | collective-permute-start | bytes 196616 | tf_op jit(solution)/shard_map/ppermute | solution.py:53
  24.6 0.1 constant_dynamic-update-slice_fusion.6
  24.8 0.6 collective-permute-start.11
  25.5 1.3 %collective-permute-start.9 = (bf16[2,272,128]{2,1,0:T(8,128)(2,1)S(1)}, bf16[2,272,128]{2,1,0:T(8,128)(2,1)S(1)}, u32[]{:S(2)}, u32[]{:S(2)}) collective-permute-start(bf16[2,272,128]{2,1,0:T(8,128)(2,1)S(1)} %pad_maximum_fusion.12), channel_id=1, source_target_pairs={{0,16},{1,49},{2,18},{3,51},{4,20},{5,53},{6,22},{7,55},{8,24},{9,... | collective-permute-start | bytes 417800 | tf_op jit(solution)/shard_map/ppermute | solution.py:53
  26.9 0.4 collective-permute-start.10
  27.3 2.6 %collective-permute-done.11 = bf16[2,256,128]{2,1,0:T(8,128)(2,1)S(1)} collective-permute-done((bf16[2,256,128]{2,1,0:T(8,128)(2,1)S(1)}, bf16[2,256,128]{2,1,0:T(8,128)(2,1)S(1)}, u32[]{:S(2)}, u32[]{:S(2)}) %collective-permute-start.11) | collective-permute-done | bytes 131104 | tf_op jit(solution)/shard_map/ppermute | solution.py:53
  30.0 0.1 collective-permute-start.14
  30.1 0.6 collective-permute-done.9
  30.7 0.1 constant_dynamic-update-slice_fusion.9
  30.8 0.2 collective-permute-start.12
  31.2 1.5 %collective-permute-start.13 = (bf16[4,256,128]{2,1,0:T(8,128)(2,1)S(1)}, bf16[4,256,128]{2,1,0:T(8,128)(2,1)S(1)}, u32[]{:S(2)}, u32[]{:S(2)}) collective-permute-start(bf16[4,256,128]{2,1,0:T(8,128)(2,1)S(1)} %pad_maximum_fusion.10), channel_id=1, source_target_pairs={{0,66},{1,65},{2,64},{3,67},{4,70},{5,69},{6,68},{7,71},{8,74},{9,... | collective-permute-start | bytes 786440 | tf_op jit(solution)/shard_map/ppermute | solution.py:53
  32.7 4.1 %collective-permute-done.14 = bf16[4,256,128]{2,1,0:T(8,128)(2,1)S(1)} collective-permute-done((bf16[4,256,128]{2,1,0:T(8,128)(2,1)S(1)}, bf16[4,256,128]{2,1,0:T(8,128)(2,1)S(1)}, u32[]{:S(2)}, u32[]{:S(2)}) %collective-permute-start.14) | collective-permute-done | bytes 262176 | tf_op jit(solution)/shard_map/ppermute | solution.py:53
  36.8 0.1 constant_dynamic-update-slice_fusion.4
  37.0 0.1 collective-permute-start.18
  37.1 0.1 constant_dynamic-update-slice_fusion.8
  37.3 0.5 collective-permute-start.15
  37.9 0.1 constant_dynamic-update-slice_fusion
  38.1 0.1 collective-permute-start.16
  38.2 7.2 %collective-permute-done.18 = bf16[8,256,128]{2,1,0:T(8,128)(2,1)S(1)} collective-permute-done((bf16[8,256,128]{2,1,0:T(8,128)(2,1)S(1)}, bf16[8,256,128]{2,1,0:T(8,128)(2,1)S(1)}, u32[]{:S(2)}, u32[]{:S(2)}) %collective-permute-start.18) | collective-permute-done | bytes 524320 | tf_op jit(solution)/shard_map/ppermute | solution.py:53
  45.4 0.2 select_dynamic-update-slice_fusion.1
  45.6 0.5 collective-permute-start.19
  46.2 0.3 collective-permute-done.16
  46.5 0.2 select_dynamic-update-slice_fusion.2
  46.7 1.4 %collective-permute-start.17 = (bf16[16,256,128]{2,1,0:T(8,128)(2,1)S(1)}, bf16[16,256,128]{2,1,0:T(8,128)(2,1)S(1)}, u32[]{:S(2)}, u32[]{:S(2)}) collective-permute-start(bf16[16,256,128]{2,1,0:T(8,128)(2,1)S(1)} %select_dynamic-update-slice_fusion.2), channel_id=1, source_target_pairs={{0,4},{1,13},{2,6},{3,15},{4,0},{5,9},{6,2},{7,11},{8,12},{9,5},{1... | collective-permute-start | bytes 3145736 | tf_op jit(solution)/shard_map/ppermute | solution.py:53
  48.1 0.2 select_dynamic-update-slice_fusion
  48.3 0.1 collective-permute-start.21
  48.4 11.2 %collective-permute-done.19 = bf16[16,256,128]{2,1,0:T(8,128)(2,1)S(1)} collective-permute-done((bf16[16,256,128]{2,1,0:T(8,128)(2,1)S(1)}, bf16[16,256,128]{2,1,0:T(8,128)(2,1)S(1)}, u32[]{:S(2)}, u32[]{:S(2)}) %collective-permute-start.19) | collective-permute-done | bytes 1048608 | tf_op jit(solution)/shard_map/ppermute | solution.py:53
  59.7 0.1 pad_maximum_fusion.3.refs_0_
  59.8 0.1 collective-permute-start.24
  59.9 5.7 %collective-permute-start.2 = (bf16[56,896]{1,0:T(8,128)(2,1)S(1)}, bf16[56,896]{1,0:T(8,128)(2,1)S(1)}, u32[]{:S(2)}, u32[]{:S(2)}) collective-permute-start(bf16[56,896]{1,0:T(8,128)(2,1)S(1)} %collective-permute-done.1.cross_ref), channel_id=1, source_target_pairs={{0,1},{1,0},{2,3},{3,2},{4,5},{5,4},{6,7},{7,6},{8,9},{9,8},{10,11... | collective-permute-start | bytes 301064 | tf_op jit(solution)/shard_map/ppermute | solution.py:63
  65.9 0.1 pad_maximum_fusion.1.refs_0_
  66.1 0.1 pad_maximum_fusion.5.refs_4_
  66.2 2.6 %collective-permute-start.26 = (bf16[32,112,128]{2,1,0:T(8,128)(2,1)S(1)}, bf16[32,112,128]{2,1,0:T(8,128)(2,1)S(1)}, u32[]{:S(2)}, u32[]{:S(2)}) collective-permute-start(bf16[32,112,128]{2,1,0:T(8,128)(2,1)S(1)} %pad_maximum_fusion.5.refs_4_), channel_id=1, source_target_pairs={{0,64},{1,67},{2,66},{3,65},{4,68},{5,71},{6,70},{7,69},{8,72},{9,... | collective-permute-start | bytes 2752520 | tf_op jit(solution)/shard_map/ppermute | solution.py:53
  68.8 0.1 pad_maximum_fusion.4.refs_2_
  68.9 1.0 collective-permute-start.25
  70.0 0.1 pad_maximum_fusion.refs_2_
  70.1 1.8 %collective-permute-start.22 = (bf16[32,160,128]{2,1,0:T(8,128)(2,1)S(1)}, bf16[32,160,128]{2,1,0:T(8,128)(2,1)S(1)}, u32[]{:S(2)}, u32[]{:S(2)}) collective-permute-start(bf16[32,160,128]{2,1,0:T(8,128)(2,1)S(1)} %pad_maximum_fusion.refs_2_), channel_id=1, source_target_pairs={{0,4},{1,13},{2,6},{3,15},{4,0},{5,9},{6,2},{7,11},{8,12},{9,5},{1... | collective-permute-start | bytes 3932168 | tf_op jit(solution)/shard_map/ppermute | solution.py:53
  71.9 0.1 pad_maximum_fusion.2.refs_4_
  72.1 0.1 collective-permute-start.20
  72.2 0.7 collective-permute-done.24.refs_1_
  72.9 1.4 %collective-permute-start.23 = (bf16[32,144,128]{2,1,0:T(8,128)(2,1)S(1)}, bf16[32,144,128]{2,1,0:T(8,128)(2,1)S(1)}, u32[]{:S(2)}, u32[]{:S(2)}) collective-permute-start(bf16[32,144,128]{2,1,0:T(8,128)(2,1)S(1)} %pad_maximum_fusion.2.refs_4_), channel_id=1, source_target_pairs={{0,64},{1,67},{2,66},{3,65},{4,68},{5,71},{6,70},{7,69},{8,72},{9,... | collective-permute-start | bytes 3538952 | tf_op jit(solution)/shard_map/ppermute | solution.py:53
  74.3 4.9 %shard_map.130 = (f32[1,3,56,3584]{3,2,1,0:T(8,128)}, f32[1,3,56,3584]{3,2,1,0:T(8,128)}, f32[1,3,56,3584]{3,2,1,0:T(8,128)}, f32[56,3584]{1,0:T(8,128)}, s32[8,128]{1,0:T(8,128)S(1)}) custom-call(s32[1]{0:T(128)S(6)} %copy.32.frag_ref, s32[3]{0:T(128)S(1)} %copy-done.10, f32[1,3,56,3584]{3,2,1,0:T(8,128)S(1)} %copy-done, ...), custom_call_target="tpu_custom_call" | custom-call | flops 12042240 | bytes 18063360 | tf_op jit(solution)/shard_map/pallas_call | solution.py:288
  79.2 0.8 collective-permute-done.26.refs_5_
  80.0 2.7 %collective-permute-done.25.refs_3_ = bf16[32,112,128]{2,1,0:T(8,128)(2,1)S(1)} collective-permute-done((bf16[32,112,128]{2,1,0:T(8,128)(2,1)S(1)}, bf16[32,112,128]{2,1,0:T(8,128)(2,1)S(1)}, u32[]{:S(2)}, u32[]{:S(2)}) %collective-permute-start.25) | collective-permute-done | bytes 917536 | tf_op jit(solution)/shard_map/ppermute | solution.py:53
  82.7 8.7 %shard_map.131 = (bf16[512,3584]{1,0:T(8,128)(2,1)}, bf16[512,768]{1,0:T(8,128)(2,1)S(1)}) custom-call(bf16[512,3584]{1,0:T(8,128)(2,1)S(1)} %copy-done.11, bf16[512,3584]{1,0:T(8,128)(2,1)S(1)} %collective-permute-done.4.after_ref.theirs_ref, bf16[32,112,128]{2,1,0:T(8,128)(2,1)S(1)} %pad_maximum_fusion.3.refs_0_, ...), custom_call_target="tpu_custom_call" | custom-call | flops 5637144576 | bytes 12845056 | tf_op jit(solution)/shard_map/pallas_call | solution.py:305
  91.4 0.9 collective-permute-done.23.refs_5_
  92.4 4.1 %collective-permute-done.22.refs_3_ = bf16[32,160,128]{2,1,0:T(8,128)(2,1)S(1)} collective-permute-done((bf16[32,160,128]{2,1,0:T(8,128)(2,1)S(1)}, bf16[32,160,128]{2,1,0:T(8,128)(2,1)S(1)}, u32[]{:S(2)}, u32[]{:S(2)}) %collective-permute-start.22) | collective-permute-done | bytes 1310752 | tf_op jit(solution)/shard_map/ppermute | solution.py:53
  96.5 11.3 %shard_map.132 = (bf16[512,3584]{1,0:T(8,128)(2,1)}, bf16[512,1024]{1,0:T(8,128)(2,1)S(1)}) custom-call(bf16[512,3584]{1,0:T(8,128)(2,1)S(1)} %copy-done.11, bf16[512,3584]{1,0:T(8,128)(2,1)S(1)} %collective-permute-done.4.after_ref.theirs_ref, bf16[32,144,128]{2,1,0:T(8,128)(2,1)S(1)} %pad_maximum_fusion.1.refs_0_, ...), custom_call_target="tpu_custom_call", output_to_operand_aliasing={{0}: (9, {})} | custom-call | flops 7516192768 | bytes 14680064 | tf_op jit(solution)/shard_map/pallas_call | solution.py:305
  107.8 0.4 collective-permute-start.28
  108.1 0.2 collective-permute-start.27
  108.4 3.3 %collective-permute-done.27.refs_0_ = bf16[512,768]{1,0:T(8,128)(2,1)S(1)} collective-permute-done((bf16[512,768]{1,0:T(8,128)(2,1)S(1)}, bf16[512,768]{1,0:T(8,128)(2,1)S(1)}, u32[]{:S(2)}, u32[]{:S(2)}) %collective-permute-start.27) | collective-permute-done | bytes 786464 | tf_op jit(solution)/shard_map/ppermute | solution.py:63
  111.6 1.3 %shard_map.133 = bf16[512,3584]{1,0:T(8,128)(2,1)} custom-call(bf16[512,3584]{1,0:T(8,128)(2,1)} %get-tuple-element.38.buffer_ref, bf16[512,768]{1,0:T(8,128)(2,1)S(1)} %collective-permute-done.27.refs_0_, bf16[512,1024]{1,0:T(8,128)(2,1)S(1)} %collective-permute-done.28.refs_1_), custom_call_target="tpu_custom_call", output_to_operand_aliasing={{}: (0, {})} | custom-call | tf_op jit(solution)/shard_map/pallas_call | solution.py:384
  (80 shorter events, 1.3 us)
Async XLA Ops:
  0.6 12.7 %collective-permute-start.4 = (bf16[512,3584]{1,0:T(8,128)(2,1)}, bf16[512,3584]{1,0:T(8,128)(2,1)S(1)}, u32[]{:S(2)}, u32[]{:S(2)}) collective-permute-start(bf16[512,3584]{1,0:T(8,128)(2,1)} %mine_ref.3), channel_id=1, source_target_pairs={{0,1},{1,0},{2,3},{3,2},{4,5},{5,4},{6,7},{7,6},{8,9},{9,8},{10,11... | collective-permute-start | bytes 11010056 | tf_op jit(solution)/shard_map/ppermute | solution.py:63
  6.1 7.2 %collective-permute-start.3 = (f32[56,896]{1,0:T(8,128)}, f32[56,896]{1,0:T(8,128)S(1)}, u32[]{:S(2)}, u32[]{:S(2)}) collective-permute-start(f32[56,896]{1,0:T(8,128)} %get-tuple-element.26), channel_id=1, source_target_pairs={{0,1},{1,0},{2,3},{3,2},{4,5},{5,4},{6,7},{7,6},{8,9},{9,8},{10,11... | collective-permute-start | bytes 602120 | tf_op jit(solution)/shard_map/ppermute | solution.py:63
  6.2 4.3 %collective-permute-start = (bf16[56,896]{1,0:T(8,128)(2,1)}, bf16[56,896]{1,0:T(8,128)(2,1)S(1)}, u32[]{:S(2)}, u32[]{:S(2)}) collective-permute-start(bf16[56,896]{1,0:T(8,128)(2,1)} %get-tuple-element.23), channel_id=1, source_target_pairs={{0,64},{64,0},{1,65},{65,1},{2,66},{66,2},{3,67},{67,3},{4,68},{68... | collective-permute-start | bytes 301064 | tf_op jit(solution)/shard_map/ppermute | solution.py:336
  7.6 5.7 %collective-permute-start.1 = (bf16[56,896]{1,0:T(8,128)(2,1)}, bf16[56,896]{1,0:T(8,128)(2,1)S(1)}, u32[]{:S(2)}, u32[]{:S(2)}) collective-permute-start(bf16[56,896]{1,0:T(8,128)(2,1)} %get-tuple-element.24), channel_id=1, source_target_pairs={{0,65},{1,64},{64,1},{65,0},{2,67},{3,66},{66,3},{67,2},{4,69},{5,... | collective-permute-start | bytes 301064 | tf_op jit(solution)/shard_map/ppermute | solution.py:337
  13.3 0.9 copy-start.8
  14.3 0.9 copy-start.9
  15.5 9.1 %collective-permute-start.8 = (bf16[1,256,128]{2,1,0:T(8,128)(2,1)S(1)}, bf16[1,256,128]{2,1,0:T(8,128)(2,1)S(1)}, u32[]{:S(2)}, u32[]{:S(2)}) collective-permute-start(bf16[1,256,128]{2,1,0:T(8,128)(2,1)S(1)} %get-tuple-element.31), channel_id=1, source_target_pairs={{0,4},{1,13},{2,6},{3,15},{4,0},{5,9},{6,2},{7,11},{8,12},{9,5},{1... | collective-permute-start | bytes 196616 | tf_op jit(solution)/shard_map/ppermute | solution.py:53
  18.1 7.4 %collective-permute-start.6 = (bf16[1,272,128]{2,1,0:T(8,128)(2,1)S(1)}, bf16[1,272,128]{2,1,0:T(8,128)(2,1)S(1)}, u32[]{:S(2)}, u32[]{:S(2)}) collective-permute-start(bf16[1,272,128]{2,1,0:T(8,128)(2,1)S(1)} %get-tuple-element.30), channel_id=1, source_target_pairs={{0,64},{1,67},{2,66},{3,65},{4,68},{5,71},{6,70},{7,69},{8,72},{9,... | collective-permute-start | bytes 208904 | tf_op jit(solution)/shard_map/ppermute | solution.py:53
  20.8 10.2 %collective-permute-start.5 = (bf16[896,128]{1,0:T(8,128)(2,1)S(1)}, bf16[896,128]{1,0:T(8,128)(2,1)S(1)}, u32[]{:S(2)}, u32[]{:S(2)}) collective-permute-start(bf16[896,128]{1,0:T(8,128)(2,1)S(1)} %get-tuple-element.28), channel_id=1, source_target_pairs={{0,64},{64,0},{1,65},{65,1},{2,66},{66,2},{3,67},{67,3},{4,68},{68... | collective-permute-start | bytes 688136 | tf_op jit(solution)/shard_map/ppermute | solution.py:348
  20.8 6.0 %collective-permute-start.7 = (bf16[1,256,128]{2,1,0:T(8,128)(2,1)S(1)}, bf16[1,256,128]{2,1,0:T(8,128)(2,1)S(1)}, u32[]{:S(2)}, u32[]{:S(2)}) collective-permute-start(bf16[1,256,128]{2,1,0:T(8,128)(2,1)S(1)} %get-tuple-element.29), channel_id=1, source_target_pairs={{0,16},{1,49},{2,18},{3,51},{4,20},{5,53},{6,22},{7,55},{8,24},{9,... | collective-permute-start | bytes 196616 | tf_op jit(solution)/shard_map/ppermute | solution.py:53
  24.8 5.1 %collective-permute-start.11 = (bf16[2,256,128]{2,1,0:T(8,128)(2,1)S(1)}, bf16[2,256,128]{2,1,0:T(8,128)(2,1)S(1)}, u32[]{:S(2)}, u32[]{:S(2)}) collective-permute-start(bf16[2,256,128]{2,1,0:T(8,128)(2,1)S(1)} %pad_maximum_fusion.14), channel_id=1, source_target_pairs={{0,64},{1,67},{2,66},{3,65},{4,68},{5,71},{6,70},{7,69},{8,72},{9,... | collective-permute-start | bytes 393224 | tf_op jit(solution)/shard_map/ppermute | solution.py:53
  25.5 5.2 %collective-permute-start.9 = (bf16[2,272,128]{2,1,0:T(8,128)(2,1)S(1)}, bf16[2,272,128]{2,1,0:T(8,128)(2,1)S(1)}, u32[]{:S(2)}, u32[]{:S(2)}) collective-permute-start(bf16[2,272,128]{2,1,0:T(8,128)(2,1)S(1)} %pad_maximum_fusion.12), channel_id=1, source_target_pairs={{0,16},{1,49},{2,18},{3,51},{4,20},{5,53},{6,22},{7,55},{8,24},{9,... | collective-permute-start | bytes 417800 | tf_op jit(solution)/shard_map/ppermute | solution.py:53
  26.9 4.2 %collective-permute-start.10 = (bf16[2,256,128]{2,1,0:T(8,128)(2,1)S(1)}, bf16[2,256,128]{2,1,0:T(8,128)(2,1)S(1)}, u32[]{:S(2)}, u32[]{:S(2)}) collective-permute-start(bf16[2,256,128]{2,1,0:T(8,128)(2,1)S(1)} %pad_maximum_fusion.13), channel_id=1, source_target_pairs={{0,12},{1,5},{2,14},{3,7},{4,8},{5,1},{6,10},{7,3},{8,4},{9,13},{1... | collective-permute-start | bytes 393224 | tf_op jit(solution)/shard_map/ppermute | solution.py:53
  30.0 6.8 %collective-permute-start.14 = (bf16[4,256,128]{2,1,0:T(8,128)(2,1)S(1)}, bf16[4,256,128]{2,1,0:T(8,128)(2,1)S(1)}, u32[]{:S(2)}, u32[]{:S(2)}) collective-permute-start(bf16[4,256,128]{2,1,0:T(8,128)(2,1)S(1)} %pad_maximum_fusion.11), channel_id=1, source_target_pairs={{0,16},{1,49},{2,18},{3,51},{4,20},{5,53},{6,22},{7,55},{8,24},{9,... | collective-permute-start | bytes 786440 | tf_op jit(solution)/shard_map/ppermute | solution.py:53
  30.8 6.3 %collective-permute-start.12 = (bf16[4,272,128]{2,1,0:T(8,128)(2,1)S(1)}, bf16[4,272,128]{2,1,0:T(8,128)(2,1)S(1)}, u32[]{:S(2)}, u32[]{:S(2)}) collective-permute-start(bf16[4,272,128]{2,1,0:T(8,128)(2,1)S(1)} %pad_maximum_fusion.9), channel_id=1, source_target_pairs={{0,12},{1,5},{2,14},{3,7},{4,8},{5,1},{6,10},{7,3},{8,4},{9,13},{1... | collective-permute-start | bytes 835592 | tf_op jit(solution)/shard_map/ppermute | solution.py:53
  31.2 6.7 %collective-permute-start.13 = (bf16[4,256,128]{2,1,0:T(8,128)(2,1)S(1)}, bf16[4,256,128]{2,1,0:T(8,128)(2,1)S(1)}, u32[]{:S(2)}, u32[]{:S(2)}) collective-permute-start(bf16[4,256,128]{2,1,0:T(8,128)(2,1)S(1)} %pad_maximum_fusion.10), channel_id=1, source_target_pairs={{0,66},{1,65},{2,64},{3,67},{4,70},{5,69},{6,68},{7,71},{8,74},{9,... | collective-permute-start | bytes 786440 | tf_op jit(solution)/shard_map/ppermute | solution.py:53
  37.0 8.4 %collective-permute-start.18 = (bf16[8,256,128]{2,1,0:T(8,128)(2,1)S(1)}, bf16[8,256,128]{2,1,0:T(8,128)(2,1)S(1)}, u32[]{:S(2)}, u32[]{:S(2)}) collective-permute-start(bf16[8,256,128]{2,1,0:T(8,128)(2,1)S(1)} %pad_maximum_fusion.8), channel_id=1, source_target_pairs={{0,12},{1,5},{2,14},{3,7},{4,8},{5,1},{6,10},{7,3},{8,4},{9,13},{1... | collective-permute-start | bytes 1572872 | tf_op jit(solution)/shard_map/ppermute | solution.py:53
  37.3 8.8 %collective-permute-start.15 = (bf16[8,272,128]{2,1,0:T(8,128)(2,1)S(1)}, bf16[8,272,128]{2,1,0:T(8,128)(2,1)S(1)}, u32[]{:S(2)}, u32[]{:S(2)}) collective-permute-start(bf16[8,272,128]{2,1,0:T(8,128)(2,1)S(1)} %pad_maximum_fusion.6), channel_id=1, source_target_pairs={{0,66},{1,65},{2,64},{3,67},{4,70},{5,69},{6,68},{7,71},{8,74},{9,... | collective-permute-start | bytes 1671176 | tf_op jit(solution)/shard_map/ppermute | solution.py:53
  38.1 8.4 %collective-permute-start.16 = (bf16[8,256,128]{2,1,0:T(8,128)(2,1)S(1)}, bf16[8,256,128]{2,1,0:T(8,128)(2,1)S(1)}, u32[]{:S(2)}, u32[]{:S(2)}) collective-permute-start(bf16[8,256,128]{2,1,0:T(8,128)(2,1)S(1)} %pad_maximum_fusion.7), channel_id=1, source_target_pairs={{0,48},{1,17},{2,50},{3,19},{4,52},{5,21},{6,54},{7,23},{8,56},{9,... | collective-permute-start | bytes 1572872 | tf_op jit(solution)/shard_map/ppermute | solution.py:53
  45.6 14.0 %collective-permute-start.19 = (bf16[16,256,128]{2,1,0:T(8,128)(2,1)S(1)}, bf16[16,256,128]{2,1,0:T(8,128)(2,1)S(1)}, u32[]{:S(2)}, u32[]{:S(2)}) collective-permute-start(bf16[16,256,128]{2,1,0:T(8,128)(2,1)S(1)} %select_dynamic-update-slice_fusion.1), channel_id=1, source_target_pairs={{0,66},{1,65},{2,64},{3,67},{4,70},{5,69},{6,68},{7,71},{8,74},{9,... | collective-permute-start | bytes 3145736 | tf_op jit(solution)/shard_map/ppermute | solution.py:53
  46.7 19.3 %collective-permute-start.17 = (bf16[16,256,128]{2,1,0:T(8,128)(2,1)S(1)}, bf16[16,256,128]{2,1,0:T(8,128)(2,1)S(1)}, u32[]{:S(2)}, u32[]{:S(2)}) collective-permute-start(bf16[16,256,128]{2,1,0:T(8,128)(2,1)S(1)} %select_dynamic-update-slice_fusion.2), channel_id=1, source_target_pairs={{0,4},{1,13},{2,6},{3,15},{4,0},{5,9},{6,2},{7,11},{8,12},{9,5},{1... | collective-permute-start | bytes 3145736 | tf_op jit(solution)/shard_map/ppermute | solution.py:53
  48.3 20.4 %collective-permute-start.21 = (bf16[16,272,128]{2,1,0:T(8,128)(2,1)S(1)}, bf16[16,272,128]{2,1,0:T(8,128)(2,1)S(1)}, u32[]{:S(2)}, u32[]{:S(2)}) collective-permute-start(bf16[16,272,128]{2,1,0:T(8,128)(2,1)S(1)} %select_dynamic-update-slice_fusion), channel_id=1, source_target_pairs={{0,48},{1,17},{2,50},{3,19},{4,52},{5,21},{6,54},{7,23},{8,56},{9,... | collective-permute-start | bytes 3342344 | tf_op jit(solution)/shard_map/ppermute | solution.py:53
  59.8 13.1 %collective-permute-start.24 = (bf16[32,112,128]{2,1,0:T(8,128)(2,1)S(1)}, bf16[32,112,128]{2,1,0:T(8,128)(2,1)S(1)}, u32[]{:S(2)}, u32[]{:S(2)}) collective-permute-start(bf16[32,112,128]{2,1,0:T(8,128)(2,1)S(1)} %pad_maximum_fusion.3.refs_0_), channel_id=1, source_target_pairs={{0,48},{1,17},{2,50},{3,19},{4,52},{5,21},{6,54},{7,23},{8,56},{9,... | collective-permute-start | bytes 2752520 | tf_op jit(solution)/shard_map/ppermute | solution.py:53
  59.9 12.2 %collective-permute-start.2 = (bf16[56,896]{1,0:T(8,128)(2,1)S(1)}, bf16[56,896]{1,0:T(8,128)(2,1)S(1)}, u32[]{:S(2)}, u32[]{:S(2)}) collective-permute-start(bf16[56,896]{1,0:T(8,128)(2,1)S(1)} %collective-permute-done.1.cross_ref), channel_id=1, source_target_pairs={{0,1},{1,0},{2,3},{3,2},{4,5},{5,4},{6,7},{7,6},{8,9},{9,8},{10,11... | collective-permute-start | bytes 301064 | tf_op jit(solution)/shard_map/ppermute | solution.py:63
  66.0 2.7 %copy-start.1 = (bf16[16,256,128]{2,1,0:T(8,128)(2,1)}, bf16[16,256,128]{2,1,0:T(8,128)(2,1)S(1)}, u32[]{:S(2)}) copy-start(bf16[16,256,128]{2,1,0:T(8,128)(2,1)S(1)} %collective-permute-done.17.refs_0_) | copy-start | bytes 3145732
  66.1 8.2 %copy-start.6 = (f32[1,3,56,3584]{3,2,1,0:T(8,128)S(1)}, f32[1,3,56,3584]{3,2,1,0:T(8,128)}, u32[]{:S(2)}) copy-start(f32[1,3,56,3584]{3,2,1,0:T(8,128)} %v_ref.1) | copy-start | bytes 7225348
  66.2 13.8 %collective-permute-start.26 = (bf16[32,112,128]{2,1,0:T(8,128)(2,1)S(1)}, bf16[32,112,128]{2,1,0:T(8,128)(2,1)S(1)}, u32[]{:S(2)}, u32[]{:S(2)}) collective-permute-start(bf16[32,112,128]{2,1,0:T(8,128)(2,1)S(1)} %pad_maximum_fusion.5.refs_4_), channel_id=1, source_target_pairs={{0,64},{1,67},{2,66},{3,65},{4,68},{5,71},{6,70},{7,69},{8,72},{9,... | collective-permute-start | bytes 2752520 | tf_op jit(solution)/shard_map/ppermute | solution.py:53
  68.7 5.5 %copy-start.7 = (bf16[1,3,56,3584]{3,2,1,0:T(8,128)(2,1)S(1)}, bf16[1,3,56,3584]{3,2,1,0:T(8,128)(2,1)}, u32[]{:S(2)}) copy-start(bf16[1,3,56,3584]{3,2,1,0:T(8,128)(2,1)} %g_ref.1) | copy-start | bytes 3612676
  68.8 5.5 %copy-start.5 = (f32[1,3,56,3584]{3,2,1,0:T(8,128)S(1)}, f32[1,3,56,3584]{3,2,1,0:T(8,128)}, u32[]{:S(2)}) copy-start(f32[1,3,56,3584]{3,2,1,0:T(8,128)} %m_ref.1) | copy-start | bytes 7225348
  68.9 13.8 %collective-permute-start.25 = (bf16[32,112,128]{2,1,0:T(8,128)(2,1)S(1)}, bf16[32,112,128]{2,1,0:T(8,128)(2,1)S(1)}, u32[]{:S(2)}, u32[]{:S(2)}) collective-permute-start(bf16[32,112,128]{2,1,0:T(8,128)(2,1)S(1)} %pad_maximum_fusion.4.refs_2_), channel_id=1, source_target_pairs={{0,4},{1,13},{2,6},{3,15},{4,0},{5,9},{6,2},{7,11},{8,12},{9,5},{1... | collective-permute-start | bytes 2752520 | tf_op jit(solution)/shard_map/ppermute | solution.py:53
  69.9 2.0 %slice-start = ((bf16[16,256,128]{2,1,0:T(8,128)(2,1)}), bf16[16,144,128]{2,1,0:T(8,128)(2,1)S(1)}, s32[]{:S(2)}) async-start(bf16[16,256,128]{2,1,0:T(8,128)(2,1)} %copy-done.1), calls=%async_computation | async-start | bytes 1179648 | tf_op jit(solution)/shard_map/slice | solution.py:371
  69.9 4.4 %copy-start.4 = (f32[56,3584]{1,0:T(8,128)S(1)}, f32[56,3584]{1,0:T(8,128)}, u32[]{:S(2)}) copy-start(f32[56,3584]{1,0:T(8,128)} %momentum_ref.3) | copy-start | bytes 2408452
  70.0 4.3 %copy-start = (f32[1,3,56,3584]{3,2,1,0:T(8,128)S(1)}, f32[1,3,56,3584]{3,2,1,0:T(8,128)}, u32[]{:S(2)}) copy-start(f32[1,3,56,3584]{3,2,1,0:T(8,128)} %p_ref.1) | copy-start | bytes 7225348
  70.1 4.2 %copy-start.2 = (bf16[16,256,128]{2,1,0:T(8,128)(2,1)S(1)}, bf16[16,256,128]{2,1,0:T(8,128)(2,1)}, u32[]{:S(2)}) copy-start(bf16[16,256,128]{2,1,0:T(8,128)(2,1)} %copy-done.1) | copy-start | bytes 3145732
  70.1 4.2 %copy-start.3 = (f32[56,3584]{1,0:T(8,128)S(1)}, f32[56,3584]{1,0:T(8,128)}, u32[]{:S(2)}) copy-start(f32[56,3584]{1,0:T(8,128)} %anchor_ref.3) | copy-start | bytes 2408452
  70.1 4.2 %copy-start.10 = (s32[3]{0:T(128)S(1)}, s32[3]{0:T(128)}, u32[]{:S(2)}) copy-start(s32[3]{0:T(128)} %plan_ref.3) | copy-start | bytes 40
  70.1 26.3 %collective-permute-start.22 = (bf16[32,160,128]{2,1,0:T(8,128)(2,1)S(1)}, bf16[32,160,128]{2,1,0:T(8,128)(2,1)S(1)}, u32[]{:S(2)}, u32[]{:S(2)}) collective-permute-start(bf16[32,160,128]{2,1,0:T(8,128)(2,1)S(1)} %pad_maximum_fusion.refs_2_), channel_id=1, source_target_pairs={{0,4},{1,13},{2,6},{3,15},{4,0},{5,9},{6,2},{7,11},{8,12},{9,5},{1... | collective-permute-start | bytes 3932168 | tf_op jit(solution)/shard_map/ppermute | solution.py:53
  72.1 10.7 %copy-start.11 = (bf16[512,3584]{1,0:T(8,128)(2,1)S(1)}, bf16[512,3584]{1,0:T(8,128)(2,1)}, u32[]{:S(2)}) copy-start(bf16[512,3584]{1,0:T(8,128)(2,1)} %mine_ref.3) | copy-start | bytes 11010052
  72.1 19.3 %collective-permute-start.20 = (bf16[32,144,128]{2,1,0:T(8,128)(2,1)S(1)}, bf16[32,144,128]{2,1,0:T(8,128)(2,1)S(1)}, u32[]{:S(2)}, u32[]{:S(2)}) collective-permute-start(bf16[32,144,128]{2,1,0:T(8,128)(2,1)S(1)} %pad_maximum_fusion.1.refs_0_), channel_id=1, source_target_pairs={{0,48},{1,17},{2,50},{3,19},{4,52},{5,21},{6,54},{7,23},{8,56},{9,... | collective-permute-start | bytes 3538952 | tf_op jit(solution)/shard_map/ppermute | solution.py:53
  72.9 19.5 %collective-permute-start.23 = (bf16[32,144,128]{2,1,0:T(8,128)(2,1)S(1)}, bf16[32,144,128]{2,1,0:T(8,128)(2,1)S(1)}, u32[]{:S(2)}, u32[]{:S(2)}) collective-permute-start(bf16[32,144,128]{2,1,0:T(8,128)(2,1)S(1)} %pad_maximum_fusion.2.refs_4_), channel_id=1, source_target_pairs={{0,64},{1,67},{2,66},{3,65},{4,68},{5,71},{6,70},{7,69},{8,72},{9,... | collective-permute-start | bytes 3538952 | tf_op jit(solution)/shard_map/ppermute | solution.py:53
  107.8 3.9 %collective-permute-start.28 = (bf16[512,1024]{1,0:T(8,128)(2,1)S(1)}, bf16[512,1024]{1,0:T(8,128)(2,1)S(1)}, u32[]{:S(2)}, u32[]{:S(2)}) collective-permute-start(bf16[512,1024]{1,0:T(8,128)(2,1)S(1)} %get-tuple-element.40), channel_id=1, source_target_pairs={{0,1},{1,0},{2,3},{3,2},{4,5},{5,4},{6,7},{7,6},{8,9},{9,8},{10,11... | collective-permute-start | bytes 3145736 | tf_op jit(solution)/shard_map/ppermute | solution.py:63
  108.1 3.5 %collective-permute-start.27 = (bf16[512,768]{1,0:T(8,128)(2,1)S(1)}, bf16[512,768]{1,0:T(8,128)(2,1)S(1)}, u32[]{:S(2)}, u32[]{:S(2)}) collective-permute-start(bf16[512,768]{1,0:T(8,128)(2,1)S(1)} %get-tuple-element.39), channel_id=1, source_target_pairs={{0,1},{1,0},{2,3},{3,2},{4,5},{5,4},{6,7},{7,6},{8,9},{9,8},{10,11... | collective-permute-start | bytes 2359304 | tf_op jit(solution)/shard_map/ppermute | solution.py:63
